TPU v7x, 128 devices: a whole 4x4x4 slice. The times are simulated.
128 devices in a mesh: seq: 8 (over x, core), exp: 16 (over z, y).
Axes of the slice: x: 4, y: 4, z: 4, core: 2. Of those that a mesh axis runs over, the one named last changes fastest.
Arguments:
- queries: bfloat16 [16, 1024, 4096], P('exp', 'seq'), may hold values from -6 to 6
- keys: bfloat16 [16, 1024, 4096], P('exp', 'seq'), may hold values from -6 to 6
- values: bfloat16 [16, 1024, 4096], P('exp', 'seq'), may hold values from -6 to 6
- residual_in: bfloat16 [16, 1024, 4096], P('exp', 'seq'), may hold values from -6 to 6
- cached_moe: bfloat16 [16, 1024, 4096], P('exp', 'seq'), may hold values from -6 to 6
- norm_gain: bfloat16 [4096], replicated, may hold values from 0.25 to 1.75
- still_masked: int32 [16, 1024], P('exp', 'seq'), may hold values from 0 to 1, as said below
- expert_ids: int32 [16, 1024, 8], P('exp', 'seq'), may hold values from 0 to 63, as said below
- gate_weights: float32 [16, 1024, 8], P('exp', 'seq'), may hold values from 0.05 to 1
- w_gate: bfloat16 [128, 4096, 768], P(('seq', 'exp')), may hold values from -0.09375 to 0.09375
- w_up: bfloat16 [128, 4096, 768], P(('seq', 'exp')), may hold values from -0.09375 to 0.09375
- w_down: bfloat16 [128, 768, 4096], P(('seq', 'exp')), may hold values from -0.15625 to 0.15625
Outputs:
- layer_out: bfloat16 [16, 1024, 4096], P('exp', 'seq')
Inputs may be any that keep to these rules, and one draw needn't show every extreme that they name: `still_masked`: among the 128 rows that one device holds at most 48 are still masked and at least half of that; some device has exactly 48. `expert_ids`: each row names 8 different experts. Among the still-masked rows of one device no expert is named more than 8 times, and on every device some expert is named exactly 8 times.
All inputs are finite; a program needn't handle non-finite values.
Results may differ from a plain program's by a relative error of at most 0.011.
Values may be sent and summed in bfloat16 or wider, within the bound.
No kernel may reach another device: no remote copies, remote signals or barrier semaphores. Data moves between devices by JAX's collectives and lax.ppermute only.
A program may use at most 192 MiB of HBM per device.

v0:
```python
import jax
import jax.numpy as jnp
from jax import lax
from jax.sharding import PartitionSpec as P

HEAD_DIM = 128
TOP = 8


def per_device(
    queries,
    keys,
    values,
    residual_in,
    cached_moe,
    norm_gain,
    still_masked,
    expert_ids,
    gate_weights,
    w_gate,
    w_up,
    w_down,
):
    query_rows = queries[0]
    key_rows = keys[0]
    value_rows = values[0]
    tok_rows = query_rows.shape[0]
    width = query_rows.shape[1]
    head_count = width // HEAD_DIM
    seq_count = lax.axis_size("seq")
    exp_count = lax.axis_size("exp")
    q_heads = query_rows.reshape(tok_rows, head_count, HEAD_DIM)
    scale = 1.0 / jnp.sqrt(jnp.float32(HEAD_DIM))
    run_max = jnp.full((head_count, tok_rows), -1e30, jnp.float32)
    key_piece = lax.all_gather(key_rows, "seq", axis=0, tiled=True)
    value_piece = lax.all_gather(value_rows, "seq", axis=0, tiled=True)
    count = key_piece.shape[0]
    k_heads = key_piece.reshape(count, head_count, HEAD_DIM)
    v_heads = value_piece.reshape(count, head_count, HEAD_DIM)
    scores = (
        jnp.einsum("qhd,khd->hqk", q_heads, k_heads, preferred_element_type=jnp.float32) * scale
    )
    new_max = jnp.maximum(run_max, jnp.max(scores, axis=-1))
    expo = jnp.exp(scores - new_max[..., None])
    new_sum = jnp.sum(expo, axis=-1)
    added = jnp.einsum(
        "hqk,khd->qhd", expo.astype(jnp.bfloat16), v_heads, preferred_element_type=jnp.float32
    )
    attn = (
        (added / jnp.transpose(new_sum)[:, :, None]).reshape(tok_rows, width).astype(jnp.bfloat16)
    )
    hidden = residual_in[0].astype(jnp.float32) + attn.astype(jnp.float32)
    meansq = jnp.mean(hidden * hidden, axis=-1, keepdims=True)
    normed = (hidden * lax.rsqrt(meansq + 1e-06) * norm_gain.astype(jnp.float32)).astype(
        jnp.bfloat16
    )
    row_flags = still_masked[0]
    expert_list = expert_ids[0]
    gate_list = gate_weights[0]
    devices = seq_count * exp_count
    experts = devices // 2
    groups = experts // TOP
    mask_most = tok_rows * 3 // 8
    capacity = max(8, -(-mask_most // groups))
    onehot = (
        (expert_list[:, :, None] == jnp.arange(experts, dtype=jnp.int32)[None, None, :])
        & (row_flags[:, None, None] == 1)
    ).astype(jnp.int32)
    per_row = jnp.sum(onehot, axis=1)
    before = jnp.cumsum(per_row, axis=0) - per_row
    slot_index = jnp.sum(onehot * before[:, None, :], axis=-1)
    target = jnp.where(
        row_flags[:, None] == 1, expert_list * capacity + slot_index, experts * capacity
    )
    copies = jnp.broadcast_to(normed[:, None, :], (tok_rows, TOP, width)).reshape(
        tok_rows * TOP, width
    )
    outgoing = (
        jnp.zeros((experts * capacity, width), jnp.bfloat16)
        .at[target.reshape(-1)]
        .set(copies, mode="drop")
    )
    outgoing = jnp.broadcast_to(
        outgoing.reshape(experts, 1, capacity, width), (experts, 2, capacity, width)
    ).reshape(devices, capacity, width)
    arrived = lax.all_to_all(outgoing, ("seq", "exp"), split_axis=0, concat_axis=0, tiled=True)
    slot_total = devices * capacity
    rows_all = arrived.reshape(slot_total, width)
    live_rows = jnp.any(rows_all != 0, axis=1)
    position = jnp.cumsum(live_rows.astype(jnp.int32)) - 1
    filled = jnp.sum(live_rows.astype(jnp.int32))
    packed = (
        jnp.zeros((slot_total, width), jnp.bfloat16)
        .at[jnp.where(live_rows, position, slot_total)]
        .set(rows_all, mode="drop")
    )
    tile_count = (filled + 127) // 128
    gate_matrix = w_gate[0]
    up_matrix = w_up[0]
    down_matrix = w_down[0]

    def one_tile(turn_index, done):
        offset = turn_index * 128
        tile_rows = lax.dynamic_slice_in_dim(packed, offset, 128, 0)
        gate_part = jnp.dot(tile_rows, gate_matrix, preferred_element_type=jnp.float32)
        up_part = jnp.dot(tile_rows, up_matrix, preferred_element_type=jnp.float32)
        act = (jax.nn.silu(gate_part) * up_part).astype(jnp.bfloat16)
        result = jnp.dot(act, down_matrix, preferred_element_type=jnp.float32).astype(jnp.bfloat16)
        return lax.dynamic_update_slice_in_dim(done, result, offset, 0)

    computed = lax.fori_loop(0, tile_count, one_tile, jnp.zeros((slot_total, width), jnp.bfloat16))
    answers = jnp.where(
        live_rows[:, None], computed[jnp.maximum(position, 0)], jnp.zeros((), jnp.bfloat16)
    )
    returned = lax.all_to_all(
        answers.reshape(devices, capacity, width),
        ("seq", "exp"),
        split_axis=0,
        concat_axis=0,
        tiled=True,
    )
    pairs = returned.reshape(experts, 2, capacity, width)
    pair_sum = (pairs[:, 0].astype(jnp.float32) + pairs[:, 1].astype(jnp.float32)).reshape(
        experts * capacity, width
    )
    picked = pair_sum[jnp.minimum(target, experts * capacity - 1)]
    mixed = jnp.sum(picked * gate_list[:, :, None], axis=1)
    moe = jnp.where(row_flags[:, None] == 1, mixed, cached_moe[0].astype(jnp.float32))
    layer_out = (hidden + moe).astype(jnp.bfloat16)
    return layer_out[None]


def solution(mesh):
    return jax.shard_map(
        per_device,
        mesh=mesh,
        in_specs=(
            P("exp", "seq", None),
            P("exp", "seq", None),
            P("exp", "seq", None),
            P("exp", "seq", None),
            P("exp", "seq", None),
            P(),
            P("exp", "seq"),
            P("exp", "seq", None),
            P("exp", "seq", None),
            P(("seq", "exp"), None, None),
            P(("seq", "exp"), None, None),
            P(("seq", "exp"), None, None),
        ),
        out_specs=P("exp", "seq", None),
        check_vma=False,
    )
```

profile of v0, /device:TPU:1, one launch (start us, length us, event | category | flops | bytes accessed | tf_op | source)
XLA Modules:
  0.0 575.8 jit_solution(14056936692004735482)
XLA Ops:
  6.5 2.3 copy.34
  8.9 0.7 all-gather.7.cloned.1.call-update
  9.6 0.7 compare_bitcast_fusion
  10.2 0.7 convert_reduce_fusion
  11.3 0.8 select_reduce_fusion
  12.5 0.7 broadcast_multiply_fusion
  13.4 1.4 copy.52
  14.8 0.7 convert_element_type.112
  15.6 51.0 %all-gather.5.cloned.1.call-done = bf16[1,1024,4096]{1,2,0:T(8,128)(2,1)} async-done(((bf16[1,128,4096]{1,2,0:T(8,128)(2,1)}), bf16[1,1024,4096]{1,2,0:T(8,128)(2,1)}) %all-gather.5.cloned.1.call-update) | async-done | bytes 8388624 | tf_op jit(solution)/shard_map/all_gather | solution.py:35
  66.6 5.4 multiply_reduce_fusion
  72.1 5.8 %copy-done = f32[32,128,1024]{2,1,0:T(8,128)} copy-done((f32[32,128,1024]{2,1,0:T(8,128)}, f32[32,128,1024]{2,1,0:T(8,128)S(1)}, u32[]{:S(2)}) %copy-start) | copy-done | bytes 16777240
  77.9 3.7 fusion.18
  81.5 37.5 %all-gather.7.cloned.1.call-done = bf16[1,1024,4096]{2,1,0:T(8,128)(2,1)} async-done(((bf16[1,128,4096]{2,1,0:T(8,128)(2,1)}), bf16[1,1024,4096]{2,1,0:T(8,128)(2,1)}) %all-gather.7.cloned.1.call-update) | async-done | bytes 8388624 | tf_op jit(solution)/shard_map/all_gather | solution.py:36
  119.0 11.9 %copy.37 = bf16[1,1024,4096]{1,2,0:T(8,128)(2,1)} copy(bf16[1,1024,4096]{2,1,0:T(8,128)(2,1)} %all-gather.7.cloned.1.call-done) | data formatting | bytes 16777216 | tf_op jit(solution)/shard_map/all_gather | solution.py:36
  130.9 11.6 %fusion.37 = f32[128,32,128]{0,2,1:T(8,128)} fusion(bf16[1024,32,128]{0,2,1:T(8,128)(2,1)} %bitcast.91, f32[32,128,1024]{2,1,0:T(8,128)} %copy-done, f32[32,128]{1,0:T(8,128)S(1)} %broadcast_maximum_fusion, f32[128,32]{0,1:T(8,128)S(1)} %bitcast.100), kind=kOutput, calls=%fused_computation.51 | convolution fusion | flops 1087897600 | bytes 27295744 | tf_op jit(solution)/shard_map/hqk,khd->qhd/dot_general | solution.py:46
  142.5 1.9 copy.44
  144.5 0.4 multiply_reduce_fusion.1
  144.8 1.3 multiply_convert_fusion
  146.2 14.4 %scatter_custom_fusion = bf16[512,4096]{1,0:T(8,128)(2,1)} fusion(s32[1024]{0:T(1024)S(1)} %bitcast.102, bf16[128,4096]{1,0:T(8,128)(2,1)} %multiply_convert_fusion, bf16[]{:T(256)} %constant.19.clone.1), kind=kCustom, calls=%fused_computation.31 | custom fusion | bytes 5242882 | tf_op jit(solution)/shard_map/scatter | solution.py:81
  160.6 6.5 %broadcast_in_dim.79 = bf16[64,2,8,4096]{3,2,1,0:T(8,128)(2,1)} broadcast(bf16[64,8,4096]{2,1,0:T(8,128)(2,1)} %bitcast.90), dimensions={0,2,3} | broadcast | bytes 12582912 | tf_op jit(solution)/shard_map/broadcast_in_dim | solution.py:83
  167.1 8.5 %all-to-all-start = ((bf16[128,8,4096]{2,1,0:T(8,128)(2,1)}), bf16[128,8,4096]{2,1,0:T(8,128)(2,1)}, u32[]{:S(2)}, u32[]{:S(2)}) async-start(bf16[128,8,4096]{2,1,0:T(8,128)(2,1)} %bitcast.88), calls=%async_computation | async-start | bytes 16777216 | tf_op jit(solution)/shard_map/all_to_all | solution.py:86
  175.6 102.2 %all-to-all-done = bf16[128,8,4096]{2,1,0:T(8,128)(2,1)} async-done(((bf16[128,8,4096]{2,1,0:T(8,128)(2,1)}), bf16[128,8,4096]{2,1,0:T(8,128)(2,1)}, u32[]{:S(2)}, u32[]{:S(2)}) %all-to-all-start) | async-done | bytes 8388640 | tf_op jit(solution)/shard_map/all_to_all | solution.py:86
  277.8 5.7 compare_reduce_fusion
  283.6 0.7 convert_reduce_fusion.1
  285.7 17.8 %scatter_custom_fusion.1 = bf16[1024,4096]{1,0:T(8,128)(2,1)} fusion(s32[1024]{0:T(1024)S(1)} %bitcast.103, bf16[128,8,4096]{2,1,0:T(8,128)(2,1)} %all-to-all-done, bf16[]{:T(256)} %constant.19.clone.1), kind=kCustom, calls=%fused_computation.29 | custom fusion | bytes 16777218 | tf_op jit(solution)/shard_map/scatter | solution.py:95
  303.5 4.3 broadcast.214
  307.8 74.9 %while.10 = (s32[]{:T(128)}, bf16[1024,4096]{1,0:T(8,128)(2,1)}, s32[]{:T(128)}, bf16[1024,4096]{1,0:T(8,128)(2,1)}, bf16[4096,768]{1,0:T(8,128)(2,1)}, /*index=...) while((s32[]{:T(128)}, bf16[1024,4096]{1,0:T(8,128)(2,1)}, ...), condition=%wide.region_13.14_spmd, body=%wide.region_12.13_spmd.sunk | while | flops 2417033216 | bytes 22807712 | solution.py:111
  307.8 4.1 fusion.63
  311.9 8.4 %fusion.64 = bf16[1024,4096]{1,0:T(8,128)(2,1)} fusion(bf16[1024,4096]{1,0:T(8,128)(2,1)} %get-tuple-element.118, s32[]{:T(128)S(6)} %select_n.106, bf16[768,4096]{1,0:T(8,128)(2,1)} %get-tuple-element.134, bf16[4096,768]{1,0:T(8,128)(2,1)} %get-tuple-element.133, bf16[1024,4096]{1,0:T(8,128)(2,1)} %get-tuple-element.131, f32[128,768]{1,0:T(8,128)S(1)} %fusion.63), kind=kOutput, calls=%fused_computation.5.clone.1 | convolution fusion | flops 1611726848 | bytes 15074304 | tf_op jit(solution)/shard_map/while/body/dot_general | solution.py:108
  320.3 4.1 fusion.63
  324.4 8.3 %fusion.64 = bf16[1024,4096]{1,0:T(8,128)(2,1)} fusion(bf16[1024,4096]{1,0:T(8,128)(2,1)} %get-tuple-element.118, s32[]{:T(128)S(6)} %select_n.106, bf16[768,4096]{1,0:T(8,128)(2,1)} %get-tuple-element.134, bf16[4096,768]{1,0:T(8,128)(2,1)} %get-tuple-element.133, bf16[1024,4096]{1,0:T(8,128)(2,1)} %get-tuple-element.131, f32[128,768]{1,0:T(8,128)S(1)} %fusion.63), kind=kOutput, calls=%fused_computation.5.clone.1 | convolution fusion | flops 1611726848 | bytes 15074304 | tf_op jit(solution)/shard_map/while/body/dot_general | solution.py:108
  332.8 4.1 fusion.63
  336.9 8.3 %fusion.64 = bf16[1024,4096]{1,0:T(8,128)(2,1)} fusion(bf16[1024,4096]{1,0:T(8,128)(2,1)} %get-tuple-element.118, s32[]{:T(128)S(6)} %select_n.106, bf16[768,4096]{1,0:T(8,128)(2,1)} %get-tuple-element.134, bf16[4096,768]{1,0:T(8,128)(2,1)} %get-tuple-element.133, bf16[1024,4096]{1,0:T(8,128)(2,1)} %get-tuple-element.131, f32[128,768]{1,0:T(8,128)S(1)} %fusion.63), kind=kOutput, calls=%fused_computation.5.clone.1 | convolution fusion | flops 1611726848 | bytes 15074304 | tf_op jit(solution)/shard_map/while/body/dot_general | solution.py:108
  345.2 4.1 fusion.63
  349.3 8.3 %fusion.64 = bf16[1024,4096]{1,0:T(8,128)(2,1)} fusion(bf16[1024,4096]{1,0:T(8,128)(2,1)} %get-tuple-element.118, s32[]{:T(128)S(6)} %select_n.106, bf16[768,4096]{1,0:T(8,128)(2,1)} %get-tuple-element.134, bf16[4096,768]{1,0:T(8,128)(2,1)} %get-tuple-element.133, bf16[1024,4096]{1,0:T(8,128)(2,1)} %get-tuple-element.131, f32[128,768]{1,0:T(8,128)S(1)} %fusion.63), kind=kOutput, calls=%fused_computation.5.clone.1 | convolution fusion | flops 1611726848 | bytes 15074304 | tf_op jit(solution)/shard_map/while/body/dot_general | solution.py:108
  357.7 4.1 fusion.63
  361.8 8.4 %fusion.64 = bf16[1024,4096]{1,0:T(8,128)(2,1)} fusion(bf16[1024,4096]{1,0:T(8,128)(2,1)} %get-tuple-element.118, s32[]{:T(128)S(6)} %select_n.106, bf16[768,4096]{1,0:T(8,128)(2,1)} %get-tuple-element.134, bf16[4096,768]{1,0:T(8,128)(2,1)} %get-tuple-element.133, bf16[1024,4096]{1,0:T(8,128)(2,1)} %get-tuple-element.131, f32[128,768]{1,0:T(8,128)S(1)} %fusion.63), kind=kOutput, calls=%fused_computation.5.clone.1 | convolution fusion | flops 1611726848 | bytes 15074304 | tf_op jit(solution)/shard_map/while/body/dot_general | solution.py:108
  370.2 4.1 fusion.63
  374.3 8.3 %fusion.64 = bf16[1024,4096]{1,0:T(8,128)(2,1)} fusion(bf16[1024,4096]{1,0:T(8,128)(2,1)} %get-tuple-element.118, s32[]{:T(128)S(6)} %select_n.106, bf16[768,4096]{1,0:T(8,128)(2,1)} %get-tuple-element.134, bf16[4096,768]{1,0:T(8,128)(2,1)} %get-tuple-element.133, bf16[1024,4096]{1,0:T(8,128)(2,1)} %get-tuple-element.131, f32[128,768]{1,0:T(8,128)S(1)} %fusion.63), kind=kOutput, calls=%fused_computation.5.clone.1 | convolution fusion | flops 1611726848 | bytes 15074304 | tf_op jit(solution)/shard_map/while/body/dot_general | solution.py:108
  382.6 19.5 %gather_fusion = bf16[1024,4096]{1,0:T(8,128)(2,1)} fusion(bf16[1024,4096]{1,0:T(8,128)(2,1)} %get-tuple-element.43, s32[1024]{0:T(1024)S(1)} %broadcast_clamp_fusion.1), kind=kCustom, calls=%fused_computation | custom fusion | bytes 16781312 | tf_op jit(solution)/shard_map/gather | solution.py:113
  402.2 7.2 %bitcast_select_fusion = bf16[128,8,4096]{2,1,0:T(8,128)(2,1)} fusion(bf16[1024,4096]{1,0:T(8,128)(2,1)} %gather_fusion, pred[128,8]{1,0:T(8,128)(4,1)S(1)} %compare_reduce_fusion), kind=kLoop, calls=%fused_computation.28 | loop fusion | flops 4194304 | bytes 16778240 | tf_op jit(solution)/shard_map/jit(_where)/select_n | solution.py:112
  409.4 20.5 %all-to-all-start.1 = ((bf16[128,8,4096]{2,1,0:T(8,128)(2,1)}), bf16[128,8,4096]{2,1,0:T(8,128)(2,1)}, u32[]{:S(2)}, u32[]{:S(2)}) async-start(bf16[128,8,4096]{2,1,0:T(8,128)(2,1)} %bitcast_select_fusion), calls=%async_computation.1 | async-start | bytes 16777216 | tf_op jit(solution)/shard_map/all_to_all | solution.py:115
  430.3 1.9 copy.38
  432.2 99.6 %all-to-all-done.1 = bf16[128,8,4096]{2,1,0:T(8,128)(2,1)} async-done(((bf16[128,8,4096]{2,1,0:T(8,128)(2,1)}), bf16[128,8,4096]{2,1,0:T(8,128)(2,1)}, u32[]{:S(2)}, u32[]{:S(2)}) %all-to-all-start.1) | async-done | bytes 8388640 | tf_op jit(solution)/shard_map/all_to_all | solution.py:115
  531.7 8.3 %add_bitcast_fusion = f32[512,4096]{1,0:T(8,128)} fusion(bf16[64,2,8,4096]{3,2,1,0:T(8,128)(2,1)} %bitcast.21), kind=kLoop, calls=%fused_computation.33 | loop fusion | flops 6291456 | bytes 16777216 | tf_op jit(solution)/shard_map/add | solution.py:123
  540.0 18.0 %gather_fusion.1 = f32[1024,4096]{1,0:T(8,128)} fusion(f32[512,4096]{1,0:T(8,128)} %add_bitcast_fusion, s32[1024]{0:T(1024)S(1)} %broadcast_clamp_fusion), kind=kCustom, calls=%fused_computation.1 | custom fusion | bytes 33558528 | tf_op jit(solution)/shard_map/gather | solution.py:126
  558.1 8.9 %fusion.17 = f32[128,4096]{1,0:T(8,128)S(1)} fusion(f32[1024,4096]{1,0:T(8,128)} %gather_fusion.1, f32[128,8]{1,0:T(8,128)S(1)} %copy.48), kind=kLoop, calls=%fused_computation.21 | loop fusion | flops 7864320 | bytes 18878464 | tf_op jit(solution)/shard_map/reduce_sum | solution.py:127
  567.0 1.5 fusion.31
  (44 shorter events, 2.1 us)
Async XLA Ops:
  6.5 60.1 %all-gather.5.cloned.1.call-start = ((), (), s32[]{:S(2)}) async-start(), calls=%async_computation.2 | async-start | bytes 9437184 | tf_op jit(solution)/shard_map/all_gather | solution.py:35
  8.8 110.2 %all-gather.7.cloned.1.call-start = ((), (), s32[]{:S(2)}) async-start(), calls=%async_computation.3 | async-start | bytes 9437184 | tf_op jit(solution)/shard_map/all_gather | solution.py:36
  72.0 5.8 %copy-start = (f32[32,128,1024]{2,1,0:T(8,128)}, f32[32,128,1024]{2,1,0:T(8,128)S(1)}, u32[]{:S(2)}) copy-start(f32[32,128,1024]{2,1,0:T(8,128)S(1)} %get-tuple-element.61) | copy-start | bytes 50331652
  130.9 13.5 %copy-start.1 = (bf16[1,128,4096]{2,1,0:T(8,128)(2,1)S(1)}, bf16[1,128,4096]{2,1,0:T(8,128)(2,1)}, u32[]{:S(2)}) copy-start(bf16[1,128,4096]{2,1,0:T(8,128)(2,1)} %param.17) | copy-start | bytes 3145732
  167.1 110.7 %all-to-all-start = ((bf16[128,8,4096]{2,1,0:T(8,128)(2,1)}), bf16[128,8,4096]{2,1,0:T(8,128)(2,1)}, u32[]{:S(2)}, u32[]{:S(2)}) async-start(bf16[128,8,4096]{2,1,0:T(8,128)(2,1)} %bitcast.88), calls=%async_computation | async-start | bytes 16777216 | tf_op jit(solution)/shard_map/all_to_all | solution.py:86
  409.4 20.5 %copy-start.5 = (s32[1,128,8]{1,2,0:T(8,128)S(1)}, s32[1,128,8]{1,2,0:T(8,128)}, u32[]{:S(2)}) copy-start(s32[1,128,8]{1,2,0:T(8,128)} %param.21) | copy-start | bytes 12292
  409.4 20.8 %copy-start.6 = (f32[1,128,8]{1,2,0:T(8,128)S(1)}, f32[1,128,8]{1,2,0:T(8,128)}, u32[]{:S(2)}) copy-start(f32[1,128,8]{1,2,0:T(8,128)} %param.22) | copy-start | bytes 12292
  409.4 20.9 %copy-start.2 = (f32[128,32,128]{0,2,1:T(8,128)S(1)}, f32[128,32,128]{0,2,1:T(8,128)}, u32[]{:S(2)}) copy-start(f32[128,32,128]{0,2,1:T(8,128)} %fusion.37) | copy-start | bytes 6291460
  409.4 122.4 %all-to-all-start.1 = ((bf16[128,8,4096]{2,1,0:T(8,128)(2,1)}), bf16[128,8,4096]{2,1,0:T(8,128)(2,1)}, u32[]{:S(2)}, u32[]{:S(2)}) async-start(bf16[128,8,4096]{2,1,0:T(8,128)(2,1)} %bitcast_select_fusion), calls=%async_computation.1 | async-start | bytes 16777216 | tf_op jit(solution)/shard_map/all_to_all | solution.py:115
  558.1 8.9 %copy-start.3 = (f32[1,128,4096]{2,1,0:T(8,128)S(1)}, f32[1,128,4096]{2,1,0:T(8,128)}, u32[]{:S(2)}) copy-start(f32[1,128,4096]{2,1,0:T(8,128)} %copy.38) | copy-start | bytes 6291460
  558.1 8.9 %copy-start.4 = (bf16[1,128,4096]{2,1,0:T(8,128)(2,1)S(1)}, bf16[1,128,4096]{2,1,0:T(8,128)(2,1)}, u32[]{:S(2)}) copy-start(bf16[1,128,4096]{2,1,0:T(8,128)(2,1)} %param.18) | copy-start | bytes 3145732
Sparse Core Ops, SparseCore 0:
  9.0 57.5 all-gather.4
  68.3 50.6 all-gather.6
where the time goes:
time: 585 us; the launch traced here: 576 us
  waiting for transfers between devices  291 us (50%)
  local copies, waits for them, and re-layouts  107 us (18%)
  matrix products  91.8 us (16%)
  other arithmetic  41.8 us (7%)
  starting transfers between devices  29.1 us (5%)
  between operations  14.8 us (3%)
    all_to_all x1, waiting for transfers between devices, per_device(): lax.all_to_all(outgoing, ('seq', 'exp'), split_axis=0, concat_axis=0, til...  102 us
    all_to_all x1, waiting for transfers between devices, per_device(): lax.all_to_all(answers.reshape(devices, capacity, width), ('seq', 'exp'),...  99.6 us
    all_gather x1, waiting for transfers between devices, per_device(): key_piece = lax.all_gather(key_rows, 'seq', axis=0, tiled=True)  51 us
    dot_general x6, matrix products, one_tile(): jnp.dot(act, down_matrix, preferred_element_type=jnp.float32)  50.2 us
    all_gather x1, waiting for transfers between devices, per_device(): value_piece = lax.all_gather(value_rows, 'seq', axis=0, tiled=True)  37.5 us
    dot_general x6, matrix products, one_tile(): jnp.dot(tile_rows, gate_matrix, preferred_element_type=jnp.float32)  24.6 us
    all_to_all x1, starting transfers between devices, per_device(): lax.all_to_all(answers.reshape(devices, capacity, width), ('seq', 'exp'),...  20.5 us
    gather x1, local copies, waits for them, and re-layouts, per_device(): computed[jnp.maximum(position, 0)]  19.5 us
  transfers between devices with their start and end apart: 4, of which 4 were waited for; matrix products, arithmetic and copies ran while one was open for 3% of the time, Pallas kernels for 0%

commit v1 on v0

v1 whole, which is shorter than its diff:
```python
import functools
import math

import jax
import jax.numpy as jnp
from jax import lax
from jax.experimental import pallas as pl
from jax.experimental.pallas import tpu as pltpu
from jax.sharding import PartitionSpec as P

HEAD_DIM = 128
TOP = 8
SLOTS = 8
bf16 = jnp.bfloat16
f32 = jnp.float32


def params(mib, *semantics):
    return pltpu.CompilerParams(
        vmem_limit_bytes=mib * 1024 * 1024, dimension_semantics=semantics or None
    )


def attend_kernel(qkv_ref, out_ref):
    blocks, _, rows, _ = qkv_ref.shape
    length = blocks * rows
    scale = math.log2(math.e) / math.sqrt(HEAD_DIM)
    k_all = qkv_ref[:, 1].reshape(length, HEAD_DIM)
    v_all = qkv_ref[:, 2].reshape(length, HEAD_DIM)
    step = 2
    for first in range(0, blocks, step):
        q_part = qkv_ref[first : first + step, 0].reshape(step * rows, HEAD_DIM)
        scores = lax.dot_general(
            q_part, k_all, (((1,), (1,)), ((), ())), preferred_element_type=f32
        )
        peak = jnp.max(scores, axis=-1, keepdims=True)
        expo = jnp.exp2((scores - peak) * scale)
        total = jnp.sum(expo, axis=-1, keepdims=True)
        mixed = jnp.dot(expo.astype(bf16), v_all, preferred_element_type=f32)
        out_ref[first : first + step] = (
            (mixed / total).astype(bf16).reshape(step, rows, HEAD_DIM)
        )


def attend(qkv):
    blocks, three, rows, cols = qkv.shape
    heads = cols // HEAD_DIM
    return pl.pallas_call(
        attend_kernel,
        grid=(heads,),
        in_specs=[pl.BlockSpec((blocks, three, rows, HEAD_DIM), lambda h: (0, 0, 0, h))],
        out_specs=pl.BlockSpec((blocks, rows, HEAD_DIM), lambda h: (0, 0, h)),
        out_shape=jax.ShapeDtypeStruct((blocks, rows, cols), bf16),
        compiler_params=params(40),
        name="attend",
    )(qkv)


def dispatch_kernel(attn_ref, res_ref, gain_ref, pick_ref, out_ref, rs_ref):
    step = pl.program_id(0)
    groups, rows, cols = attn_ref.shape

    @pl.when(step == 0)
    def _():
        total = jnp.zeros((rows, 1), f32)
        for g in range(groups):
            hid = res_ref[:, g * cols : (g + 1) * cols].astype(f32) + attn_ref[g].astype(f32)
            total += jnp.sum(hid * hid, axis=-1, keepdims=True)
        rs_ref[...] = lax.rsqrt(total / (groups * cols) + 1e-06)

    here = pl.ds(pl.multiple_of(step * cols, cols), cols)
    hid = res_ref[:, here].astype(f32) + attn_ref[step].astype(f32)
    normed = (hid * rs_ref[...] * gain_ref[:, here].astype(f32)).astype(bf16)
    picked = jnp.dot(pick_ref[...], normed, preferred_element_type=f32)
    experts = out_ref.shape[0]
    picked = picked.reshape(experts, SLOTS, cols).astype(bf16)
    out_ref[:, 0] = picked
    out_ref[:, 1] = picked


def dispatch(attn, residual, gain, pick):
    groups, rows, cols = attn.shape
    experts = pick.shape[0] // SLOTS
    width = groups * cols
    return pl.pallas_call(
        dispatch_kernel,
        grid=(groups,),
        in_specs=[
            pl.BlockSpec((groups, rows, cols), lambda j: (0, 0, 0)),
            pl.BlockSpec((rows, width), lambda j: (0, 0)),
            pl.BlockSpec((1, width), lambda j: (0, 0)),
            pl.BlockSpec(pick.shape, lambda j: (0, 0)),
        ],
        out_specs=pl.BlockSpec((experts, 2, SLOTS, cols), lambda j: (0, 0, 0, j)),
        out_shape=jax.ShapeDtypeStruct((experts, 2, SLOTS, width), bf16),
        scratch_shapes=[pltpu.VMEM((rows, 1), f32)],
        compiler_params=params(40),
        name="dispatch",
    )(attn, residual, gain, pick)


def expert_kernel(rows_ref, gate_ref, up_ref, down_ref, out_ref):
    tile = rows_ref[...]
    gate_part = jnp.dot(tile, gate_ref[...], preferred_element_type=f32)
    up_part = jnp.dot(tile, up_ref[...], preferred_element_type=f32)
    act = (gate_part / (1.0 + jnp.exp(-gate_part)) * up_part).astype(bf16)
    out_ref[...] = jnp.dot(act, down_ref[...], preferred_element_type=f32).astype(bf16)


def expert(rows, gate, up, down):
    total, width = rows.shape
    half = gate.shape[1]
    tile = 256
    return pl.pallas_call(
        expert_kernel,
        grid=(total // tile,),
        in_specs=[
            pl.BlockSpec((tile, width), lambda i: (i, 0)),
            pl.BlockSpec((width, half), lambda i: (0, 0)),
            pl.BlockSpec((width, half), lambda i: (0, 0)),
            pl.BlockSpec((half, width), lambda i: (0, 0)),
        ],
        out_specs=pl.BlockSpec((tile, width), lambda i: (i, 0)),
        out_shape=jax.ShapeDtypeStruct((total, width), bf16),
        compiler_params=params(60),
        name="expert",
    )(rows, gate, up, down)


def combine_kernel(back_ref, mix_ref, attn_ref, res_ref, cached_ref, flag_ref, out_ref):
    rows = res_ref.shape[0]
    both = jnp.dot(mix_ref[...], back_ref[...], preferred_element_type=f32)
    mixed = both[:rows] + both[rows:]
    moe = jnp.where(flag_ref[...] == 1, mixed, cached_ref[...].astype(f32))
    hid = res_ref[...].astype(f32) + attn_ref[0].astype(f32)
    out_ref[...] = (hid + moe).astype(bf16)


def combine(back, mix, attn, residual, cached, flags):
    groups, rows, cols = attn.shape
    slots, width = back.shape
    return pl.pallas_call(
        combine_kernel,
        grid=(groups,),
        in_specs=[
            pl.BlockSpec((slots, cols), lambda j: (0, j)),
            pl.BlockSpec(mix.shape, lambda j: (0, 0)),
            pl.BlockSpec((1, rows, cols), lambda j: (j, 0, 0)),
            pl.BlockSpec((rows, cols), lambda j: (0, j)),
            pl.BlockSpec((rows, cols), lambda j: (0, j)),
            pl.BlockSpec((rows, 1), lambda j: (0, 0)),
        ],
        out_specs=pl.BlockSpec((rows, cols), lambda j: (0, j)),
        out_shape=jax.ShapeDtypeStruct((rows, width), bf16),
        compiler_params=params(40),
        name="combine",
    )(back, mix, attn, residual, cached, flags)


def per_device(
    queries,
    keys,
    values,
    residual_in,
    cached_moe,
    norm_gain,
    still_masked,
    expert_ids,
    gate_weights,
    w_gate,
    w_up,
    w_down,
):
    rows, width = queries.shape[1:]
    seq_count = lax.axis_size("seq")
    devices = seq_count * lax.axis_size("exp")
    experts = devices // 2
    cols = width // seq_count

    qkv = jnp.stack([queries[0], keys[0], values[0]])
    qkv = qkv.reshape(3, rows, seq_count, cols).transpose(2, 0, 1, 3)
    qkv = lax.all_to_all(qkv, "seq", split_axis=0, concat_axis=0, tiled=True)

    flags = still_masked[0][:, None]
    hits = (expert_ids[0][:, :, None] == jnp.arange(experts, dtype=jnp.int32)) & (
        flags[:, :, None] == 1
    )
    named = jnp.any(hits, axis=1)
    gates = jnp.sum(jnp.where(hits, gate_weights[0][:, :, None], 0.0), axis=1)
    below = jnp.tril(jnp.ones((rows, rows), bf16), -1)
    before = jnp.dot(below, named.astype(bf16), preferred_element_type=f32).astype(jnp.int32)
    slot = jnp.where(named, before, -1)
    pick = (slot.T[:, None, :] == jnp.arange(SLOTS)[None, :, None]).astype(bf16)
    pick = pick.reshape(experts * SLOTS, rows)
    spread = jnp.where(
        slot[:, :, None, None] == jnp.arange(SLOTS)[None, None, None, :],
        gates[:, :, None, None],
        0.0,
    )
    spread = jnp.broadcast_to(spread, (rows, experts, 2, SLOTS)).reshape(rows, devices * SLOTS)
    high = spread.astype(bf16)
    low = (spread - high.astype(f32)).astype(bf16)
    mix = jnp.concatenate([high, low], axis=0)

    attn = attend(qkv)
    attn = lax.all_to_all(attn, "seq", split_axis=0, concat_axis=0, tiled=True)
    outgoing = dispatch(attn, residual_in[0], norm_gain[None, :], pick)
    arrived = lax.all_to_all(
        outgoing.reshape(devices, SLOTS, width),
        ("seq", "exp"),
        split_axis=0,
        concat_axis=0,
        tiled=True,
    )
    done = expert(arrived.reshape(devices * SLOTS, width), w_gate[0], w_up[0], w_down[0])
    back = lax.all_to_all(
        done.reshape(devices, SLOTS, width),
        ("seq", "exp"),
        split_axis=0,
        concat_axis=0,
        tiled=True,
    )
    out = combine(
        back.reshape(devices * SLOTS, width), mix, attn, residual_in[0], cached_moe[0], flags
    )
    return out[None]


def solution(mesh):
    return jax.shard_map(
        per_device,
        mesh=mesh,
        in_specs=(
            P("exp", "seq", None),
            P("exp", "seq", None),
            P("exp", "seq", None),
            P("exp", "seq", None),
            P("exp", "seq", None),
            P(),
            P("exp", "seq"),
            P("exp", "seq", None),
            P("exp", "seq", None),
            P(("seq", "exp"), None, None),
            P(("seq", "exp"), None, None),
            P(("seq", "exp"), None, None),
        ),
        out_specs=P("exp", "seq", None),
        check_vma=False,
    )
```

time: 585 us -> 347 us (0.59)
  waiting for transfers between devices: 291 us -> 116 us
  blocking collectives: 0 us -> 150 us
  local copies, waits for them, and re-layouts: 107 us -> 11.2 us
  matrix products: 91.8 us -> 0.2 us
  Pallas kernels: 0 us -> 50.2 us
  other arithmetic: 41.8 us -> 2.4 us
  starting transfers between devices: 29.1 us -> 12.4 us
  between operations: 14.8 us -> 0.16 us
    all_to_all x0 -> x2, blocking collectives: none -> 150 us  [the longest x1 106 us: per_device(): lax.all_to_all(outgoing.reshape(devices, SLOTS, width), ('seq', 'exp'), s...]
    dot_general x14 -> x1, matrix products: 91.8 us -> 0.2 us  [per_device(): jnp.dot(below, named.astype(bf16), preferred_element_type=f32)]
    all_gather x2 -> x0, waiting for transfers between devices: 88.5 us -> none  [the longest x1 51 us: per_device(): key_piece = lax.all_gather(key_rows, 'seq', axis=0, tiled=True)]
    all_to_all x2, waiting for transfers between devices: 202 us -> 116 us  [the longest x1 102 us: per_device(): lax.all_to_all(done.reshape(devices, SLOTS, width), ('seq', 'exp'), split...]
    pallas_call x0 -> x4, Pallas kernels: none -> 50.2 us  [the longest x1 28.6 us: expert(): pl.pallas_call(expert_kernel, grid=(total // tile,), in_specs=[pl.BlockSp...]
    gather x2 -> x0, local copies, waits for them, and re-layouts: 37.6 us -> none  [the longest x1 19.5 us: per_device(): computed[jnp.maximum(position, 0)]]
    scatter x2 -> x0, local copies, waits for them, and re-layouts: 32.2 us -> none  [the longest x1 17.8 us: per_device(): packed = jnp.zeros((slot_total, width), jnp.bfloat16).at[jnp.where(live_r...]
    all_to_all x2, starting transfers between devices: 29 us -> 12.4 us  [the longest x1 7.89 us: per_device(): lax.all_to_all(done.reshape(devices, SLOTS, width), ('seq', 'exp'), split...]
  transfers between devices with their start and end apart: 4 -> 2, of which waited for: 4 -> 2; matrix products, arithmetic and copies ran while one was open for 3% -> 0% of each run, Pallas kernels for 0% -> 0%
where the time goes in v1:
time: 347 us; the launch traced here: 342 us
  blocking collectives  150 us (43%)
  waiting for transfers between devices  116 us (33%)
  Pallas kernels  50.2 us (14%)
  starting transfers between devices  12.4 us (4%)
  local copies, waits for them, and re-layouts  11.2 us (3%)
    all_to_all x1, blocking collectives, per_device(): lax.all_to_all(outgoing.reshape(devices, SLOTS, width), ('seq', 'exp'), s...  106 us
    all_to_all x1, waiting for transfers between devices, per_device(): lax.all_to_all(done.reshape(devices, SLOTS, width), ('seq', 'exp'), split...  102 us
    all_to_all x1, blocking collectives, per_device(): qkv = lax.all_to_all(qkv, 'seq', split_axis=0, concat_axis=0, tiled=True)  43.7 us
    pallas_call x1, Pallas kernels, expert(): pl.pallas_call(expert_kernel, grid=(total // tile,), in_specs=[pl.BlockSp...  28.6 us
    all_to_all x1, waiting for transfers between devices, per_device(): attn = lax.all_to_all(attn, 'seq', split_axis=0, concat_axis=0, tiled=True)  14.5 us
    pallas_call x1, Pallas kernels, attend(): pl.pallas_call(attend_kernel, grid=(heads,), in_specs=[pl.BlockSpec((bloc...  9.38 us
    pallas_call x1, Pallas kernels, combine(): pl.pallas_call(combine_kernel, grid=(groups,), in_specs=[pl.BlockSpec((sl...  8.35 us
    all_to_all x1, starting transfers between devices, per_device(): lax.all_to_all(done.reshape(devices, SLOTS, width), ('seq', 'exp'), split...  7.89 us
  transfers between devices with their start and end apart: 2, of which 2 were waited for; matrix products, arithmetic and copies ran while one was open for 0% of the time, Pallas kernels for 0%

profile of v1, /device:TPU:1, one launch (start us, length us, event | category | flops | bytes accessed | tf_op | source)
XLA Modules:
  0.0 342.3 jit_solution(8847154172240135182)
XLA Ops:
  0.0 1.6 copy.28
  1.6 1.6 copy.27
  3.2 1.6 copy.26
  4.9 2.0 pad_maximum_fusion
  6.9 4.6 %copy.29 = bf16[3,128,8,512]{3,1,0,2:T(8,128)(2,1)} copy(bf16[3,128,8,512]{1,3,2,0:T(8,128)(2,1)} %bitcast.30) | data formatting | bytes 6291456 | tf_op jit(solution)/shard_map/reshape | solution.py:181
  11.5 43.7 %all_to_all.20.qkv_ref = bf16[8,3,128,512]{3,2,1,0:T(8,128)(2,1)S(1)} all-to-all(bf16[8,3,128,512]{3,2,1,0:T(8,128)(2,1)} %bitcast.31), channel_id=1, replica_groups=mesh['seq'=8,'exp'=16] {'seq'}, dimensions={0} | all-to-all | bytes 6291456 | tf_op jit(solution)/shard_map/all_to_all | solution.py:182
  55.2 0.0 copy-start.3
  55.2 0.0 copy-start.5
  55.2 0.0 copy-start.2
  55.2 0.0 copy-start
  55.2 9.4 %attend.1 = bf16[8,128,512]{2,1,0:T(8,128)(2,1)} custom-call(bf16[8,3,128,512]{3,2,1,0:T(8,128)(2,1)S(1)} %all_to_all.20.qkv_ref), custom_call_target="tpu_custom_call" | custom-call | tf_op jit(solution)/shard_map/attend/pallas_call | solution.py:48
  64.6 4.5 %all-to-all-start.1 = ((bf16[8,128,512]{2,1,0:T(8,128)(2,1)}), bf16[8,128,512]{2,1,0:T(8,128)(2,1)S(1)}, u32[]{:S(2)}, u32[]{:S(2)}) async-start(bf16[8,128,512]{2,1,0:T(8,128)(2,1)} %attend.1), calls=%async_computation.1 | async-start | bytes 2097152 | tf_op jit(solution)/shard_map/all_to_all | solution.py:206
  69.1 0.0 copy-done.3
  69.1 0.1 eq.77
  69.2 0.0 copy-done.5
  69.2 0.0 copy-done.2
  69.3 0.2 fusion
  69.5 0.2 fusion.4.pick_ref
  69.7 14.5 %all-to-all-done.1.attn_ref = bf16[8,128,512]{2,1,0:T(8,128)(2,1)S(1)} async-done(((bf16[8,128,512]{2,1,0:T(8,128)(2,1)}), bf16[8,128,512]{2,1,0:T(8,128)(2,1)S(1)}, u32[]{:S(2)}, u32[]{:S(2)}) %all-to-all-start.1) | async-done | bytes 1048608 | tf_op jit(solution)/shard_map/all_to_all | solution.py:206
  84.2 0.0 copy-done
  84.2 3.9 %dispatch.1 = bf16[64,2,8,4096]{3,2,1,0:T(8,128)(2,1)S(1)} custom-call(bf16[8,128,512]{2,1,0:T(8,128)(2,1)S(1)} %all-to-all-done.1.attn_ref, bf16[128,4096]{1,0:T(8,128)(2,1)S(1)} %bitcast.25, bf16[1,4096]{1,0:T(2,128)(2,1)S(1)} %broadcast_in_dim.54.gain_ref, bf16[512,128]{1,0:T(8,128)(2,1)S(1)} %fusion.4.pick_ref), custom_call_target="tpu_custom_call" | custom-call | tf_op jit(solution)/shard_map/dispatch/pallas_call | solution.py:85
  88.1 106.0 %all_to_all.21 = bf16[128,8,4096]{2,1,0:T(8,128)(2,1)} all-to-all(bf16[128,8,4096]{2,1,0:T(8,128)(2,1)S(1)} %bitcast.24), channel_id=1, replica_groups=mesh['seq'=8,'exp'=16] {'seq','exp'}, dimensions={0} | all-to-all | bytes 16777216 | tf_op jit(solution)/shard_map/all_to_all | solution.py:208
  194.1 28.6 %expert.1 = bf16[1024,4096]{1,0:T(8,128)(2,1)} custom-call(bf16[1024,4096]{1,0:T(8,128)(2,1)} %bitcast.29, bf16[4096,768]{1,0:T(8,128)(2,1)} %bitcast.32, bf16[4096,768]{1,0:T(8,128)(2,1)} %bitcast.33, bf16[768,4096]{1,0:T(8,128)(2,1)} %bitcast.34), custom_call_target="tpu_custom_call" | custom-call | tf_op jit(solution)/shard_map/expert/pallas_call | solution.py:114
  222.7 0.0 copy-start.4
  222.7 7.9 %all-to-all-start.3 = ((bf16[128,8,4096]{2,1,0:T(8,128)(2,1)}), bf16[128,8,4096]{2,1,0:T(8,128)(2,1)}, u32[]{:S(2)}, u32[]{:S(2)}) async-start(bf16[128,8,4096]{2,1,0:T(8,128)(2,1)} %bitcast.28), calls=%async_computation.3 | async-start | bytes 16777216 | tf_op jit(solution)/shard_map/all_to_all | solution.py:216
  230.6 0.0 copy-done.4
  230.6 0.1 select_reduce_fusion
  230.7 0.2 copy.30
  231.0 0.1 copy.32.flag_ref
  231.1 0.1 subtract_convert_fusion
  231.2 101.6 %all-to-all-done.3 = bf16[128,8,4096]{2,1,0:T(8,128)(2,1)} async-done(((bf16[128,8,4096]{2,1,0:T(8,128)(2,1)}), bf16[128,8,4096]{2,1,0:T(8,128)(2,1)}, u32[]{:S(2)}, u32[]{:S(2)}) %all-to-all-start.3) | async-done | bytes 8388640 | tf_op jit(solution)/shard_map/all_to_all | solution.py:216
  332.8 0.0 copy-start.1
  332.8 1.2 copy-done.1
  334.0 8.3 %combine.1 = bf16[128,4096]{1,0:T(8,128)(2,1)} custom-call(bf16[1024,4096]{1,0:T(8,128)(2,1)} %bitcast.13.back_ref, bf16[256,1024]{1,0:T(8,128)(2,1)S(1)} %pad_maximum_fusion.1.mix_ref, bf16[8,128,512]{2,1,0:T(8,128)(2,1)S(1)} %all-to-all-done.1.attn_ref, bf16[128,4096]{1,0:T(8,128)(2,1)S(1)} %bitcast.26, bf16[128,4096]{1,0:T(8,128)(2,1)S(1)} %bitcast.27, ...), custom_call_target="tpu_custom_call" | custom-call | tf_op jit(solution)/shard_map/combine/pallas_call | solution.py:142
  (8 shorter events, 0.2 us)
Async XLA Ops:
  55.2 13.9 %copy-start.3 = (bf16[4096]{0:T(1024)(128)(2,1)S(1)}, bf16[4096]{0:T(1024)(128)(2,1)}, u32[]{:S(2)}) copy-start(bf16[4096]{0:T(1024)(128)(2,1)} %param.17) | copy-start | bytes 24580
  55.2 14.0 %copy-start.5 = (s32[1,128]{1,0:T(1,128)S(1)}, s32[1,128]{1,0:T(1,128)}, u32[]{:S(2)}) copy-start(s32[1,128]{1,0:T(1,128)} %param.18) | copy-start | bytes 1540
  55.2 14.1 %copy-start.2 = (s32[1,128,8]{1,2,0:T(8,128)S(1)}, s32[1,128,8]{1,2,0:T(8,128)}, u32[]{:S(2)}) copy-start(s32[1,128,8]{1,2,0:T(8,128)} %param.19) | copy-start | bytes 12292
  55.2 29.0 %copy-start = (bf16[1,128,4096]{2,1,0:T(8,128)(2,1)S(1)}, bf16[1,128,4096]{2,1,0:T(8,128)(2,1)}, u32[]{:S(2)}) copy-start(bf16[1,128,4096]{2,1,0:T(8,128)(2,1)} %param.15) | copy-start | bytes 3145732
  64.6 19.6 %all-to-all-start.1 = ((bf16[8,128,512]{2,1,0:T(8,128)(2,1)}), bf16[8,128,512]{2,1,0:T(8,128)(2,1)S(1)}, u32[]{:S(2)}, u32[]{:S(2)}) async-start(bf16[8,128,512]{2,1,0:T(8,128)(2,1)} %attend.1), calls=%async_computation.1 | async-start | bytes 2097152 | tf_op jit(solution)/shard_map/all_to_all | solution.py:206
  222.7 7.9 %copy-start.4 = (f32[1,128,8]{1,2,0:T(8,128)S(1)}, f32[1,128,8]{1,2,0:T(8,128)}, u32[]{:S(2)}) copy-start(f32[1,128,8]{1,2,0:T(8,128)} %param.20) | copy-start | bytes 12292
  222.7 110.1 %all-to-all-start.3 = ((bf16[128,8,4096]{2,1,0:T(8,128)(2,1)}), bf16[128,8,4096]{2,1,0:T(8,128)(2,1)}, u32[]{:S(2)}, u32[]{:S(2)}) async-start(bf16[128,8,4096]{2,1,0:T(8,128)(2,1)} %bitcast.28), calls=%async_computation.3 | async-start | bytes 16777216 | tf_op jit(solution)/shard_map/all_to_all | solution.py:216
  332.8 1.2 copy-start.1

commit v2 on v1

v2 whole, which is shorter than its diff:
```python
import math

import jax
import jax.numpy as jnp
from jax import lax
from jax.experimental import pallas as pl
from jax.experimental.pallas import tpu as pltpu
from jax.sharding import PartitionSpec as P

HEAD_DIM = 128
TOP = 8
SLOTS = 8
bf16 = jnp.bfloat16
f32 = jnp.float32


def params(mib):
    return pltpu.CompilerParams(vmem_limit_bytes=mib * 1024 * 1024)


def iota(shape, dim):
    return lax.broadcasted_iota(jnp.int32, shape, dim)


def ones(where):
    return jnp.where(where, jnp.float32(1.0), jnp.float32(0.0)).astype(bf16)


def dot(a, b, dims=((1,), (0,))):
    return lax.dot_general(a, b, (dims, ((), ())), preferred_element_type=f32)


def prepare_kernel(
    q_ref, k_ref, v_ref, res_ref, flag_ref, ids_ref, gates_ref, out_ref, meta_ref, own_ref, pick_ref
):
    rows = q_ref.shape[0]
    most = pick_ref.shape[0]

    @pl.when(pl.program_id(0) == 0)
    def _():
        experts = own_ref.shape[2]
        flags = ones(jnp.broadcast_to(flag_ref[...], (rows, rows)) == 1)
        upper = ones(iota((rows, rows), 0) < iota((rows, rows), 1))
        lower = ones(iota((rows, rows), 0) > iota((rows, rows), 1))
        eye = ones(iota((rows, rows), 0) == iota((rows, rows), 1))
        rank = dot(flags, upper)[:1].astype(jnp.int32)
        pick = ones((iota((most, rows), 0) == rank) & (flag_ref[...] == 1))
        pick_ref[...] = pick
        masked = dot(eye, flags, ((1,), (1,)))[:, :1] > 0.5
        named = jnp.zeros((rows, experts), f32)
        gates = jnp.zeros((rows, experts), f32)
        for k in range(TOP):
            hit = (ids_ref[:, k : k + 1] == iota((rows, experts), 1)) & masked
            named = jnp.where(hit, 1.0, named)
            gates = jnp.where(hit, gates_ref[:, k : k + 1], gates)
        place = named * (dot(lower, named.astype(bf16)) + 1.0)
        place = place.astype(bf16)
        high = gates.astype(bf16)
        own_ref[0] = place
        own_ref[1] = high
        own_ref[2] = (gates - high.astype(f32)).astype(bf16)
        meta_ref[...] = jnp.zeros_like(meta_ref)
        meta_ref[:experts, :most] = dot(place, pick, ((0,), (1,))).astype(bf16)
        meta_ref[experts:] = pick

    out_ref[0, :rows] = q_ref[...]
    out_ref[0, rows : 2 * rows] = k_ref[...]
    out_ref[0, 2 * rows : 3 * rows] = v_ref[...]
    out_ref[0, 3 * rows :] = dot(pick_ref[...], res_ref[...]).astype(bf16)


def prepare(q, k, v, res, flags, ids, gates, groups, experts, most):
    rows, width = q.shape
    cols = width // groups
    piece = pl.BlockSpec((rows, cols), lambda j: (0, j))
    return pl.pallas_call(
        prepare_kernel,
        grid=(groups,),
        in_specs=[
            piece,
            piece,
            piece,
            piece,
            pl.BlockSpec((1, rows), lambda j: (0, 0)),
            pl.BlockSpec((rows, TOP), lambda j: (0, 0)),
            pl.BlockSpec((rows, TOP), lambda j: (0, 0)),
        ],
        out_specs=[
            pl.BlockSpec((1, 3 * rows + most, cols), lambda j: (j, 0, 0)),
            pl.BlockSpec((experts + most, rows), lambda j: (0, 0)),
            pl.BlockSpec((3, rows, experts), lambda j: (0, 0, 0)),
        ],
        out_shape=[
            jax.ShapeDtypeStruct((groups, 3 * rows + most, cols), bf16),
            jax.ShapeDtypeStruct((experts + most, rows), bf16),
            jax.ShapeDtypeStruct((3, rows, experts), bf16),
        ],
        scratch_shapes=[pltpu.VMEM((most, rows), bf16)],
        compiler_params=params(24),
        name="prepare",
    )(q, k, v, res, flags, ids, gates)


def attend_kernel(in_ref, meta_ref, gain_ref, attn_ref, out_ref, place_ref):
    blocks, rows, _ = attn_ref.shape
    experts = out_ref.shape[0]
    most = in_ref.shape[1] - 3 * rows
    length = blocks * rows

    @pl.when(pl.program_id(0) == 0)
    def _():
        for b in range(blocks):
            table = meta_ref[b, :experts, :most].astype(f32)
            wanted = iota((experts, SLOTS, most), 1).astype(f32) + 1.0
            hit = jnp.where(table[:, None, :] == wanted, 1.0, 0.0)
            place_ref[b] = hit.reshape(experts * SLOTS, most).astype(bf16)

    scale = math.log2(math.e) / math.sqrt(HEAD_DIM)
    k_all = in_ref[:, rows : 2 * rows].reshape(length, HEAD_DIM)
    v_all = in_ref[:, 2 * rows : 3 * rows].reshape(length, HEAD_DIM)
    gain = gain_ref[...].astype(f32)
    step = 2
    for first in range(0, blocks, step):
        q_part = in_ref[first : first + step, :rows].reshape(step * rows, HEAD_DIM)
        scores = dot(q_part, k_all, ((1,), (1,)))
        peak = jnp.max(scores, axis=-1, keepdims=True)
        expo = jnp.exp2((scores - peak) * scale)
        total = jnp.sum(expo, axis=-1, keepdims=True)
        mixed = dot(expo.astype(bf16), v_all)
        attn = (mixed / total).astype(bf16).reshape(step, rows, HEAD_DIM)
        attn_ref[first : first + step] = attn
        for i in range(step):
            b = first + i
            hidden = dot(meta_ref[b, experts:], attn[i]) + in_ref[b, 3 * rows :].astype(f32)
            sent = dot(place_ref[b], (hidden * gain).astype(bf16))
            sent = sent.reshape(experts, SLOTS, HEAD_DIM).astype(bf16)
            out_ref[:, 0, b] = sent
            out_ref[:, 1, b] = sent


def attend(pieces, meta, gain, rows, experts):
    blocks, total, cols = pieces.shape
    most = total - 3 * rows
    return pl.pallas_call(
        attend_kernel,
        grid=(cols // HEAD_DIM,),
        in_specs=[
            pl.BlockSpec((blocks, total, HEAD_DIM), lambda h: (0, 0, h)),
            pl.BlockSpec(meta.shape, lambda h: (0, 0, 0)),
            pl.BlockSpec((1, HEAD_DIM), lambda h: (0, h)),
        ],
        out_specs=[
            pl.BlockSpec((blocks, rows, HEAD_DIM), lambda h: (0, 0, h)),
            pl.BlockSpec((experts, 2, blocks, SLOTS, HEAD_DIM), lambda h: (0, 0, 0, 0, h)),
        ],
        out_shape=[
            jax.ShapeDtypeStruct((blocks, rows, cols), bf16),
            jax.ShapeDtypeStruct((experts, 2, blocks, SLOTS, cols), bf16),
        ],
        scratch_shapes=[pltpu.VMEM((blocks, experts * SLOTS, most), bf16)],
        compiler_params=params(40),
        name="attend",
    )(pieces, meta, gain)


CHUNKS = 4


def expert_kernel(
    rows_ref, back_ref, gate_hbm, up_hbm, down_hbm, out_ref, x_ref, gate_ref, up_ref, down_ref, sems
):
    step = pl.program_id(0)
    groups, part, per, cols = rows_ref.shape
    tile = part * per
    width, half = gate_ref.shape
    depth = width // CHUNKS

    def loads(c):
        here = pl.ds(c * depth, depth)
        return (
            pltpu.make_async_copy(gate_hbm.at[here], gate_ref.at[here], sems.at[0, c]),
            pltpu.make_async_copy(up_hbm.at[here], up_ref.at[here], sems.at[1, c]),
        )

    down_load = pltpu.make_async_copy(down_hbm, down_ref, sems.at[2, 0])

    @pl.when(step == 0)
    def _():
        for c in range(CHUNKS):
            for load in loads(c):
                load.start()
        down_load.start()

    square = jnp.zeros((tile, 1), f32)
    for g in range(groups):
        piece = rows_ref[g].reshape(tile, cols)
        x_ref[:, g * cols : (g + 1) * cols] = piece
        hidden = piece.astype(f32) * back_ref[:, g * cols : (g + 1) * cols]
        square += jnp.sum(hidden * hidden, axis=-1, keepdims=True)
    scale = lax.rsqrt(square / width + 1e-06)

    def finish(gate_part, up_part):
        gate_part = gate_part * scale
        act = (gate_part / (1.0 + jnp.exp(-gate_part)) * (up_part * scale)).astype(bf16)

        @pl.when(step == 0)
        def _():
            down_load.wait()

        span = 1024
        for c in range(0, width, span):
            result = dot(act, down_ref[:, c : c + span])
            result = result.reshape(part, groups, SLOTS, span).astype(bf16)
            for i in range(part):
                out_ref[:, i, :, c : c + span] = result[i]

    @pl.when(step == 0)
    def _():
        gate_part = jnp.zeros((tile, half), f32)
        up_part = jnp.zeros((tile, half), f32)
        for c in range(CHUNKS):
            for load in loads(c):
                load.wait()
            here = slice(c * depth, (c + 1) * depth)
            gate_part += dot(x_ref[:, here], gate_ref[here])
            up_part += dot(x_ref[:, here], up_ref[here])
        finish(gate_part, up_part)

    @pl.when(step > 0)
    def _():
        finish(dot(x_ref[...], gate_ref[...]), dot(x_ref[...], up_ref[...]))


def expert(arrived, back_gain, gate, up, down):
    groups, count, per, cols = arrived.shape
    width, half = gate.shape
    part = 256 // per
    total = count * per
    return pl.pallas_call(
        expert_kernel,
        grid=(count // part,),
        in_specs=[
            pl.BlockSpec((groups, part, per, cols), lambda i: (0, i, 0, 0)),
            pl.BlockSpec((1, width), lambda i: (0, 0)),
            pl.BlockSpec(memory_space=pl.ANY),
            pl.BlockSpec(memory_space=pl.ANY),
            pl.BlockSpec(memory_space=pl.ANY),
        ],
        out_specs=pl.BlockSpec((groups, part, SLOTS, width), lambda i: (0, i, 0, 0)),
        out_shape=jax.ShapeDtypeStruct((groups, count, SLOTS, width), bf16),
        scratch_shapes=[
            pltpu.VMEM((part * per, width), bf16),
            pltpu.VMEM((width, half), bf16),
            pltpu.VMEM((width, half), bf16),
            pltpu.VMEM((half, width), bf16),
            pltpu.SemaphoreType.DMA((3, CHUNKS)),
        ],
        compiler_params=params(50),
        cost_estimate=pl.CostEstimate(
            flops=6 * total * width * half,
            bytes_accessed=2 * (3 * width * half + 2 * total * width),
            transcendentals=total * half,
        ),
        name="expert",
    )(arrived, back_gain, gate, up, down)


def combine_kernel(back_ref, own_ref, attn_ref, res_ref, cached_ref, flag_ref, out_ref, mix_ref):
    rows, experts = own_ref.shape[1:]
    slots = back_ref.shape[0]
    per = slots // experts

    @pl.when(pl.program_id(0) == 0)
    def _():
        column = iota((experts, slots), 1)
        spread = ones(iota((experts, slots), 0) == column // per)
        wanted = (iota((rows, slots), 1) % SLOTS + 1).astype(f32)
        hit = dot(own_ref[0], spread) == wanted
        mix_ref[:rows] = jnp.where(hit, dot(own_ref[1], spread), 0.0).astype(bf16)
        mix_ref[rows:] = jnp.where(hit, dot(own_ref[2], spread), 0.0).astype(bf16)

    both = dot(mix_ref[...], back_ref[...])
    mixed = both[:rows] + both[rows:]
    moe = jnp.where(flag_ref[...] == 1, mixed, cached_ref[...].astype(f32))
    hid = res_ref[...].astype(f32) + attn_ref[0].astype(f32)
    out_ref[...] = (hid + moe).astype(bf16)


def combine(back, own, attn, residual, cached, flags):
    groups, rows, cols = attn.shape
    slots, width = back.shape
    return pl.pallas_call(
        combine_kernel,
        grid=(groups,),
        in_specs=[
            pl.BlockSpec((slots, cols), lambda j: (0, j)),
            pl.BlockSpec(own.shape, lambda j: (0, 0, 0)),
            pl.BlockSpec((1, rows, cols), lambda j: (j, 0, 0)),
            pl.BlockSpec((rows, cols), lambda j: (0, j)),
            pl.BlockSpec((rows, cols), lambda j: (0, j)),
            pl.BlockSpec((rows, 1), lambda j: (0, 0)),
        ],
        out_specs=pl.BlockSpec((rows, cols), lambda j: (0, j)),
        out_shape=jax.ShapeDtypeStruct((rows, width), bf16),
        scratch_shapes=[pltpu.VMEM((2 * rows, slots), bf16)],
        compiler_params=params(40),
        name="combine",
    )(back, own, attn, residual, cached, flags)


def exchange(blocks, axes):
    return lax.all_to_all(blocks, axes, split_axis=0, concat_axis=0, tiled=True)


def per_device(
    queries,
    keys,
    values,
    residual_in,
    cached_moe,
    norm_gain,
    still_masked,
    expert_ids,
    gate_weights,
    w_gate,
    w_up,
    w_down,
):
    rows, width = queries.shape[1:]
    seq_count = lax.axis_size("seq")
    exp_count = lax.axis_size("exp")
    devices = seq_count * exp_count
    experts = devices // 2
    cols = width // seq_count
    most = rows * 3 // 8

    pieces, meta, own = prepare(
        queries[0],
        keys[0],
        values[0],
        residual_in[0],
        still_masked,
        expert_ids[0],
        gate_weights[0],
        seq_count,
        experts,
        most,
    )
    meta = lax.all_gather(meta, "seq", axis=0)
    pieces = exchange(pieces, "seq")
    gain = norm_gain[None, :]
    own_gain = lax.dynamic_slice_in_dim(gain, lax.axis_index("seq") * cols, cols, 1)
    back_gain = 1.0 / gain.astype(f32)

    attn, outgoing = attend(pieces, meta, own_gain, rows, experts)
    arrived = exchange(outgoing.reshape(devices, seq_count * SLOTS, cols), ("seq", "exp"))
    attn, arrived = lax.optimization_barrier((attn, arrived))
    attn = exchange(attn, "seq")
    arrived = arrived.reshape(seq_count, exp_count, seq_count * SLOTS, cols)
    done = expert(arrived, back_gain, w_gate[0], w_up[0], w_down[0])
    back = exchange(done.reshape(devices, SLOTS, width), ("seq", "exp"))
    out = combine(
        back.reshape(devices * SLOTS, width),
        own,
        attn,
        residual_in[0],
        cached_moe[0],
        still_masked[0][:, None],
    )
    return out[None]


def solution(mesh):
    return jax.shard_map(
        per_device,
        mesh=mesh,
        in_specs=(
            P("exp", "seq", None),
            P("exp", "seq", None),
            P("exp", "seq", None),
            P("exp", "seq", None),
            P("exp", "seq", None),
            P(),
            P("exp", "seq"),
            P("exp", "seq", None),
            P("exp", "seq", None),
            P(("seq", "exp"), None, None),
            P(("seq", "exp"), None, None),
            P(("seq", "exp"), None, None),
        ),
        out_specs=P("exp", "seq", None),
        check_vma=False,
    )
```

time: 347 us -> 358 us (1.032)
  blocking collectives: 150 us -> 49.5 us
  waiting for transfers between devices: 116 us -> 204 us
  starting transfers between devices: 12.4 us -> 30.3 us
  Pallas kernels: 50.2 us -> 56.3 us
    all_to_all x2 -> x0, blocking collectives: 150 us -> none  [the longest x1 106 us: per_device(): lax.all_to_all(outgoing.reshape(devices, SLOTS, width), ('seq', 'exp'), s...]
    all_to_all x2 -> x4, waiting for transfers between devices: 116 us -> 204 us  [exchange(): return lax.all_to_all(blocks, axes, split_axis=0, concat_axis=0, tiled=True)]
    all_gather x0 -> x1, blocking collectives: none -> 49.5 us  [per_device(): meta = lax.all_gather(meta, 'seq', axis=0)]
    all_to_all x2 -> x4, starting transfers between devices: 12.4 us -> 30.3 us  [exchange(): return lax.all_to_all(blocks, axes, split_axis=0, concat_axis=0, tiled=True)]
    unnamed x15 -> x32, local copies, waits for them, and re-layouts: 6.09 us -> 14.3 us
    pallas_call x3, Pallas kernels: 41.9 us -> 47.6 us  [the longest x1 28.9 us: expert(): pl.pallas_call(expert_kernel, grid=(count // part,), in_specs=[pl.BlockSp...]
    reshape x2 -> x0, local copies, waits for them, and re-layouts: 4.83 us -> none  [the longest x1 4.63 us: per_device(): qkv = qkv.reshape(3, rows, seq_count, cols).transpose(2, 0, 1, 3)]
  transfers between devices with their start and end apart: 2 -> 4, of which waited for: 2 -> 2; matrix products, arithmetic and copies ran while one was open for 0% -> 0% of each run, Pallas kernels for 0% -> 8%
where the time goes in v2:
time: 358 us; the launch traced here: 355 us
  waiting for transfers between devices  204 us (57%)
  Pallas kernels  56.3 us (16%)
  blocking collectives  49.5 us (14%)
  starting transfers between devices  30.3 us (8%)
  local copies, waits for them, and re-layouts  14.5 us (4%)
    all_to_all x4, waiting for transfers between devices, exchange(): return lax.all_to_all(blocks, axes, split_axis=0, concat_axis=0, tiled=True)  204 us
    all_gather x1, blocking collectives, per_device(): meta = lax.all_gather(meta, 'seq', axis=0)  49.5 us
    all_to_all x4, starting transfers between devices, exchange(): return lax.all_to_all(blocks, axes, split_axis=0, concat_axis=0, tiled=True)  30.3 us
    pallas_call x1, Pallas kernels, expert(): pl.pallas_call(expert_kernel, grid=(count // part,), in_specs=[pl.BlockSp...  28.9 us
    pallas_call x1, Pallas kernels, attend(): pl.pallas_call(attend_kernel, grid=(cols // HEAD_DIM,), in_specs=[pl.Bloc...  16.3 us
    unnamed x32, local copies, waits for them, and re-layouts  14.3 us
    pallas_call x1, Pallas kernels, combine(): pl.pallas_call(combine_kernel, grid=(groups,), in_specs=[pl.BlockSpec((sl...  8.71 us
  transfers between devices with their start and end apart: 4, of which 2 were waited for; matrix products, arithmetic and copies ran while one was open for 0% of the time, Pallas kernels for 8%

profile of v2, /device:TPU:1, one launch (start us, length us, event | category | flops | bytes accessed | tf_op | source)
XLA Modules:
  0.0 354.9 jit_solution(16563316209785946689)
XLA Ops:
  0.0 0.0 copy-start.14
  0.0 0.8 copy.13
  0.8 0.8 copy.14
  1.6 0.0 copy-start.1
  1.6 1.2 copy-done.1
  2.8 0.0 copy-start.4
  2.8 1.2 copy-done.4
  4.0 0.0 copy-start.5
  4.0 1.2 copy-done.5
  5.3 0.0 copy-start.6
  5.3 1.2 copy-done.6
  6.5 0.0 copy-start.12
  6.5 0.7 copy-done.12
  7.1 2.3 prepare.1
  9.5 0.0 copy-start.3
  9.5 1.8 copy-done.3
  11.3 0.0 copy-start.9
  11.3 0.6 copy-done.9
  11.9 0.0 copy-start.11
  11.9 0.6 copy-done.11
  12.5 5.8 %all-to-all-start = ((bf16[8,432,512]{2,1,0:T(8,128)(2,1)}), bf16[8,432,512]{2,1,0:T(8,128)(2,1)S(1)}, u32[]{:S(2)}, u32[]{:S(2)}) async-start(bf16[8,432,512]{2,1,0:T(8,128)(2,1)} %copy-done.3), calls=%async_computation | async-start | bytes 7077888 | tf_op jit(solution)/shard_map/all_to_all | solution.py:312
  18.3 0.0 copy-done.14
  18.3 0.1 dynamic-slice.3
  18.4 49.5 %all-gather = bf16[896,128]{1,0:T(8,128)(2,1)} all-gather(bf16[112,128]{1,0:T(8,128)(2,1)} %copy-done.11), channel_id=2, replica_groups=mesh['seq'=8,'exp'=16] {'seq'}, dimensions={0}, use_global_device_ids=true | all-gather | bytes 258048 | tf_op jit(solution)/shard_map/all_gather | solution.py:349
  67.9 0.0 all-to-all-done.in_ref
  67.9 0.0 copy-start.8
  67.9 0.9 copy-done.8
  68.8 16.3 %attend.1 = (bf16[8,128,512]{2,1,0:T(8,128)(2,1)}, bf16[64,2,8,8,512]{4,3,2,1,0:T(8,128)(2,1)S(1)}) custom-call(bf16[8,432,512]{2,1,0:T(8,128)(2,1)S(1)} %all-to-all-done.in_ref, bf16[8,112,128]{2,1,0:T(8,128)(2,1)S(1)} %bitcast.25, bf16[1,512]{1,0:T(2,128)(2,1)S(1)} %dynamic_slice.3.gain_ref), custom_call_target="tpu_custom_call" | custom-call | tf_op jit(solution)/shard_map/attend/pallas_call | solution.py:144
  85.2 0.0 copy-start
  85.2 3.2 copy-done
  88.4 9.7 %all-to-all-start.1 = ((bf16[128,64,512]{2,1,0:T(8,128)(2,1)}), bf16[128,64,512]{2,1,0:T(8,128)(2,1)}, u32[]{:S(2)}, u32[]{:S(2)}) async-start(bf16[128,64,512]{2,1,0:T(8,128)(2,1)} %bitcast.18), calls=%async_computation.1 | async-start | bytes 16777216 | tf_op jit(solution)/shard_map/all_to_all | solution.py:312
  98.0 102.2 %all-to-all-done.1 = bf16[128,64,512]{2,1,0:T(8,128)(2,1)} async-done(((bf16[128,64,512]{2,1,0:T(8,128)(2,1)}), bf16[128,64,512]{2,1,0:T(8,128)(2,1)}, u32[]{:S(2)}, u32[]{:S(2)}) %all-to-all-start.1) | async-done | bytes 8388640 | tf_op jit(solution)/shard_map/all_to_all | solution.py:312
  200.2 7.3 %all-to-all-start.3 = ((bf16[8,128,512]{2,1,0:T(8,128)(2,1)}), bf16[8,128,512]{2,1,0:T(8,128)(2,1)S(1)}, u32[]{:S(2)}, u32[]{:S(2)}) async-start(bf16[8,128,512]{2,1,0:T(8,128)(2,1)} %get-tuple-element.18), calls=%async_computation.3 | async-start | bytes 2097152 | tf_op jit(solution)/shard_map/all_to_all | solution.py:312
  207.5 28.9 %expert.1 = bf16[8,16,8,4096]{3,2,1,0:T(8,128)(2,1)} custom-call(bf16[8,16,64,512]{3,2,1,0:T(8,128)(2,1)} %bitcast.8.rows_ref, f32[1,4096]{1,0:T(1,128)S(1)} %bitcast.28, bf16[4096,768]{1,0:T(8,128)(2,1)} %bitcast.31, bf16[4096,768]{1,0:T(8,128)(2,1)} %bitcast.32, bf16[768,4096]{1,0:T(8,128)(2,1)} %bitcast.33), custom_call_target="tpu_custom_call" | custom-call | flops 19327352832 | bytes 35651584 | tf_op jit(solution)/shard_map/expert/pallas_call | solution.py:239
  236.5 0.0 all-to-all-done.3.attn_ref
  236.5 0.0 copy-start.13
  236.5 0.0 copy-start.2
  236.5 0.0 copy-start.7
  236.5 0.0 copy-start.10
  236.5 7.5 %all-to-all-start.2 = ((bf16[128,8,4096]{2,1,0:T(8,128)(2,1)}), bf16[128,8,4096]{2,1,0:T(8,128)(2,1)}, u32[]{:S(2)}, u32[]{:S(2)}) async-start(bf16[128,8,4096]{2,1,0:T(8,128)(2,1)} %bitcast.30), calls=%async_computation.2 | async-start | bytes 16777216 | tf_op jit(solution)/shard_map/all_to_all | solution.py:312
  244.0 0.0 copy-done.13
  244.0 0.1 copy.15.flag_ref
  244.1 102.1 %all-to-all-done.2 = bf16[128,8,4096]{2,1,0:T(8,128)(2,1)} async-done(((bf16[128,8,4096]{2,1,0:T(8,128)(2,1)}), bf16[128,8,4096]{2,1,0:T(8,128)(2,1)}, u32[]{:S(2)}, u32[]{:S(2)}) %all-to-all-start.2) | async-done | bytes 8388640 | tf_op jit(solution)/shard_map/all_to_all | solution.py:312
  346.2 0.0 copy-done.2
  346.2 0.0 copy-done.7
  346.2 0.0 copy-done.10
  346.2 8.7 %combine.1 = bf16[128,4096]{1,0:T(8,128)(2,1)} custom-call(bf16[1024,4096]{1,0:T(8,128)(2,1)} %bitcast.14.back_ref, bf16[3,128,64]{2,1,0:T(8,128)(2,1)S(1)} %copy-done.10, bf16[8,128,512]{2,1,0:T(8,128)(2,1)S(1)} %all-to-all-done.3.attn_ref, bf16[128,4096]{1,0:T(8,128)(2,1)S(1)} %bitcast.20, bf16[128,4096]{1,0:T(8,128)(2,1)S(1)} %bitcast.24, ...), custom_call_target="tpu_custom_call" | custom-call | tf_op jit(solution)/shard_map/combine/pallas_call | solution.py:292
  (2 shorter events, 0.0 us)
Async XLA Ops:
  0.0 18.3 %copy-start.14 = (bf16[4096]{0:T(1024)(128)(2,1)S(1)}, bf16[4096]{0:T(1024)(128)(2,1)}, u32[]{:S(2)}) copy-start(bf16[4096]{0:T(1024)(128)(2,1)} %param.17) | copy-start | bytes 24580
  1.6 1.2 copy-start.1
  2.8 1.2 copy-start.4
  4.0 1.2 copy-start.5
  5.3 1.2 copy-start.6
  6.5 0.7 copy-start.12
  9.5 1.8 copy-start.3
  11.3 0.6 copy-start.9
  11.9 0.6 copy-start.11
  12.5 55.4 %all-to-all-start = ((bf16[8,432,512]{2,1,0:T(8,128)(2,1)}), bf16[8,432,512]{2,1,0:T(8,128)(2,1)S(1)}, u32[]{:S(2)}, u32[]{:S(2)}) async-start(bf16[8,432,512]{2,1,0:T(8,128)(2,1)} %copy-done.3), calls=%async_computation | async-start | bytes 7077888 | tf_op jit(solution)/shard_map/all_to_all | solution.py:312
  67.9 0.9 copy-start.8
  85.2 3.2 copy-start
  88.4 111.8 %all-to-all-start.1 = ((bf16[128,64,512]{2,1,0:T(8,128)(2,1)}), bf16[128,64,512]{2,1,0:T(8,128)(2,1)}, u32[]{:S(2)}, u32[]{:S(2)}) async-start(bf16[128,64,512]{2,1,0:T(8,128)(2,1)} %bitcast.18), calls=%async_computation.1 | async-start | bytes 16777216 | tf_op jit(solution)/shard_map/all_to_all | solution.py:312
  200.2 36.3 %all-to-all-start.3 = ((bf16[8,128,512]{2,1,0:T(8,128)(2,1)}), bf16[8,128,512]{2,1,0:T(8,128)(2,1)S(1)}, u32[]{:S(2)}, u32[]{:S(2)}) async-start(bf16[8,128,512]{2,1,0:T(8,128)(2,1)} %get-tuple-element.18), calls=%async_computation.3 | async-start | bytes 2097152 | tf_op jit(solution)/shard_map/all_to_all | solution.py:312
  236.5 7.5 %copy-start.13 = (s32[1,128]{1,0:T(1,128)S(1)}, s32[1,128]{1,0:T(1,128)}, u32[]{:S(2)}) copy-start(s32[1,128]{1,0:T(1,128)} %flag_ref.1) | copy-start | bytes 1540
  236.5 109.7 %copy-start.2 = (bf16[1,128,4096]{2,1,0:T(8,128)(2,1)S(1)}, bf16[1,128,4096]{2,1,0:T(8,128)(2,1)}, u32[]{:S(2)}) copy-start(bf16[1,128,4096]{2,1,0:T(8,128)(2,1)} %param.15) | copy-start | bytes 3145732
  236.5 109.7 %copy-start.7 = (bf16[1,128,4096]{2,1,0:T(8,128)(2,1)S(1)}, bf16[1,128,4096]{2,1,0:T(8,128)(2,1)}, u32[]{:S(2)}) copy-start(bf16[1,128,4096]{2,1,0:T(8,128)(2,1)} %param.16) | copy-start | bytes 3145732
  236.5 109.7 %copy-start.10 = (bf16[3,128,64]{2,1,0:T(8,128)(2,1)S(1)}, bf16[3,128,64]{2,1,0:T(8,128)(2,1)}, u32[]{:S(2)}) copy-start(bf16[3,128,64]{2,1,0:T(8,128)(2,1)} %copy-done.9) | copy-start | bytes 147460
  236.5 109.7 %all-to-all-start.2 = ((bf16[128,8,4096]{2,1,0:T(8,128)(2,1)}), bf16[128,8,4096]{2,1,0:T(8,128)(2,1)}, u32[]{:S(2)}, u32[]{:S(2)}) async-start(bf16[128,8,4096]{2,1,0:T(8,128)(2,1)} %bitcast.30), calls=%async_computation.2 | async-start | bytes 16777216 | tf_op jit(solution)/shard_map/all_to_all | solution.py:312

commit v3 on v2

v3 whole, which is shorter than its diff:
```python
import math

import jax
import jax.numpy as jnp
from jax import lax
from jax.experimental import pallas as pl
from jax.experimental.pallas import tpu as pltpu
from jax.sharding import PartitionSpec as P

HEAD_DIM = 128
TOP = 8
SLOTS = 8
bf16 = jnp.bfloat16
f32 = jnp.float32


def params(mib):
    return pltpu.CompilerParams(vmem_limit_bytes=mib * 1024 * 1024)


def iota(shape, dim):
    return lax.broadcasted_iota(jnp.int32, shape, dim)


def ones(where):
    return jnp.where(where, jnp.float32(1.0), jnp.float32(0.0)).astype(bf16)


def dot(a, b, dims=((1,), (0,))):
    return lax.dot_general(a, b, (dims, ((), ())), preferred_element_type=f32)


def prepare_kernel(
    q_ref, k_ref, v_ref, res_ref, flag_ref, ids_ref, gates_ref, out_ref, own_ref, pick_ref, table_ref
):
    rows, cols = q_ref.shape
    experts, most = table_ref.shape

    @pl.when(pl.program_id(0) == 0)
    def _():
        flags = ones(jnp.broadcast_to(flag_ref[...], (rows, rows)) == 1)
        upper = ones(iota((rows, rows), 0) < iota((rows, rows), 1))
        lower = ones(iota((rows, rows), 0) > iota((rows, rows), 1))
        eye = ones(iota((rows, rows), 0) == iota((rows, rows), 1))
        rank = dot(flags, upper)[:1].astype(jnp.int32)
        pick = ones((iota((most, rows), 0) == rank) & (flag_ref[...] == 1))
        pick_ref[...] = pick
        masked = dot(eye, flags, ((1,), (1,)))[:, :1] > 0.5
        named = jnp.zeros((rows, experts), f32)
        gates = jnp.zeros((rows, experts), f32)
        for k in range(TOP):
            hit = (ids_ref[:, k : k + 1] == iota((rows, experts), 1)) & masked
            named = jnp.where(hit, 1.0, named)
            gates = jnp.where(hit, gates_ref[:, k : k + 1], gates)
        place = (named * (dot(lower, named.astype(bf16)) + 1.0)).astype(bf16)
        high = gates.astype(bf16)
        own_ref[0] = place
        own_ref[1] = high
        own_ref[2] = (gates - high.astype(f32)).astype(bf16)
        table_ref[...] = dot(place, pick, ((0,), (1,))).astype(bf16)

    out_ref[0, :rows] = q_ref[...]
    out_ref[0, rows : 2 * rows] = k_ref[...]
    out_ref[0, 2 * rows : 3 * rows] = v_ref[...]
    out_ref[0, 3 * rows : 3 * rows + most] = dot(pick_ref[...], res_ref[...]).astype(bf16)
    extra = 3 * rows + most
    numbers = iota((16, rows), 1).astype(f32).astype(bf16)
    spot = dot(numbers, pick_ref[...], ((1,), (1,))).astype(bf16)
    count = dot(jnp.ones((16, rows), bf16), pick_ref[...], ((1,), (1,)))
    spot = jnp.where(count > 0.5, spot.astype(f32), -1.0).astype(bf16)
    out_ref[0, extra:] = jnp.zeros((16, cols), bf16)
    for h in range(experts // 16):
        out_ref[0, extra:, h * 128 : h * 128 + most] = table_ref[h * 16 : (h + 1) * 16]
        out_ref[0, extra:, h * 128 + 64 : h * 128 + 64 + most] = spot


def prepare(q, k, v, res, flags, ids, gates, groups, experts, most):
    rows, width = q.shape
    cols = width // groups
    total = 3 * rows + most + 16
    piece = pl.BlockSpec((rows, cols), lambda j: (0, j))
    return pl.pallas_call(
        prepare_kernel,
        grid=(groups,),
        in_specs=[
            piece,
            piece,
            piece,
            piece,
            pl.BlockSpec((1, rows), lambda j: (0, 0)),
            pl.BlockSpec((rows, TOP), lambda j: (0, 0)),
            pl.BlockSpec((rows, TOP), lambda j: (0, 0)),
        ],
        out_specs=[
            pl.BlockSpec((1, total, cols), lambda j: (j, 0, 0)),
            pl.BlockSpec((3, rows, experts), lambda j: (0, 0, 0)),
        ],
        out_shape=[
            jax.ShapeDtypeStruct((groups, total, cols), bf16),
            jax.ShapeDtypeStruct((3, rows, experts), bf16),
        ],
        scratch_shapes=[pltpu.VMEM((most, rows), bf16), pltpu.VMEM((experts, most), bf16)],
        compiler_params=params(60),
        name="prepare",
    )(q, k, v, res, flags, ids, gates)


def attend_kernel(
    in_ref, table_ref, gain_ref, attn_ref, first_ref, second_ref, place_ref, spot_ref, v_ref
):
    blocks, rows, cols = attn_ref.shape
    experts = first_ref.shape[0]
    most = spot_ref.shape[2]
    length = blocks * rows
    heads = cols // HEAD_DIM
    part = SLOTS // 2

    @pl.when(pl.program_id(0) == 0)
    def _():
        inner = iota((16, SLOTS, 2 * most), 1)
        mine = inner // part == iota((16, SLOTS, 2 * most), 2) // most
        slot = (inner % part + 1).astype(f32)
        for b in range(0, blocks, 2):
            for h in range(experts // 16):
                here = slice(h * 128, h * 128 + most)
                pair = [table_ref[b + i, :, here].astype(f32) for i in range(2)]
                table = jnp.concatenate(pair, axis=1)[:, None, :]
                for q in range(2):
                    hit = jnp.where(mine & (table == slot + q * part), 1.0, 0.0)
                    hit = hit.reshape(128, 2 * most).astype(bf16)
                    place_ref[q, b // 2, h * 128 : (h + 1) * 128] = hit
            for i in range(2):
                spot = table_ref[b + i, :, 64 : 64 + most].astype(f32)[:1]
                spot_ref[b + i] = ones(iota((rows, most), 0).astype(f32) == spot)
        v_ref[:, HEAD_DIM:] = jnp.ones((length, HEAD_DIM), bf16)

    scale = math.log2(math.e) / math.sqrt(HEAD_DIM)
    gain = gain_ref[...].astype(f32)
    step = 2
    for h in range(heads):
        here = slice(h * HEAD_DIM, (h + 1) * HEAD_DIM)
        k_all = in_ref[:, rows : 2 * rows, here].reshape(length, HEAD_DIM)
        v_ref[:, :HEAD_DIM] = in_ref[:, 2 * rows : 3 * rows, here].reshape(length, HEAD_DIM)
        for first in range(0, blocks, step):
            q_part = in_ref[first : first + step, :rows, here].reshape(step * rows, HEAD_DIM)
            scores = dot(q_part, k_all, ((1,), (1,)))
            peak = jnp.max(scores, axis=-1, keepdims=True)
            expo = jnp.exp2((scores - peak) * scale).astype(bf16)
            mixed = dot(expo, v_ref[...])
            attn = (mixed[:, :HEAD_DIM] / mixed[:, HEAD_DIM:]).astype(bf16)
            attn_ref[first : first + step, :, here] = attn.reshape(step, rows, HEAD_DIM)
    for b in range(0, blocks, 2):
        pair = []
        for i in range(b, b + 2):
            hidden = dot(spot_ref[i], attn_ref[i], ((0,), (0,)))
            hidden += in_ref[i, 3 * rows : 3 * rows + most].astype(f32)
            pair.append((hidden * gain).astype(bf16))
        both = jnp.concatenate(pair, axis=0)
        for q, out_ref in enumerate((first_ref, second_ref)):
            sent = dot(place_ref[q, b // 2], both)
            sent = sent.reshape(experts, SLOTS, cols).astype(bf16)
            out_ref[:, 0, b // 2] = sent
            out_ref[:, 1, b // 2] = sent


def attend(pieces, gain, rows, experts, heads=2):
    blocks, total, cols = pieces.shape
    most = total - 3 * rows - 16
    span = heads * HEAD_DIM
    sent = pl.BlockSpec((experts, 2, blocks // 2, SLOTS, span), lambda h: (0, 0, 0, 0, h))
    return pl.pallas_call(
        attend_kernel,
        grid=(cols // span,),
        in_specs=[
            pl.BlockSpec((blocks, total, span), lambda h: (0, 0, h)),
            pl.BlockSpec((blocks, 16, cols), lambda h: (0, total // 16 - 1, 0)),
            pl.BlockSpec((1, span), lambda h: (0, h)),
        ],
        out_specs=[pl.BlockSpec((blocks, rows, span), lambda h: (0, 0, h)), sent, sent],
        out_shape=[
            jax.ShapeDtypeStruct((blocks, rows, cols), bf16),
            jax.ShapeDtypeStruct((experts, 2, blocks // 2, SLOTS, cols), bf16),
            jax.ShapeDtypeStruct((experts, 2, blocks // 2, SLOTS, cols), bf16),
        ],
        scratch_shapes=[
            pltpu.VMEM((2, blocks // 2, experts * SLOTS, 2 * most), bf16),
            pltpu.VMEM((blocks, rows, most), bf16),
            pltpu.VMEM((blocks * rows, 2 * HEAD_DIM), bf16),
        ],
        compiler_params=params(60),
        name="attend",
    )(pieces, pieces, gain)


def open_kernel(rows_ref, gain_ref, gate_ref, up_ref, out_ref, scale_ref):
    groups, count, per, cols = rows_ref.shape
    total = count * per

    @pl.when(pl.program_id(0) == 0)
    def _():
        back = 1.0 / gain_ref[...].astype(f32)
        square = jnp.zeros((total, 128), f32)
        for g in range(groups):
            hidden = rows_ref[g].reshape(total, cols).astype(f32)
            hidden = hidden * back[:, g * cols : (g + 1) * cols]
            for c in range(0, cols, 128):
                square += hidden[:, c : c + 128] * hidden[:, c : c + 128]
        mean = jnp.sum(square, axis=-1, keepdims=True) / (groups * cols)
        scale_ref[...] = lax.rsqrt(mean + 1e-06)

    gate_part = jnp.zeros((total, out_ref.shape[1]), f32)
    up_part = jnp.zeros((total, out_ref.shape[1]), f32)
    for g in range(groups):
        x = rows_ref[g].reshape(total, cols)
        gate_part += dot(x, gate_ref[g * cols : (g + 1) * cols])
        up_part += dot(x, up_ref[g * cols : (g + 1) * cols])
    gate_part = gate_part * scale_ref[...]
    act = gate_part / (1.0 + jnp.exp(-gate_part)) * (up_part * scale_ref[...])
    out_ref[...] = act.astype(bf16)


def expert_open(arrived, gain, gate, up):
    groups, count, per, cols = arrived.shape
    width, half = gate.shape
    total = count * per
    span = 256
    weight = pl.BlockSpec((width, span), lambda n: (0, n))
    return pl.pallas_call(
        open_kernel,
        grid=(half // span,),
        in_specs=[
            pl.BlockSpec((groups, count, per, cols), lambda n: (0, 0, 0, 0)),
            pl.BlockSpec((1, width), lambda n: (0, 0)),
            weight,
            weight,
        ],
        out_specs=pl.BlockSpec((total, span), lambda n: (0, n)),
        out_shape=jax.ShapeDtypeStruct((total, half), bf16),
        scratch_shapes=[pltpu.VMEM((total, 1), f32)],
        compiler_params=params(60),
        cost_estimate=pl.CostEstimate(
            flops=4 * total * width * half,
            bytes_accessed=4 * width * half + 2 * total * (width + half),
            transcendentals=total * half,
        ),
        name="expert_open",
    )(arrived, gain, gate, up)


def close_kernel(
    side_ref, mine_ref, other_ref, own_a, own_b, far_a, far_b, out_ref
):
    del side_ref
    groups, count, _, span = out_ref.shape
    left = dot(mine_ref[...], own_a[...]) + dot(other_ref[...], far_a[...])
    right = dot(mine_ref[...], own_b[...]) + dot(other_ref[...], far_b[...])
    total = left.shape[0]
    part = SLOTS // 2
    low = iota((total, span), 0) % SLOTS < part
    even = jnp.where(low, left, pltpu.roll(right, part, 0))
    odd = jnp.where(low, pltpu.roll(left, total - part, 0), right)
    for i, tile in enumerate((even, odd)):
        tile = tile.reshape(count, groups // 2, SLOTS, span).astype(bf16)
        for p in range(count):
            for b in range(groups // 2):
                out_ref[2 * b + i, p] = tile[p, b]


def expert_close(side, mine, other, down, far, groups, count):
    total, half = mine.shape
    width = far.shape[1]
    span = 512
    steps = width // 2 // span
    act = pl.BlockSpec((total, half), lambda c, side: (0, 0))

    def own(shift):
        return pl.BlockSpec((half, span), lambda c, side: (0, side[0] * 2 * steps + shift + c))

    def recv(shift):
        return pl.BlockSpec((half, span), lambda c, side: (0, shift + c))

    return pl.pallas_call(
        close_kernel,
        grid_spec=pltpu.PrefetchScalarGridSpec(
            num_scalar_prefetch=1,
            grid=(steps,),
            in_specs=[act, act, own(0), own(steps), recv(0), recv(steps)],
            out_specs=pl.BlockSpec((groups, count, SLOTS, span), lambda c, side: (0, 0, 0, c)),
        ),
        out_shape=jax.ShapeDtypeStruct((groups, count, SLOTS, width // 2), bf16),
        compiler_params=params(60),
        cost_estimate=pl.CostEstimate(
            flops=4 * total * width * half,
            bytes_accessed=2 * (2 * width * half + total * (2 * half + width)),
            transcendentals=0,
        ),
        name="expert_close",
    )(side, mine, other, down, down, far, far)


def combine_kernel(first_ref, second_ref, own_ref, attn_ref, res_ref, cached_ref, out_ref, mix_ref):
    rows, experts = own_ref.shape[1:]
    per = first_ref.shape[2]
    slots = experts * per
    part = SLOTS // 2
    step = pl.program_id(0)

    @pl.when(step == 0)
    def _():
        spread = ones(iota((experts, slots), 0) == iota((experts, slots), 1) // per)
        place = dot(own_ref[0], spread)
        high = dot(own_ref[1], spread)
        low = dot(own_ref[2], spread)
        inner = iota((rows, slots), 1) % per
        for side in range(2):
            for q in range(2):
                slot = (inner % part + 1 + q * part).astype(f32)
                hit = (inner // part == side) & (place == slot)
                mix_ref[side, q, :rows] = jnp.where(hit, high, 0.0).astype(bf16)
                mix_ref[side, q, rows:] = jnp.where(hit, low, 0.0).astype(bf16)

    side = step % 2
    cols = out_ref.shape[1]
    both = dot(mix_ref[side, 0], first_ref[:, 0].reshape(slots, cols))
    both += dot(mix_ref[side, 1], second_ref[:, 0].reshape(slots, cols))
    mixed = both[:rows] + both[rows:]
    masked = jnp.max(own_ref[0].astype(f32), axis=-1, keepdims=True) > 0.5
    moe = jnp.where(masked, mixed, cached_ref[...].astype(f32))
    merge, _, piece = attn_ref.shape
    for m in range(merge):
        here = slice(m * piece, (m + 1) * piece)
        hid = res_ref[:, here].astype(f32) + attn_ref[m].astype(f32)
        out_ref[:, here] = (hid + moe[:, here]).astype(bf16)


def combine(first, second, own, attn, residual, cached):
    experts, _, per, cols = first.shape
    groups, rows, piece = attn.shape
    width = groups * piece
    merge = cols // piece
    flat = pl.BlockSpec((rows, cols), lambda j: (0, j))
    back = pl.BlockSpec((experts, 1, per, cols), lambda j: (0, j // 2, 0, 0))
    return pl.pallas_call(
        combine_kernel,
        grid=(width // cols,),
        in_specs=[
            back,
            back,
            pl.BlockSpec(own.shape, lambda j: (0, 0, 0)),
            pl.BlockSpec((merge, rows, piece), lambda j: (j, 0, 0)),
            flat,
            flat,
        ],
        out_specs=flat,
        out_shape=jax.ShapeDtypeStruct((rows, width), bf16),
        scratch_shapes=[pltpu.VMEM((2, 2, 2 * rows, experts * per), bf16)],
        compiler_params=params(60),
        name="combine",
    )(first, second, own, attn, residual, cached)


def exchange(blocks, axes):
    return lax.all_to_all(blocks, axes, split_axis=0, concat_axis=0, tiled=True)


def home(blocks):
    count = blocks.shape[0]
    here = lax.axis_index("seq")
    parts = [lax.dynamic_index_in_dim(blocks, here, 0, keepdims=False)]
    for d in range(1, count):
        part = lax.dynamic_index_in_dim(blocks, (here + d) % count, 0, keepdims=False)
        parts.append(lax.ppermute(part, "seq", [(i, (i + d) % count) for i in range(count)]))
    order = (here - jnp.arange(count, dtype=jnp.int32)) % count
    return jnp.stack(parts)[order]


def per_device(
    queries,
    keys,
    values,
    residual_in,
    cached_moe,
    norm_gain,
    still_masked,
    expert_ids,
    gate_weights,
    w_gate,
    w_up,
    w_down,
):
    rows, width = queries.shape[1:]
    seq_count = lax.axis_size("seq")
    exp_count = lax.axis_size("exp")
    devices = seq_count * exp_count
    experts = devices // 2
    cols = width // seq_count
    most = rows * 3 // 8

    pieces, own = prepare(
        queries[0],
        keys[0],
        values[0],
        residual_in[0],
        still_masked,
        expert_ids[0],
        gate_weights[0],
        seq_count,
        experts,
        most,
    )
    pieces = exchange(pieces, "seq")
    gain = norm_gain[None, :]
    own_gain = lax.dynamic_slice_in_dim(gain, lax.axis_index("seq") * cols, cols, 1)

    exp_index = lax.axis_index("exp")
    side = exp_index % 2
    partner = [(p, p ^ 1) for p in range(exp_count)]
    far = lax.dynamic_slice_in_dim(w_down[0], (1 - side) * (width // 2), width // 2, 1)
    far = lax.ppermute(far, "exp", partner)

    attn, *sent = attend(pieces, own_gain, rows, experts)
    per = seq_count * SLOTS // 2
    sent = [part.reshape(devices, per, cols) for part in sent]
    first = exchange(sent[0], ("seq", "exp"))
    first, sent[1] = lax.optimization_barrier((first, sent[1]))
    second = exchange(sent[1], ("seq", "exp"))

    def experts_on(arrived):
        arrived = arrived.reshape(seq_count, exp_count, per, cols)
        mine = expert_open(arrived, gain, w_gate[0], w_up[0])
        other = lax.ppermute(mine, "exp", partner)
        done = expert_close(side[None], mine, other, w_down[0], far, seq_count, exp_count)
        return done.reshape(devices, SLOTS, width // 4)

    attn = home(attn)
    back = []
    for arrived in (first, second):
        done = experts_on(arrived)
        back.append(exchange(done, ("seq", "exp")).reshape(experts, 2, SLOTS, width // 4))
    out = combine(*back, own, attn, residual_in[0], cached_moe[0])
    return out[None]


def solution(mesh):
    return jax.shard_map(
        per_device,
        mesh=mesh,
        in_specs=(
            P("exp", "seq", None),
            P("exp", "seq", None),
            P("exp", "seq", None),
            P("exp", "seq", None),
            P("exp", "seq", None),
            P(),
            P("exp", "seq"),
            P("exp", "seq", None),
            P("exp", "seq", None),
            P(("seq", "exp"), None, None),
            P(("seq", "exp"), None, None),
            P(("seq", "exp"), None, None),
        ),
        out_specs=P("exp", "seq", None),
        check_vma=False,
    )
```

time: 358 us -> 393 us (1.098)
  starting transfers between devices: 30.3 us -> 45.8 us
  Pallas kernels: 56.3 us -> 67.1 us
  blocking collectives: 49.5 us -> 60.2 us
    ppermute x0 -> x10, waiting for transfers between devices: none -> 163 us  [the longest x1 95.6 us: per_device(): far = lax.ppermute(far, 'exp', partner)]
    all_to_all x4, waiting for transfers between devices: 204 us -> 42.7 us  [exchange(): return lax.all_to_all(blocks, axes, split_axis=0, concat_axis=0, tiled=True)]
    all_to_all x0 -> x1, blocking collectives: none -> 60.2 us  [exchange(): return lax.all_to_all(blocks, axes, split_axis=0, concat_axis=0, tiled=True)]
    all_gather x1 -> x0, blocking collectives: 49.5 us -> none  [per_device(): meta = lax.all_gather(meta, 'seq', axis=0)]
    ppermute x0 -> x10, starting transfers between devices: none -> 13.9 us  [the longest x7 11 us: home(): lax.ppermute(part, 'seq', [(i, (i + d) % count) for i in range(count)])]
    unnamed x32 -> x18, local copies, waits for them, and re-layouts: 14.3 us -> 4.66 us
    pallas_call x1, Pallas kernels: 2.33 us -> 8.01 us  [prepare(): pl.pallas_call(prepare_kernel, grid=(groups,), in_specs=[piece, piece, pi...]
    pallas_call x3 -> x6, Pallas kernels: 53.9 us -> 59 us  [the longest x2 25.2 us: expert_open(): pl.pallas_call(open_kernel, grid=(half // span,), in_specs=[pl.BlockSpec(...]
  transfers between devices with their start and end apart: 4 -> 14, of which waited for: 2 -> 9; matrix products, arithmetic and copies ran while one was open for 0% -> 2% of each run, Pallas kernels for 8% -> 10%
where the time goes in v3:
time: 393 us; the launch traced here: 392 us
  waiting for transfers between devices  206 us (52%)
  Pallas kernels  67.1 us (17%)
  blocking collectives  60.2 us (15%)
  starting transfers between devices  45.8 us (12%)
  local copies, waits for them, and re-layouts  12.8 us (3%)
    ppermute x1, waiting for transfers between devices, per_device(): far = lax.ppermute(far, 'exp', partner)  95.6 us
    all_to_all x1, blocking collectives, exchange(): return lax.all_to_all(blocks, axes, split_axis=0, concat_axis=0, tiled=True)  60.2 us
    ppermute x2, waiting for transfers between devices, experts_on(): other = lax.ppermute(mine, 'exp', partner)  43.7 us
    all_to_all x4, waiting for transfers between devices, exchange(): return lax.all_to_all(blocks, axes, split_axis=0, concat_axis=0, tiled=True)  42.7 us
    all_to_all x4, starting transfers between devices, exchange(): return lax.all_to_all(blocks, axes, split_axis=0, concat_axis=0, tiled=True)  31.9 us
    pallas_call x2, Pallas kernels, expert_open(): pl.pallas_call(open_kernel, grid=(half // span,), in_specs=[pl.BlockSpec(...  25.2 us
    ppermute x7, waiting for transfers between devices, home(): lax.ppermute(part, 'seq', [(i, (i + d) % count) for i in range(count)])  23.9 us
    pallas_call x2, Pallas kernels, expert_close(): pl.pallas_call(close_kernel, grid_spec=pltpu.PrefetchScalarGridSpec(num_s...  14.8 us
  transfers between devices with their start and end apart: 14, of which 9 were waited for; matrix products, arithmetic and copies ran while one was open for 2% of the time, Pallas kernels for 10%

profile of v3, /device:TPU:1, one launch (start us, length us, event | category | flops | bytes accessed | tf_op | source)
XLA Modules:
  0.0 391.9 jit_solution(11857347270461100652)
XLA Ops:
  0.0 1.4 copy.13
  1.4 1.4 copy.14
  2.8 8.0 %prepare.1 = (bf16[8,448,512]{2,1,0:T(8,128)(2,1)}, bf16[3,128,64]{2,1,0:T(8,128)(2,1)}) custom-call(bf16[128,4096]{1,0:T(8,128)(2,1)} %bitcast.64, bf16[128,4096]{1,0:T(8,128)(2,1)} %bitcast.65, bf16[128,4096]{1,0:T(8,128)(2,1)} %bitcast.66, bf16[128,4096]{1,0:T(8,128)(2,1)} %bitcast.62, s32[1,128]{1,0:T(1,128)} %flag_ref.1, s32[128,8]{1,0:T(8,128)} %bitcast.68, ...), custom_call_target="tpu_custom_call" | custom-call | tf_op jit(solution)/shard_map/prepare/pallas_call | solution.py:82
  10.8 6.0 %all-to-all-start = ((bf16[8,448,512]{2,1,0:T(8,128)(2,1)}), bf16[8,448,512]{2,1,0:T(8,128)(2,1)}, u32[]{:S(2)}, u32[]{:S(2)}) async-start(bf16[8,448,512]{2,1,0:T(8,128)(2,1)} %get-tuple-element.12), calls=%async_computation | async-start | bytes 7340032 | tf_op jit(solution)/shard_map/all_to_all | solution.py:363
  16.8 0.0 copy-done.4
  16.8 0.1 dynamic-slice.4
  16.9 0.5 dynamic_slice.33.gain_ref
  17.4 42.7 %all-to-all-done.in_ref.table_ref = bf16[8,448,512]{2,1,0:T(8,128)(2,1)} async-done(((bf16[8,448,512]{2,1,0:T(8,128)(2,1)}), bf16[8,448,512]{2,1,0:T(8,128)(2,1)}, u32[]{:S(2)}, u32[]{:S(2)}) %all-to-all-start) | async-done | bytes 3670048 | tf_op jit(solution)/shard_map/all_to_all | solution.py:363
  60.1 11.8 %attend.1 = (bf16[8,128,512]{2,1,0:T(8,128)(2,1)}, bf16[64,2,4,8,512]{4,3,2,1,0:T(8,128)(2,1)}, bf16[64,2,4,8,512]{4,3,2,1,0:T(8,128)(2,1)}) custom-call(bf16[8,448,512]{2,1,0:T(8,128)(2,1)} %all-to-all-done.in_ref.table_ref, bf16[8,448,512]{2,1,0:T(8,128)(2,1)} %all-to-all-done.in_ref.table_ref, bf16[1,512]{1,0:T(2,128)(2,1)} %dynamic_slice.33.gain_ref), custom_call_target="tpu_custom_call" | custom-call | tf_op jit(solution)/shard_map/attend/pallas_call | solution.py:171
  71.9 60.2 %all_to_all.25 = bf16[128,32,512]{2,1,0:T(8,128)(2,1)} all-to-all(bf16[128,32,512]{2,1,0:T(8,128)(2,1)} %bitcast.61), channel_id=1, replica_groups=mesh['seq'=8,'exp'=16] {'seq','exp'}, dimensions={0} | all-to-all | bytes 8388608 | tf_op jit(solution)/shard_map/all_to_all | solution.py:363
  132.2 6.4 %all-to-all-start.3 = ((bf16[128,32,512]{2,1,0:T(8,128)(2,1)}), bf16[128,32,512]{2,1,0:T(8,128)(2,1)}, u32[]{:S(2)}, u32[]{:S(2)}) async-start(bf16[128,32,512]{2,1,0:T(8,128)(2,1)} %bitcast.59), calls=%async_computation.3 | async-start | bytes 8388608 | tf_op jit(solution)/shard_map/all_to_all | solution.py:363
  138.6 4.0 %dynamic-slice_bitcast_fusion = bf16[768,2048]{1,0:T(8,128)(2,1)} fusion(bf16[1,768,4096]{2,1,0:T(8,128)(2,1)} %param.23, s32[]{:T(128)S(6)} %select_n.91), kind=kLoop, calls=%fused_computation.1 | loop fusion | bytes 6291460 | tf_op jit(solution)/shard_map/dynamic_slice | solution.py:418
  142.6 1.4 collective-permute-start.1
  144.0 0.6 broadcast_in_dim.12.gain_ref
  144.6 12.6 %expert_open.2.mine_ref = bf16[512,768]{1,0:T(8,128)(2,1)} custom-call(bf16[8,16,32,512]{3,2,1,0:T(8,128)(2,1)} %bitcast.60, bf16[1,4096]{1,0:T(2,128)(2,1)} %broadcast_in_dim.12.gain_ref, bf16[4096,768]{1,0:T(8,128)(2,1)} %bitcast.70, bf16[4096,768]{1,0:T(8,128)(2,1)} %bitcast.72), custom_call_target="tpu_custom_call" | custom-call | flops 6442450944 | bytes 17563648 | tf_op jit(solution)/shard_map/expert_open/pallas_call | solution.py:228
  157.1 0.1 collective-permute-start
  157.2 95.6 %collective-permute-done.1.far_a.far_b = bf16[768,2048]{1,0:T(8,128)(2,1)S(1)} collective-permute-done((bf16[768,2048]{1,0:T(8,128)(2,1)}, bf16[768,2048]{1,0:T(8,128)(2,1)S(1)}, u32[]{:S(2)}, u32[]{:S(2)}) %collective-permute-start.1) | collective-permute-done | bytes 3145760 | tf_op jit(solution)/shard_map/ppermute | solution.py:419
  252.8 16.9 %collective-permute-done.other_ref = bf16[512,768]{1,0:T(8,128)(2,1)S(1)} collective-permute-done((bf16[512,768]{1,0:T(8,128)(2,1)}, bf16[512,768]{1,0:T(8,128)(2,1)S(1)}, u32[]{:S(2)}, u32[]{:S(2)}) %collective-permute-start) | collective-permute-done | bytes 786464 | tf_op jit(solution)/shard_map/ppermute | solution.py:431
  269.7 0.0 copy-done
  269.7 0.9 copy-done.2
  270.6 7.4 %expert_close.2 = bf16[8,16,8,1024]{3,2,1,0:T(8,128)(2,1)} custom-call(s32[1]{0:T(128)} %bitcast.side_ref, bf16[512,768]{1,0:T(8,128)(2,1)} %expert_open.2.mine_ref, bf16[512,768]{1,0:T(8,128)(2,1)} %copy-done.2, bf16[768,4096]{1,0:T(8,128)(2,1)} %bitcast.52, bf16[768,4096]{1,0:T(8,128)(2,1)} %bitcast.53, bf16[768,2048]{1,0:T(8,128)(2,1)} %copy-done, ...), custom_call_target="tpu_custom_call" | custom-call | flops 3221225472 | bytes 9961472 | tf_op jit(solution)/shard_map/expert_close/pallas_call | solution.py:282
  278.0 0.0 all-to-all-done.3
  278.0 9.2 %all-to-all-start.2 = ((bf16[128,8,1024]{2,1,0:T(8,128)(2,1)}), bf16[128,8,1024]{2,1,0:T(8,128)(2,1)S(1)}, u32[]{:S(2)}, u32[]{:S(2)}) async-start(bf16[128,8,1024]{2,1,0:T(8,128)(2,1)} %bitcast.57), calls=%async_computation.2 | async-start | bytes 4194304 | tf_op jit(solution)/shard_map/all_to_all | solution.py:363
  287.2 12.6 %expert_open.3.mine_ref = bf16[512,768]{1,0:T(8,128)(2,1)} custom-call(bf16[8,16,32,512]{3,2,1,0:T(8,128)(2,1)} %bitcast.16.rows_ref, bf16[1,4096]{1,0:T(2,128)(2,1)} %broadcast_in_dim.12.gain_ref, bf16[4096,768]{1,0:T(8,128)(2,1)} %bitcast.71, bf16[4096,768]{1,0:T(8,128)(2,1)} %bitcast.73), custom_call_target="tpu_custom_call" | custom-call | flops 6442450944 | bytes 17563648 | tf_op jit(solution)/shard_map/expert_open/pallas_call | solution.py:228
  299.8 1.4 collective-permute-start.2
  301.2 26.8 %collective-permute-done.2.other_ref = bf16[512,768]{1,0:T(8,128)(2,1)S(1)} collective-permute-done((bf16[512,768]{1,0:T(8,128)(2,1)}, bf16[512,768]{1,0:T(8,128)(2,1)S(1)}, u32[]{:S(2)}, u32[]{:S(2)}) %collective-permute-start.2) | collective-permute-done | bytes 786464 | tf_op jit(solution)/shard_map/ppermute | solution.py:431
  328.0 0.9 copy-done.3
  328.9 7.4 %expert_close.3 = bf16[8,16,8,1024]{3,2,1,0:T(8,128)(2,1)} custom-call(s32[1]{0:T(128)} %bitcast.side_ref, bf16[512,768]{1,0:T(8,128)(2,1)} %expert_open.3.mine_ref, bf16[512,768]{1,0:T(8,128)(2,1)} %copy-done.3, bf16[768,4096]{1,0:T(8,128)(2,1)} %bitcast.54, bf16[768,4096]{1,0:T(8,128)(2,1)} %bitcast.55, bf16[768,2048]{1,0:T(8,128)(2,1)} %copy-done, ...), custom_call_target="tpu_custom_call" | custom-call | flops 3221225472 | bytes 9961472 | tf_op jit(solution)/shard_map/expert_close/pallas_call | solution.py:282
  336.3 0.0 all-to-all-done.2
  336.3 10.3 %all-to-all-start.4 = ((bf16[128,8,1024]{2,1,0:T(8,128)(2,1)}), bf16[128,8,1024]{2,1,0:T(8,128)(2,1)}, u32[]{:S(2)}, u32[]{:S(2)}) async-start(bf16[128,8,1024]{2,1,0:T(8,128)(2,1)} %bitcast.56), calls=%async_computation.4 | async-start | bytes 4194304 | tf_op jit(solution)/shard_map/all_to_all | solution.py:363
  346.7 1.4 dynamic-slice_bitcast_fusion.1
  348.1 1.6 collective-permute-start.3
  349.7 1.3 collective-permute-start.4
  351.0 1.6 collective-permute-start.5
  352.6 0.6 collective-permute-start.6
  353.2 2.5 collective-permute-start.7
  355.7 14.4 %collective-permute-done.3 = bf16[128,512]{1,0:T(8,128)(2,1)S(1)} collective-permute-done((bf16[128,512]{1,0:T(8,128)(2,1)S(1)}, bf16[128,512]{1,0:T(8,128)(2,1)S(1)}, u32[]{:S(2)}, u32[]{:S(2)}) %collective-permute-start.3) | collective-permute-done | bytes 131104 | tf_op jit(solution)/shard_map/ppermute | solution.py:372
  370.1 3.4 collective-permute-start.8
  373.5 3.2 collective-permute-done.4
  376.8 0.0 collective-permute-start.9
  376.8 0.8 collective-permute-done.5
  377.6 4.9 %collective-permute-done.6 = bf16[128,512]{1,0:T(8,128)(2,1)S(1)} collective-permute-done((bf16[128,512]{1,0:T(8,128)(2,1)S(1)}, bf16[128,512]{1,0:T(8,128)(2,1)S(1)}, u32[]{:S(2)}, u32[]{:S(2)}) %collective-permute-start.6) | collective-permute-done | bytes 131104 | tf_op jit(solution)/shard_map/ppermute | solution.py:372
  382.6 0.5 collective-permute-done.7
  383.0 0.0 collective-permute-done.8
  383.1 0.0 collective-permute-done.9
  383.1 1.6 gather_fusion
  384.7 0.0 all-to-all-done.4
  384.7 7.2 %combine.1 = bf16[128,4096]{1,0:T(8,128)(2,1)} custom-call(bf16[64,2,8,1024]{3,2,1,0:T(8,128)(2,1)} %bitcast.58, bf16[64,2,8,1024]{3,2,1,0:T(8,128)(2,1)} %bitcast.18.second_ref, bf16[3,128,64]{2,1,0:T(8,128)(2,1)} %get-tuple-element.17.own_ref, bf16[8,128,512]{2,1,0:T(8,128)(2,1)} %gather_fusion, bf16[128,4096]{1,0:T(8,128)(2,1)} %bitcast.63, ...), custom_call_target="tpu_custom_call" | custom-call | tf_op jit(solution)/shard_map/combine/pallas_call | solution.py:343
  (15 shorter events, 0.1 us)
Async XLA Ops:
  10.8 6.0 %copy-start.4 = (bf16[4096]{0:T(1024)(128)(2,1)S(1)}, bf16[4096]{0:T(1024)(128)(2,1)}, u32[]{:S(2)}) copy-start(bf16[4096]{0:T(1024)(128)(2,1)} %param.17) | copy-start | bytes 24580
  10.8 49.3 %all-to-all-start = ((bf16[8,448,512]{2,1,0:T(8,128)(2,1)}), bf16[8,448,512]{2,1,0:T(8,128)(2,1)}, u32[]{:S(2)}, u32[]{:S(2)}) async-start(bf16[8,448,512]{2,1,0:T(8,128)(2,1)} %get-tuple-element.12), calls=%async_computation | async-start | bytes 7340032 | tf_op jit(solution)/shard_map/all_to_all | solution.py:363
  132.2 145.8 %all-to-all-start.3 = ((bf16[128,32,512]{2,1,0:T(8,128)(2,1)}), bf16[128,32,512]{2,1,0:T(8,128)(2,1)}, u32[]{:S(2)}, u32[]{:S(2)}) async-start(bf16[128,32,512]{2,1,0:T(8,128)(2,1)} %bitcast.59), calls=%async_computation.3 | async-start | bytes 8388608 | tf_op jit(solution)/shard_map/all_to_all | solution.py:363
  142.6 110.2 %collective-permute-start.1 = (bf16[768,2048]{1,0:T(8,128)(2,1)}, bf16[768,2048]{1,0:T(8,128)(2,1)S(1)}, u32[]{:S(2)}, u32[]{:S(2)}) collective-permute-start(bf16[768,2048]{1,0:T(8,128)(2,1)} %dynamic-slice_bitcast_fusion), channel_id=1, source_target_pairs={{0,1},{1,0},{2,3},{3,2},{4,5},{5,4},{6,7},{7,6},{8,9},{9,8},{10,11... | collective-permute-start | bytes 9437192 | tf_op jit(solution)/shard_map/ppermute | solution.py:419
  157.1 112.5 %collective-permute-start = (bf16[512,768]{1,0:T(8,128)(2,1)}, bf16[512,768]{1,0:T(8,128)(2,1)S(1)}, u32[]{:S(2)}, u32[]{:S(2)}) collective-permute-start(bf16[512,768]{1,0:T(8,128)(2,1)} %expert_open.2.mine_ref), channel_id=1, source_target_pairs={{0,1},{1,0},{2,3},{3,2},{4,5},{5,4},{6,7},{7,6},{8,9},{9,8},{10,11... | collective-permute-start | bytes 2359304 | tf_op jit(solution)/shard_map/ppermute | solution.py:431
  252.8 16.9 %copy-start = (bf16[768,2048]{1,0:T(8,128)(2,1)}, bf16[768,2048]{1,0:T(8,128)(2,1)S(1)}, u32[]{:S(2)}) copy-start(bf16[768,2048]{1,0:T(8,128)(2,1)S(1)} %collective-permute-done.1.far_a.far_b) | copy-start | bytes 9437188
  269.7 0.9 copy-start.2
  278.0 58.4 %all-to-all-start.2 = ((bf16[128,8,1024]{2,1,0:T(8,128)(2,1)}), bf16[128,8,1024]{2,1,0:T(8,128)(2,1)S(1)}, u32[]{:S(2)}, u32[]{:S(2)}) async-start(bf16[128,8,1024]{2,1,0:T(8,128)(2,1)} %bitcast.57), calls=%async_computation.2 | async-start | bytes 4194304 | tf_op jit(solution)/shard_map/all_to_all | solution.py:363
  299.8 28.2 %collective-permute-start.2 = (bf16[512,768]{1,0:T(8,128)(2,1)}, bf16[512,768]{1,0:T(8,128)(2,1)S(1)}, u32[]{:S(2)}, u32[]{:S(2)}) collective-permute-start(bf16[512,768]{1,0:T(8,128)(2,1)} %expert_open.3.mine_ref), channel_id=1, source_target_pairs={{0,1},{1,0},{2,3},{3,2},{4,5},{5,4},{6,7},{7,6},{8,9},{9,8},{10,11... | collective-permute-start | bytes 2359304 | tf_op jit(solution)/shard_map/ppermute | solution.py:431
  328.0 0.9 copy-start.3
  336.3 46.2 %copy-start.1 = (bf16[128,8,1024]{2,1,0:T(8,128)(2,1)}, bf16[128,8,1024]{2,1,0:T(8,128)(2,1)S(1)}, u32[]{:S(2)}) copy-start(bf16[128,8,1024]{2,1,0:T(8,128)(2,1)S(1)} %all-to-all-done.2) | copy-start | bytes 6291460
  336.3 48.4 %all-to-all-start.4 = ((bf16[128,8,1024]{2,1,0:T(8,128)(2,1)}), bf16[128,8,1024]{2,1,0:T(8,128)(2,1)}, u32[]{:S(2)}, u32[]{:S(2)}) async-start(bf16[128,8,1024]{2,1,0:T(8,128)(2,1)} %bitcast.56), calls=%async_computation.4 | async-start | bytes 4194304 | tf_op jit(solution)/shard_map/all_to_all | solution.py:363
  348.1 22.1 %collective-permute-start.3 = (bf16[128,512]{1,0:T(8,128)(2,1)S(1)}, bf16[128,512]{1,0:T(8,128)(2,1)S(1)}, u32[]{:S(2)}, u32[]{:S(2)}) collective-permute-start(bf16[128,512]{1,0:T(8,128)(2,1)S(1)} %get-tuple-element.25), channel_id=1, source_target_pairs={{0,16},{16,32},{32,48},{48,64},{64,80},{80,96},{96,112},{112,0},{1... | collective-permute-start | bytes 393224 | tf_op jit(solution)/shard_map/ppermute | solution.py:372
  349.7 27.0 %collective-permute-start.4 = (bf16[128,512]{1,0:T(8,128)(2,1)S(1)}, bf16[128,512]{1,0:T(8,128)(2,1)S(1)}, u32[]{:S(2)}, u32[]{:S(2)}) collective-permute-start(bf16[128,512]{1,0:T(8,128)(2,1)S(1)} %get-tuple-element.24), channel_id=1, source_target_pairs={{0,32},{16,48},{32,64},{48,80},{64,96},{80,112},{96,0},{112,16},{1... | collective-permute-start | bytes 393224 | tf_op jit(solution)/shard_map/ppermute | solution.py:372
  351.0 26.6 %collective-permute-start.5 = (bf16[128,512]{1,0:T(8,128)(2,1)S(1)}, bf16[128,512]{1,0:T(8,128)(2,1)S(1)}, u32[]{:S(2)}, u32[]{:S(2)}) collective-permute-start(bf16[128,512]{1,0:T(8,128)(2,1)S(1)} %get-tuple-element.23), channel_id=1, source_target_pairs={{0,48},{16,64},{32,80},{48,96},{64,112},{80,0},{96,16},{112,32},{1... | collective-permute-start | bytes 393224 | tf_op jit(solution)/shard_map/ppermute | solution.py:372
  352.6 29.9 %collective-permute-start.6 = (bf16[128,512]{1,0:T(8,128)(2,1)S(1)}, bf16[128,512]{1,0:T(8,128)(2,1)S(1)}, u32[]{:S(2)}, u32[]{:S(2)}) collective-permute-start(bf16[128,512]{1,0:T(8,128)(2,1)S(1)} %get-tuple-element.22), channel_id=1, source_target_pairs={{0,64},{16,80},{32,96},{48,112},{64,0},{80,16},{96,32},{112,48},{1... | collective-permute-start | bytes 393224 | tf_op jit(solution)/shard_map/ppermute | solution.py:372
  353.2 29.8 %collective-permute-start.7 = (bf16[128,512]{1,0:T(8,128)(2,1)S(1)}, bf16[128,512]{1,0:T(8,128)(2,1)S(1)}, u32[]{:S(2)}, u32[]{:S(2)}) collective-permute-start(bf16[128,512]{1,0:T(8,128)(2,1)S(1)} %get-tuple-element.21), channel_id=1, source_target_pairs={{0,80},{16,96},{32,112},{48,0},{64,16},{80,32},{96,48},{112,64},{1... | collective-permute-start | bytes 393224 | tf_op jit(solution)/shard_map/ppermute | solution.py:372
  370.1 12.9 %collective-permute-start.8 = (bf16[128,512]{1,0:T(8,128)(2,1)S(1)}, bf16[128,512]{1,0:T(8,128)(2,1)S(1)}, u32[]{:S(2)}, u32[]{:S(2)}) collective-permute-start(bf16[128,512]{1,0:T(8,128)(2,1)S(1)} %get-tuple-element.20), channel_id=1, source_target_pairs={{0,96},{16,112},{32,0},{48,16},{64,32},{80,48},{96,64},{112,80},{1... | collective-permute-start | bytes 393224 | tf_op jit(solution)/shard_map/ppermute | solution.py:372
  376.8 6.3 %collective-permute-start.9 = (bf16[128,512]{1,0:T(8,128)(2,1)S(1)}, bf16[128,512]{1,0:T(8,128)(2,1)S(1)}, u32[]{:S(2)}, u32[]{:S(2)}) collective-permute-start(bf16[128,512]{1,0:T(8,128)(2,1)S(1)} %get-tuple-element.19), channel_id=1, source_target_pairs={{0,112},{16,0},{32,16},{48,32},{64,48},{80,64},{96,80},{112,96},{1... | collective-permute-start | bytes 393224 | tf_op jit(solution)/shard_map/ppermute | solution.py:372

commit v4 on v3

v4 whole, which is shorter than its diff:
```python
import math

import jax
import jax.numpy as jnp
from jax import lax
from jax.experimental import pallas as pl
from jax.experimental.pallas import tpu as pltpu
from jax.sharding import PartitionSpec as P

HEAD_DIM = 128
TOP = 8
SLOTS = 8
bf16 = jnp.bfloat16
f32 = jnp.float32


def params(mib):
    return pltpu.CompilerParams(vmem_limit_bytes=mib * 1024 * 1024)


def iota(shape, dim):
    return lax.broadcasted_iota(jnp.int32, shape, dim)


def ones(where):
    return jnp.where(where, jnp.float32(1.0), jnp.float32(0.0)).astype(bf16)


def dot(a, b, dims=((1,), (0,))):
    return lax.dot_general(a, b, (dims, ((), ())), preferred_element_type=f32)


def split_kernel(side_ref, down_ref, *far_refs):
    del side_ref
    step = pl.program_id(0)
    for i, far_ref in enumerate(far_refs):

        @pl.when(step == i)
        def _(far_ref=far_ref):
            far_ref[...] = down_ref[...]


def split(side, down, parts):
    half, width = down.shape
    span = width // 2 // parts
    return pl.pallas_call(
        split_kernel,
        grid_spec=pltpu.PrefetchScalarGridSpec(
            num_scalar_prefetch=1,
            grid=(parts,),
            in_specs=[pl.BlockSpec((half, span), lambda c, side: (0, (1 - side[0]) * parts + c))],
            out_specs=[pl.BlockSpec((half, span), lambda c, side: (0, 0))] * parts,
        ),
        out_shape=[jax.ShapeDtypeStruct((half, span), bf16)] * parts,
        compiler_params=params(60),
        name="split",
    )(side, down)


def prepare_kernel(
    q_ref,
    k_ref,
    v_ref,
    res_ref,
    flag_ref,
    ids_ref,
    gates_ref,
    out_ref,
    own_ref,
    pick_ref,
    table_ref,
):
    rows = q_ref.shape[0]
    merge, _, cols = out_ref.shape
    experts, most = table_ref.shape
    extra = 3 * rows + most

    @pl.when(pl.program_id(0) == 0)
    def _():
        upper = ones(iota((rows, rows), 0) < iota((rows, rows), 1))
        masked = flag_ref[...] == 1
        rank = dot(ones(jnp.broadcast_to(flag_ref[...], (16, rows)) == 1), upper)[:1]
        pick = ones((iota((most, rows), 0).astype(f32) == rank) & masked)
        pick_ref[...] = pick
        named = jnp.zeros((experts, rows), f32)
        gates = jnp.zeros((experts, rows), f32)
        for k in range(TOP):
            hit = (ids_ref[k : k + 1, :] == iota((experts, rows), 0)) & masked
            named = jnp.where(hit, 1.0, named)
            gates = jnp.where(hit, gates_ref[k : k + 1, :], gates)
        place = (named * (dot(named.astype(bf16), upper) + 1.0)).astype(bf16)
        high = gates.astype(bf16)
        own_ref[0] = place
        own_ref[1] = high
        own_ref[2] = (gates - high.astype(f32)).astype(bf16)
        table_ref[...] = dot(place, pick, ((1,), (1,))).astype(bf16)

    numbers = iota((16, rows), 1).astype(f32).astype(bf16)
    spot = dot(numbers, pick_ref[...], ((1,), (1,)))
    count = dot(jnp.ones((16, rows), bf16), pick_ref[...], ((1,), (1,)))
    spot = jnp.where(count > 0.5, spot, -1.0).astype(bf16)
    for m in range(merge):
        here = slice(m * cols, (m + 1) * cols)
        out_ref[m, :rows] = q_ref[:, here]
        out_ref[m, rows : 2 * rows] = k_ref[:, here]
        out_ref[m, 2 * rows : 3 * rows] = v_ref[:, here]
        out_ref[m, 3 * rows : extra] = dot(pick_ref[...], res_ref[:, here]).astype(bf16)
        out_ref[m, extra:] = jnp.zeros((16, cols), bf16)
        for h in range(experts // 16):
            out_ref[m, extra:, h * 128 : h * 128 + most] = table_ref[h * 16 : (h + 1) * 16]
            out_ref[m, extra:, h * 128 + 64 : h * 128 + 64 + most] = spot


def prepare(q, k, v, res, flags, ids, gates, groups, experts, most):
    rows, width = q.shape
    cols = width // groups
    total = 3 * rows + most + 16
    merge = 2
    piece = pl.BlockSpec((rows, merge * cols), lambda j: (0, j))
    return pl.pallas_call(
        prepare_kernel,
        grid=(groups // merge,),
        in_specs=[
            piece,
            piece,
            piece,
            piece,
            pl.BlockSpec((1, rows), lambda j: (0, 0)),
            pl.BlockSpec((TOP, rows), lambda j: (0, 0)),
            pl.BlockSpec((TOP, rows), lambda j: (0, 0)),
        ],
        out_specs=[
            pl.BlockSpec((merge, total, cols), lambda j: (j, 0, 0)),
            pl.BlockSpec((3, experts, rows), lambda j: (0, 0, 0)),
        ],
        out_shape=[
            jax.ShapeDtypeStruct((groups, total, cols), bf16),
            jax.ShapeDtypeStruct((3, experts, rows), bf16),
        ],
        scratch_shapes=[pltpu.VMEM((most, rows), bf16), pltpu.VMEM((experts, most), bf16)],
        compiler_params=params(60),
        name="prepare",
    )(q, k, v, res, flags, ids, gates)


def attend_kernel(in_ref, table_ref, gain_ref, attn_ref, out_ref, place_ref, spot_ref, v_ref):
    cores, chips, rows, cols = attn_ref.shape
    blocks = cores * chips
    experts = out_ref.shape[0]
    most = spot_ref.shape[2]
    length = blocks * rows
    heads = cols // HEAD_DIM

    @pl.when(pl.program_id(0) == 0)
    def _():
        wanted = iota((16, SLOTS, most), 1).astype(f32) + 1.0
        for b in range(blocks):
            for h in range(experts // 16):
                table = table_ref[b, :, h * 128 : h * 128 + most].astype(f32)
                hit = jnp.where(table[:, None, :] == wanted, 1.0, 0.0)
                place_ref[b, h * 128 : (h + 1) * 128] = hit.reshape(128, most).astype(bf16)
            spot = table_ref[b, :, 64 : 64 + most].astype(f32)[:1]
            spot_ref[b] = ones(iota((rows, most), 0).astype(f32) == spot)
        v_ref[:, HEAD_DIM:] = jnp.ones((length, HEAD_DIM), bf16)

    scale = math.log2(math.e) / math.sqrt(HEAD_DIM)
    gain = gain_ref[...].astype(f32)
    step = 2
    for h in range(heads):
        here = slice(h * HEAD_DIM, (h + 1) * HEAD_DIM)
        k_all = in_ref[:, rows : 2 * rows, here].reshape(length, HEAD_DIM)
        v_ref[:, :HEAD_DIM] = in_ref[:, 2 * rows : 3 * rows, here].reshape(length, HEAD_DIM)
        for first in range(0, blocks, step):
            q_part = in_ref[first : first + step, :rows, here].reshape(step * rows, HEAD_DIM)
            scores = dot(q_part, k_all, ((1,), (1,)))
            peak = jnp.max(scores, axis=-1, keepdims=True)
            expo = jnp.exp2((scores - peak) * scale).astype(bf16)
            mixed = dot(expo, v_ref[...])
            attn = (mixed[:, :HEAD_DIM] / mixed[:, HEAD_DIM:]).astype(bf16)
            attn_ref[:, first // 2, :, here] = attn.reshape(step, rows, HEAD_DIM)
    for b in range(blocks):
        hidden = dot(spot_ref[b], attn_ref[b % 2, b // 2], ((0,), (0,)))
        hidden += in_ref[b, 3 * rows : 3 * rows + most].astype(f32)
        sent = dot(place_ref[b], (hidden * gain).astype(bf16))
        sent = sent.reshape(experts, SLOTS, cols).astype(bf16)
        out_ref[:, 0, b] = sent
        out_ref[:, 1, b] = sent


def attend(pieces, gain, rows, experts, heads=2):
    blocks, total, cols = pieces.shape
    most = total - 3 * rows - 16
    span = heads * HEAD_DIM
    return pl.pallas_call(
        attend_kernel,
        grid=(cols // span,),
        in_specs=[
            pl.BlockSpec((blocks, total, span), lambda h: (0, 0, h)),
            pl.BlockSpec((blocks, 16, cols), lambda h: (0, total // 16 - 1, 0)),
            pl.BlockSpec((1, span), lambda h: (0, h)),
        ],
        out_specs=[
            pl.BlockSpec((2, blocks // 2, rows, span), lambda h: (0, 0, 0, h)),
            pl.BlockSpec((experts, 2, blocks, SLOTS, span), lambda h: (0, 0, 0, 0, h)),
        ],
        out_shape=[
            jax.ShapeDtypeStruct((2, blocks // 2, rows, cols), bf16),
            jax.ShapeDtypeStruct((experts, 2, blocks, SLOTS, cols), bf16),
        ],
        scratch_shapes=[
            pltpu.VMEM((blocks, experts * SLOTS, most), bf16),
            pltpu.VMEM((blocks, rows, most), bf16),
            pltpu.VMEM((blocks * rows, 2 * HEAD_DIM), bf16),
        ],
        compiler_params=params(60),
        name="attend",
    )(pieces, pieces, gain)


def open_kernel(rows_ref, gain_ref, gate_ref, up_ref, *rest):
    *out_refs, gates_ref, ups_ref, square_ref = rest
    step = pl.program_id(0)
    merge, count, per, cols = rows_ref.shape
    total = count * per
    half = gate_ref.shape[1]
    back = 1.0 / gain_ref[...].astype(f32)
    square = jnp.zeros((total, 128), f32)
    gate_part = jnp.zeros((total, half), f32)
    up_part = jnp.zeros((total, half), f32)
    for m in range(merge):
        here = slice(m * cols, (m + 1) * cols)
        x = rows_ref[m].reshape(total, cols)
        gate_part += dot(x, gate_ref[here])
        up_part += dot(x, up_ref[here])
        hidden = x.astype(f32) * back[:, here]
        for c in range(0, cols, 128):
            square += hidden[:, c : c + 128] * hidden[:, c : c + 128]

    @pl.when(step == 0)
    def _():
        square_ref[...] = square
        gates_ref[...] = gate_part
        ups_ref[...] = up_part

    @pl.when(step > 0)
    def _():
        square_ref[...] += square
        gates_ref[...] += gate_part
        ups_ref[...] += up_part

    @pl.when(step == pl.num_programs(0) - 1)
    def _():
        width = pl.num_programs(0) * merge * cols
        mean = jnp.sum(square_ref[...], axis=-1, keepdims=True) / width
        scale = lax.rsqrt(mean + 1e-06)
        gate_full = gates_ref[...] * scale
        act = gate_full / (1.0 + jnp.exp(-gate_full)) * (ups_ref[...] * scale)
        act = act.astype(bf16).reshape(count, per, half)
        piece = per // len(out_refs)
        for i, out_ref in enumerate(out_refs):
            out_ref[...] = act[:, i * piece : (i + 1) * piece].reshape(count * piece, half)


def expert_open(arrived, part, pieces, gain, gate, up):
    groups, count, _, cols = arrived.shape
    per = 2 * SLOTS * pieces
    width, half = gate.shape
    total = count * per
    merge = 2
    weight = pl.BlockSpec((merge * cols, half), lambda n: (n, 0))
    return pl.pallas_call(
        open_kernel,
        grid=(groups // merge,),
        in_specs=[
            pl.BlockSpec((merge, count, per, cols), lambda n: (n, 0, part, 0)),
            pl.BlockSpec((1, merge * cols), lambda n: (0, n)),
            weight,
            weight,
        ],
        out_specs=[pl.BlockSpec((total // pieces, half), lambda n: (0, 0))] * pieces,
        out_shape=[jax.ShapeDtypeStruct((total // pieces, half), bf16)] * pieces,
        scratch_shapes=[
            pltpu.VMEM((total, half), f32),
            pltpu.VMEM((total, half), f32),
            pltpu.VMEM((total, 128), f32),
        ],
        compiler_params=params(20),
        cost_estimate=pl.CostEstimate(
            flops=4 * total * width * half,
            bytes_accessed=4 * width * half + 2 * total * (width + half),
            transcendentals=total * half,
        ),
        name="expert_open",
    )(arrived, gain, gate, up)


def close_kernel(side_ref, mine_ref, other_ref, own_ref, *rest):
    del side_ref
    out_ref = rest[-1]
    step = pl.program_id(0)
    merge, count, _, span = out_ref.shape
    parts = 2
    for i in range(parts):

        @pl.when(step // 2 == i)
        def _(far_ref=rest[i]):
            result = dot(mine_ref[...], own_ref[...]) + dot(other_ref[...], far_ref[...])
            result = result.reshape(count, merge, SLOTS, span).astype(bf16)
            for m in range(merge):
                out_ref[m] = result[:, m]


def expert_close(side, mine, other, down, far, part, groups, count, done):
    total, half = mine.shape
    width = down.shape[1] // 2
    steps = 2 * len(far)
    span = width // steps
    merge = total // (count * SLOTS)
    act = pl.BlockSpec((total, half), lambda c, side: (0, 0))
    held = [] if done is None else [done]
    return pl.pallas_call(
        close_kernel,
        grid_spec=pltpu.PrefetchScalarGridSpec(
            num_scalar_prefetch=1,
            grid=(steps,),
            in_specs=[
                act,
                act,
                pl.BlockSpec((half, span), lambda c, side: (0, side[0] * steps + c)),
            ]
            + [
                pl.BlockSpec((half, span), lambda c, side, i=i: (0, jnp.clip(c - 2 * i, 0, 1)))
                for i in range(len(far))
            ]
            + [pl.BlockSpec(memory_space=pl.ANY)] * len(held),
            out_specs=pl.BlockSpec((merge, count, SLOTS, span), lambda c, side: (part, 0, 0, c)),
        ),
        out_shape=jax.ShapeDtypeStruct((groups, count, SLOTS, width), bf16),
        input_output_aliases={4 + len(far): 0} if held else {},
        compiler_params=params(20),
        cost_estimate=pl.CostEstimate(
            flops=4 * total * width * half,
            bytes_accessed=2 * (2 * width * half + total * (2 * half + width)),
            transcendentals=0,
        ),
        name="expert_close",
    )(side, mine, other, down, *far, *held)


def combine_kernel(chip_ref, back_ref, own_ref, res_ref, cached_ref, *rest):
    del chip_ref
    *attn_refs, out_ref, mix_ref = rest
    step = pl.program_id(0)
    _, experts, rows = own_ref.shape
    slots = experts * SLOTS
    cols = out_ref.shape[1]

    @pl.when(step == 0)
    def _():
        spread = ones(iota((experts, slots), 0) == iota((experts, slots), 1) // SLOTS)
        slot = (iota((rows, slots), 1) % SLOTS + 1).astype(f32)
        hit = dot(own_ref[0], spread, ((0,), (0,))) == slot
        for i in range(2):
            gates = dot(own_ref[1 + i], spread, ((0,), (0,)))
            mix_ref[i * rows : (i + 1) * rows] = jnp.where(hit, gates, 0.0).astype(bf16)

    both = dot(mix_ref[...], back_ref[:, 0].reshape(slots, cols))
    mixed = both[:rows] + both[rows:]
    named = dot(own_ref[0], jnp.ones((experts, 128), bf16), ((0,), (0,)))
    moe = jnp.where(named[:, :1] > 0.5, mixed, cached_ref[...].astype(f32))
    for i, attn_ref in enumerate(attn_refs):

        @pl.when(step == i)
        def _(attn_ref=attn_ref):
            merge, _, piece = attn_ref.shape
            for m in range(merge):
                here = slice(m * piece, (m + 1) * piece)
                hid = res_ref[:, here].astype(f32) + attn_ref[m].astype(f32)
                out_ref[:, here] = (hid + moe[:, here]).astype(bf16)


def combine(chip, back, own, attn, residual, cached):
    experts, sides, _, half = back.shape
    merge, rows, piece = attn[0].shape
    chips = len(attn)
    span = merge * piece
    steps = half // span

    def place(i, chip):
        return lax.rem(chip[0] + chips - i, chips)

    flat = pl.BlockSpec((rows, span), lambda i, chip: (0, place(i, chip)))
    back_spec = pl.BlockSpec(
        (experts, 1, SLOTS, span),
        lambda i, chip: (0, lax.div(place(i, chip), steps), 0, lax.rem(place(i, chip), steps)),
    )
    return pl.pallas_call(
        combine_kernel,
        grid_spec=pltpu.PrefetchScalarGridSpec(
            num_scalar_prefetch=1,
            grid=(chips,),
            in_specs=[back_spec, pl.BlockSpec(own.shape, lambda i, chip: (0, 0, 0)), flat, flat]
            + [pl.BlockSpec((merge, rows, piece), lambda i, chip: (0, 0, 0))] * chips,
            out_specs=flat,
            scratch_shapes=[pltpu.VMEM((2 * rows, experts * SLOTS), bf16)],
        ),
        out_shape=jax.ShapeDtypeStruct((rows, chips * span), bf16),
        compiler_params=params(60),
        name="combine",
    )(chip, back, own, residual, cached, *attn)


def home(attn):
    chips = attn.shape[1]
    count = 2 * chips
    here = lax.axis_index("seq")
    core = here % 2
    keep = lax.dynamic_index_in_dim(attn, core, 0, keepdims=False)
    give = lax.dynamic_index_in_dim(attn, 1 - core, 0, keepdims=False)
    took = lax.ppermute(give, "seq", [(i, i ^ 1) for i in range(count)])
    lower = jnp.where(core == 0, keep, took)
    upper = jnp.where(core == 0, took, keep)
    both = jnp.stack([lower, upper], axis=1)
    chip = here // 2
    parts = []
    for d in range(chips):
        part = lax.dynamic_index_in_dim(both, (chip + d) % chips, 0, keepdims=False)
        if d:
            hops = [(i, (i + 2 * d) % count) for i in range(count)]
            part = lax.ppermute(part, "seq", hops)
        parts.append(part)
    return parts


def exchange(blocks, axes):
    return lax.all_to_all(blocks, axes, split_axis=0, concat_axis=0, tiled=True)


def per_device(
    queries,
    keys,
    values,
    residual_in,
    cached_moe,
    norm_gain,
    still_masked,
    expert_ids,
    gate_weights,
    w_gate,
    w_up,
    w_down,
):
    rows, width = queries.shape[1:]
    seq_count = lax.axis_size("seq")
    exp_count = lax.axis_size("exp")
    devices = seq_count * exp_count
    experts = devices // 2
    cols = width // seq_count
    most = rows * 3 // 8
    all_axes = ("seq", "exp")
    partner = [(p, p ^ 1) for p in range(exp_count)]
    side = (lax.axis_index("exp") % 2)[None].astype(jnp.int32)
    gain = norm_gain[None, :]
    own_gain = lax.dynamic_slice_in_dim(gain, lax.axis_index("seq") * cols, cols, 1)

    far = split(side, w_down[0], 2)
    *far, queries = lax.optimization_barrier((*far, queries))
    far = [lax.ppermute(part, "exp", partner) for part in far]
    pieces, own = prepare(
        queries[0],
        keys[0],
        values[0],
        residual_in[0],
        still_masked,
        expert_ids[0].T,
        gate_weights[0].T,
        seq_count,
        experts,
        most,
    )
    pieces = exchange(pieces, "seq")
    tied = lax.optimization_barrier((pieces, gain, own_gain, far[0]))
    pieces, gain, own_gain, far[0] = tied

    attn, sent = attend(pieces, own_gain, rows, experts)
    sent, far[1] = lax.optimization_barrier((sent, far[1]))
    arrived = exchange(sent.reshape(devices, seq_count * SLOTS, cols), all_axes)
    arrived = arrived.reshape(seq_count, exp_count, seq_count * SLOTS, cols)

    def opened(part):
        return expert_open(arrived, part, 1, gain, w_gate[0], w_up[0])[0]

    def closed(part, mine, done):
        other = lax.ppermute(mine, "exp", partner)
        return expert_close(side, mine, other, w_down[0], far, part, seq_count, exp_count, done)

    parts = seq_count // 2
    mine = opened(0)
    arrived, mine = lax.optimization_barrier((arrived, mine))
    done = None
    for part in range(parts):
        following = opened(part + 1) if part + 1 < parts else None
        done = closed(part, mine, done)
        arrived, done = lax.optimization_barrier((arrived, done))
        mine = following
    attn, done = lax.optimization_barrier((attn, done))
    attn = home(attn)
    back = exchange(done.reshape(devices, SLOTS, width // 2), all_axes)
    back = back.reshape(experts, 2, SLOTS, width // 2)
    chip = (lax.axis_index("seq") // 2)[None].astype(jnp.int32)
    out = combine(chip, back, own, attn, residual_in[0], cached_moe[0])
    return out[None]


def solution(mesh):
    return jax.shard_map(
        per_device,
        mesh=mesh,
        in_specs=(
            P("exp", "seq", None),
            P("exp", "seq", None),
            P("exp", "seq", None),
            P("exp", "seq", None),
            P("exp", "seq", None),
            P(),
            P("exp", "seq"),
            P("exp", "seq", None),
            P("exp", "seq", None),
            P(("seq", "exp"), None, None),
            P(("seq", "exp"), None, None),
            P(("seq", "exp"), None, None),
        ),
        out_specs=P("exp", "seq", None),
        check_vma=False,
    )
```

time: 393 us -> 323 us (0.82)
  waiting for transfers between devices: 206 us -> 117 us
  blocking collectives: 60.2 us -> 108 us
  starting transfers between devices: 45.8 us -> 26.9 us
  local copies, waits for them, and re-layouts: 12.8 us -> 3.41 us
    ppermute x10, waiting for transfers between devices: 163 us -> 109 us  [the longest x3 51.4 us: home(): part = lax.ppermute(part, 'seq', hops)]
    all_to_all x1, blocking collectives: 60.2 us -> 108 us  [exchange(): return lax.all_to_all(blocks, axes, split_axis=0, concat_axis=0, tiled=True)]
    all_to_all x4 -> x2, waiting for transfers between devices: 42.7 us -> 7.42 us  [exchange(): return lax.all_to_all(blocks, axes, split_axis=0, concat_axis=0, tiled=True)]
    all_to_all x4 -> x2, starting transfers between devices: 31.9 us -> 17.2 us  [exchange(): return lax.all_to_all(blocks, axes, split_axis=0, concat_axis=0, tiled=True)]
    pallas_call x4 -> x7, Pallas kernels: 40.4 us -> 35.6 us  [the longest x4 20.5 us: expert_open(): pl.pallas_call(open_kernel, grid=(groups // merge,), in_specs=[pl.BlockSp...]
    ppermute x10, starting transfers between devices: 13.9 us -> 9.71 us  [the longest x3 3.59 us: home(): part = lax.ppermute(part, 'seq', hops)]
    dynamic_slice x1 -> x0, local copies, waits for them, and re-layouts: 3.95 us -> none  [per_device(): lax.dynamic_slice_in_dim(w_down[0], (1 - side) * (width // 2), width // 2...]
    pallas_call x2 -> x4, Pallas kernels: 14.8 us -> 17.6 us  [expert_close(): pl.pallas_call(close_kernel, grid_spec=pltpu.PrefetchScalarGridSpec(num_s...]
  transfers between devices with their start and end apart: 14 -> 12, of which waited for: 9 -> 9; matrix products, arithmetic and copies ran while one was open for 2% -> 0% of each run, Pallas kernels for 10% -> 11%
where the time goes in v4:
time: 323 us; the launch traced here: 322 us
  waiting for transfers between devices  117 us (36%)
  blocking collectives  108 us (33%)
  Pallas kernels  65.4 us (20%)
  starting transfers between devices  26.9 us (8%)
  local copies, waits for them, and re-layouts  3.41 us (1%)
    all_to_all x1, blocking collectives, exchange(): return lax.all_to_all(blocks, axes, split_axis=0, concat_axis=0, tiled=True)  108 us
    ppermute x3, waiting for transfers between devices, home(): part = lax.ppermute(part, 'seq', hops)  51.4 us
    ppermute x2, waiting for transfers between devices, per_device(): far = [lax.ppermute(part, 'exp', partner) for part in far]  47.9 us
    pallas_call x4, Pallas kernels, expert_open(): pl.pallas_call(open_kernel, grid=(groups // merge,), in_specs=[pl.BlockSp...  20.5 us
    pallas_call x4, Pallas kernels, expert_close(): pl.pallas_call(close_kernel, grid_spec=pltpu.PrefetchScalarGridSpec(num_s...  17.6 us
    all_to_all x2, starting transfers between devices, exchange(): return lax.all_to_all(blocks, axes, split_axis=0, concat_axis=0, tiled=True)  17.2 us
    pallas_call x1, Pallas kernels, attend(): pl.pallas_call(attend_kernel, grid=(cols // span,), in_specs=[pl.BlockSpe...  12.2 us
    ppermute x4, waiting for transfers between devices, closed(): other = lax.ppermute(mine, 'exp', partner)  8.36 us
  transfers between devices with their start and end apart: 12, of which 9 were waited for; matrix products, arithmetic and copies ran while one was open for 0% of the time, Pallas kernels for 11%

profile of v4, /device:TPU:1, one launch (start us, length us, event | category | flops | bytes accessed | tf_op | source)
XLA Modules:
  0.0 321.8 jit_solution(9240500670639557381)
XLA Ops:
  0.0 3.7 %split.1 = (bf16[768,1024]{1,0:T(8,128)(2,1)}, bf16[768,1024]{1,0:T(8,128)(2,1)}) custom-call(s32[1]{0:T(128)} %bitcast.1.side_ref, bf16[768,4096]{1,0:T(8,128)(2,1)} %bitcast.48), custom_call_target="tpu_custom_call" | custom-call | tf_op jit(solution)/shard_map/split/pallas_call | solution.py:46
  3.7 5.1 %prepare.1 = (bf16[8,448,512]{2,1,0:T(8,128)(2,1)}, bf16[3,64,128]{2,1,0:T(8,128)(2,1)}) custom-call(bf16[128,4096]{1,0:T(8,128)(2,1)} %bitcast.71, bf16[128,4096]{1,0:T(8,128)(2,1)} %bitcast.72, bf16[128,4096]{1,0:T(8,128)(2,1)} %bitcast.73, bf16[128,4096]{1,0:T(8,128)(2,1)} %bitcast.69, s32[1,128]{1,0:T(1,128)} %flag_ref.1, s32[8,128]{1,0:T(8,128)} %bitcast.75, ...), custom_call_target="tpu_custom_call" | custom-call | tf_op jit(solution)/shard_map/prepare/pallas_call | solution.py:120
  8.7 6.0 %all-to-all-start = ((bf16[8,448,512]{2,1,0:T(8,128)(2,1)}), bf16[8,448,512]{2,1,0:T(8,128)(2,1)}, u32[]{:S(2)}, u32[]{:S(2)}) async-start(bf16[8,448,512]{2,1,0:T(8,128)(2,1)} %get-tuple-element.32), calls=%async_computation | async-start | bytes 7340032 | tf_op jit(solution)/shard_map/all_to_all | solution.py:436
  14.7 0.0 copy-done.6
  14.7 1.4 collective-permute-start
  16.1 0.1 collective-permute-start.1
  16.2 0.1 dynamic-slice.3
  16.3 0.5 dynamic_slice.23.gain_ref
  16.8 33.8 %collective-permute-done.rest_0_ = bf16[768,1024]{1,0:T(8,128)(2,1)S(1)} collective-permute-done((bf16[768,1024]{1,0:T(8,128)(2,1)S(1)}, bf16[768,1024]{1,0:T(8,128)(2,1)S(1)}, u32[]{:S(2)}, u32[]{:S(2)}) %collective-permute-start) | collective-permute-done | bytes 1572896 | tf_op jit(solution)/shard_map/ppermute | solution.py:468
  50.6 7.4 %all-to-all-done.in_ref.table_ref = bf16[8,448,512]{2,1,0:T(8,128)(2,1)} async-done(((bf16[8,448,512]{2,1,0:T(8,128)(2,1)}), bf16[8,448,512]{2,1,0:T(8,128)(2,1)}, u32[]{:S(2)}, u32[]{:S(2)}) %all-to-all-start) | async-done | bytes 3670048 | tf_op jit(solution)/shard_map/all_to_all | solution.py:436
  58.0 12.2 %attend.1 = (bf16[2,4,128,512]{3,2,1,0:T(8,128)(2,1)}, bf16[64,2,8,8,512]{4,3,2,1,0:T(8,128)(2,1)}) custom-call(bf16[8,448,512]{2,1,0:T(8,128)(2,1)} %all-to-all-done.in_ref.table_ref, bf16[8,448,512]{2,1,0:T(8,128)(2,1)} %all-to-all-done.in_ref.table_ref, bf16[1,512]{1,0:T(2,128)(2,1)} %dynamic_slice.23.gain_ref), custom_call_target="tpu_custom_call" | custom-call | tf_op jit(solution)/shard_map/attend/pallas_call | solution.py:194
  70.2 14.1 %collective-permute-done.1.rest_1_ = bf16[768,1024]{1,0:T(8,128)(2,1)} collective-permute-done((bf16[768,1024]{1,0:T(8,128)(2,1)}, bf16[768,1024]{1,0:T(8,128)(2,1)}, u32[]{:S(2)}, u32[]{:S(2)}) %collective-permute-start.1) | collective-permute-done | bytes 1572896 | tf_op jit(solution)/shard_map/ppermute | solution.py:468
  84.3 108.4 %all_to_all.15 = bf16[128,64,512]{2,1,0:T(8,128)(2,1)S(1)} all-to-all(bf16[128,64,512]{2,1,0:T(8,128)(2,1)} %bitcast.68), channel_id=1, replica_groups=mesh['seq'=8,'exp'=16] {'seq','exp'}, dimensions={0} | all-to-all | bytes 16777216 | tf_op jit(solution)/shard_map/all_to_all | solution.py:436
  192.7 0.0 slice-done.2
  192.8 0.0 slice-start
  192.8 5.1 %expert_open.4.mine_ref = bf16[256,768]{1,0:T(8,128)(2,1)S(1)} custom-call(bf16[8,16,64,512]{3,2,1,0:T(8,128)(2,1)S(1)} %bitcast.44, bf16[1,4096]{1,0:T(2,128)(2,1)S(1)} %broadcast_in_dim.14.gain_ref, bf16[4096,768]{1,0:T(8,128)(2,1)S(1)} %bitcast.58, bf16[4096,768]{1,0:T(8,128)(2,1)S(1)} %bitcast.64), custom_call_target="tpu_custom_call" | custom-call | flops 3221225472 | bytes 15073280 | tf_op jit(solution)/shard_map/expert_open/pallas_call | solution.py:271
  197.9 0.0 slice-start.1
  197.9 0.2 collective-permute-start.2
  198.2 5.1 %expert_open.5.mine_ref = bf16[256,768]{1,0:T(8,128)(2,1)S(1)} custom-call(bf16[8,16,64,512]{3,2,1,0:T(8,128)(2,1)S(1)} %bitcast.45, bf16[1,4096]{1,0:T(2,128)(2,1)S(1)} %broadcast_in_dim.14.gain_ref, bf16[4096,768]{1,0:T(8,128)(2,1)S(1)} %bitcast.59, bf16[4096,768]{1,0:T(8,128)(2,1)S(1)} %bitcast.65), custom_call_target="tpu_custom_call" | custom-call | flops 3221225472 | bytes 15073280 | tf_op jit(solution)/shard_map/expert_open/pallas_call | solution.py:271
  203.3 1.6 collective-permute-start.3
  204.9 2.5 collective-permute-done.2.other_ref
  207.4 0.0 slice-done
  207.4 4.4 %expert_close.4.rest_2_ = bf16[8,16,8,2048]{3,2,1,0:T(8,128)(2,1)S(1)} custom-call(s32[1]{0:T(128)} %bitcast.1.side_ref, bf16[256,768]{1,0:T(8,128)(2,1)S(1)} %expert_open.4.mine_ref, bf16[256,768]{1,0:T(8,128)(2,1)S(1)} %collective-permute-done.2.other_ref, bf16[768,4096]{1,0:T(8,128)(2,1)S(1)} %bitcast.51, ...), custom_call_target="tpu_custom_call" | custom-call | flops 1610612736 | bytes 8126464 | tf_op jit(solution)/shard_map/expert_close/pallas_call | solution.py:321
  211.8 5.1 %expert_open.7.mine_ref = bf16[256,768]{1,0:T(8,128)(2,1)S(1)} custom-call(bf16[8,16,64,512]{3,2,1,0:T(8,128)(2,1)S(1)} %bitcast.46, bf16[1,4096]{1,0:T(2,128)(2,1)S(1)} %broadcast_in_dim.14.gain_ref, bf16[4096,768]{1,0:T(8,128)(2,1)S(1)} %bitcast.60, bf16[4096,768]{1,0:T(8,128)(2,1)S(1)} %bitcast.66), custom_call_target="tpu_custom_call" | custom-call | flops 3221225472 | bytes 15073280 | tf_op jit(solution)/shard_map/expert_open/pallas_call | solution.py:271
  216.9 0.0 collective-permute-done.3.other_ref
  216.9 4.4 %expert_close.5.rest_2_ = bf16[8,16,8,2048]{3,2,1,0:T(8,128)(2,1)S(1)} custom-call(s32[1]{0:T(128)} %bitcast.1.side_ref, bf16[256,768]{1,0:T(8,128)(2,1)S(1)} %expert_open.5.mine_ref, bf16[256,768]{1,0:T(8,128)(2,1)S(1)} %collective-permute-done.3.other_ref, bf16[768,4096]{1,0:T(8,128)(2,1)S(1)} %bitcast.52, ...), custom_call_target="tpu_custom_call", output_to_operand_aliasing={{}: (6, {})} | custom-call | flops 1610612736 | bytes 8126464 | tf_op jit(solution)/shard_map/expert_close/pallas_call | solution.py:321
  221.4 0.6 collective-permute-start.5
  222.0 5.1 %expert_open.6.mine_ref = bf16[256,768]{1,0:T(8,128)(2,1)S(1)} custom-call(bf16[8,16,64,512]{3,2,1,0:T(8,128)(2,1)S(1)} %bitcast.47, bf16[1,4096]{1,0:T(2,128)(2,1)S(1)} %broadcast_in_dim.14.gain_ref, bf16[4096,768]{1,0:T(8,128)(2,1)S(1)} %bitcast.61, bf16[4096,768]{1,0:T(8,128)(2,1)S(1)} %bitcast.67), custom_call_target="tpu_custom_call" | custom-call | flops 3221225472 | bytes 15073280 | tf_op jit(solution)/shard_map/expert_open/pallas_call | solution.py:271
  227.1 1.0 collective-permute-start.4
  228.1 0.0 collective-permute-done.5.other_ref
  228.1 4.4 %expert_close.6.rest_2_ = bf16[8,16,8,2048]{3,2,1,0:T(8,128)(2,1)S(1)} custom-call(s32[1]{0:T(128)} %bitcast.1.side_ref, bf16[256,768]{1,0:T(8,128)(2,1)S(1)} %expert_open.7.mine_ref, bf16[256,768]{1,0:T(8,128)(2,1)S(1)} %collective-permute-done.5.other_ref, bf16[768,4096]{1,0:T(8,128)(2,1)S(1)} %bitcast.53, ...), custom_call_target="tpu_custom_call", output_to_operand_aliasing={{}: (6, {})} | custom-call | flops 1610612736 | bytes 8126464 | tf_op jit(solution)/shard_map/expert_close/pallas_call | solution.py:321
  232.5 5.9 %collective-permute-done.4.other_ref = bf16[256,768]{1,0:T(8,128)(2,1)S(1)} collective-permute-done((bf16[256,768]{1,0:T(8,128)(2,1)S(1)}, bf16[256,768]{1,0:T(8,128)(2,1)S(1)}, u32[]{:S(2)}, u32[]{:S(2)}) %collective-permute-start.4) | collective-permute-done | bytes 393248 | tf_op jit(solution)/shard_map/ppermute | solution.py:494
  238.4 4.4 %expert_close.7 = bf16[8,16,8,2048]{3,2,1,0:T(8,128)(2,1)S(1)} custom-call(s32[1]{0:T(128)} %bitcast.1.side_ref, bf16[256,768]{1,0:T(8,128)(2,1)S(1)} %expert_open.6.mine_ref, bf16[256,768]{1,0:T(8,128)(2,1)S(1)} %collective-permute-done.4.other_ref, bf16[768,4096]{1,0:T(8,128)(2,1)S(1)} %bitcast.54, ...), custom_call_target="tpu_custom_call", output_to_operand_aliasing={{}: (6, {})} | custom-call | flops 1610612736 | bytes 8126464 | tf_op jit(solution)/shard_map/expert_close/pallas_call | solution.py:321
  242.8 2.0 copy-done
  244.8 11.2 %all-to-all-start.2 = ((bf16[128,8,2048]{2,1,0:T(8,128)(2,1)}), bf16[128,8,2048]{2,1,0:T(8,128)(2,1)}, u32[]{:S(2)}, u32[]{:S(2)}) async-start(bf16[128,8,2048]{2,1,0:T(8,128)(2,1)} %bitcast.55), calls=%async_computation.2 | async-start | bytes 8388608 | tf_op jit(solution)/shard_map/all_to_all | solution.py:436
  256.1 1.2 collective-permute-start.6
  257.3 1.5 collective-permute-done.6
  258.9 0.1 fusion.1
  258.9 0.8 fusion.3
  259.8 2.1 collective-permute-start.9
  261.9 0.0 collective-permute-start.7
  261.9 1.5 collective-permute-start.8
  263.4 44.4 %collective-permute-done.9.rest_3_ = bf16[2,128,512]{2,1,0:T(8,128)(2,1)S(1)} collective-permute-done((bf16[2,128,512]{2,1,0:T(8,128)(2,1)S(1)}, bf16[2,128,512]{2,1,0:T(8,128)(2,1)S(1)}, u32[]{:S(2)}, u32[]{:S(2)}) %collective-permute-start.9) | collective-permute-done | bytes 262176 | tf_op jit(solution)/shard_map/ppermute | solution.py:430
  307.7 1.3 collective-permute-done.7.rest_1_
  309.0 5.8 %collective-permute-done.8.rest_2_ = bf16[2,128,512]{2,1,0:T(8,128)(2,1)S(1)} collective-permute-done((bf16[2,128,512]{2,1,0:T(8,128)(2,1)S(1)}, bf16[2,128,512]{2,1,0:T(8,128)(2,1)S(1)}, u32[]{:S(2)}, u32[]{:S(2)}) %collective-permute-start.8) | collective-permute-done | bytes 262176 | tf_op jit(solution)/shard_map/ppermute | solution.py:430
  314.7 0.0 all-to-all-done.2
  314.8 0.7 copy-done.4
  315.4 6.3 %combine.1 = bf16[128,4096]{1,0:T(8,128)(2,1)} custom-call(s32[1]{0:T(128)} %bitcast.chip_ref, bf16[64,2,8,2048]{3,2,1,0:T(8,128)(2,1)} %bitcast.16.back_ref, bf16[3,64,128]{2,1,0:T(8,128)(2,1)} %get-tuple-element.51.own_ref, bf16[128,4096]{1,0:T(8,128)(2,1)} %bitcast.70, bf16[128,4096]{1,0:T(8,128)(2,1)} %bitcast.74, ...), custom_call_target="tpu_custom_call" | custom-call | tf_op jit(solution)/shard_map/combine/pallas_call | solution.py:397
  (24 shorter events, 0.1 us)
Async XLA Ops:
  8.7 6.0 %copy-start.6 = (bf16[768,1024]{1,0:T(8,128)(2,1)S(1)}, bf16[768,1024]{1,0:T(8,128)(2,1)}, u32[]{:S(2)}) copy-start(bf16[768,1024]{1,0:T(8,128)(2,1)} %get-tuple-element.33) | copy-start | bytes 4718596
  8.7 7.5 %copy-start.5 = (bf16[4096]{0:T(1024)(128)(2,1)S(1)}, bf16[4096]{0:T(1024)(128)(2,1)}, u32[]{:S(2)}) copy-start(bf16[4096]{0:T(1024)(128)(2,1)} %param.17) | copy-start | bytes 24580
  8.7 49.3 %all-to-all-start = ((bf16[8,448,512]{2,1,0:T(8,128)(2,1)}), bf16[8,448,512]{2,1,0:T(8,128)(2,1)}, u32[]{:S(2)}, u32[]{:S(2)}) async-start(bf16[8,448,512]{2,1,0:T(8,128)(2,1)} %get-tuple-element.32), calls=%async_computation | async-start | bytes 7340032 | tf_op jit(solution)/shard_map/all_to_all | solution.py:436
  14.7 35.9 %collective-permute-start = (bf16[768,1024]{1,0:T(8,128)(2,1)S(1)}, bf16[768,1024]{1,0:T(8,128)(2,1)S(1)}, u32[]{:S(2)}, u32[]{:S(2)}) collective-permute-start(bf16[768,1024]{1,0:T(8,128)(2,1)S(1)} %copy-done.6), channel_id=1, source_target_pairs={{0,1},{1,0},{2,3},{3,2},{4,5},{5,4},{6,7},{7,6},{8,9},{9,8},{10,11... | collective-permute-start | bytes 4718600 | tf_op jit(solution)/shard_map/ppermute | solution.py:468
  16.1 68.2 %collective-permute-start.1 = (bf16[768,1024]{1,0:T(8,128)(2,1)}, bf16[768,1024]{1,0:T(8,128)(2,1)}, u32[]{:S(2)}, u32[]{:S(2)}) collective-permute-start(bf16[768,1024]{1,0:T(8,128)(2,1)} %get-tuple-element.38), channel_id=1, source_target_pairs={{0,1},{1,0},{2,3},{3,2},{4,5},{5,4},{6,7},{7,6},{8,9},{9,8},{10,11... | collective-permute-start | bytes 4718600 | tf_op jit(solution)/shard_map/ppermute | solution.py:468
  58.0 134.7 %slice-start.4 = ((s8[6291456]{0:T(1024)(128)(4,1)}), s8[2097152]{0:T(1024)(128)(4,1)S(1)}, s32[]{:S(2)}) async-start(s8[6291456]{0:T(1024)(128)(4,1)} %bitcast.62), calls=%async_computation.7 | async-start | bytes 4194304
  84.3 108.4 %slice-start.2 = ((s8[6291456]{0:T(1024)(128)(4,1)}), s8[4194304]{0:T(1024)(128)(4,1)S(1)}, s32[]{:S(2)}) async-start(s8[6291456]{0:T(1024)(128)(4,1)} %bitcast.56), calls=%async_computation.5 | async-start | bytes 8388608
  84.3 108.4 %slice-start.3 = ((s8[6291456]{0:T(1024)(128)(4,1)}), s8[2097152]{0:T(1024)(128)(4,1)S(1)}, s32[]{:S(2)}) async-start(s8[6291456]{0:T(1024)(128)(4,1)} %bitcast.56), calls=%async_computation.6 | async-start | bytes 4194304
  84.3 108.4 %slice-start.5 = ((s8[6291456]{0:T(1024)(128)(4,1)}), s8[4194304]{0:T(1024)(128)(4,1)S(1)}, s32[]{:S(2)}) async-start(s8[6291456]{0:T(1024)(128)(4,1)} %bitcast.62), calls=%async_computation.8 | async-start | bytes 8388608
  192.8 14.6 %slice-start = ((s8[6291456]{0:T(1024)(128)(4,1)}), s8[4194304]{0:T(1024)(128)(4,1)S(1)}, s32[]{:S(2)}) async-start(s8[6291456]{0:T(1024)(128)(4,1)} %bitcast.49), calls=%async_computation.3 | async-start | bytes 8388608
  197.9 9.4 %slice-start.1 = ((s8[6291456]{0:T(1024)(128)(4,1)}), s8[2097152]{0:T(1024)(128)(4,1)S(1)}, s32[]{:S(2)}) async-start(s8[6291456]{0:T(1024)(128)(4,1)} %bitcast.49), calls=%async_computation.4 | async-start | bytes 4194304
  197.9 9.4 %collective-permute-start.2 = (bf16[256,768]{1,0:T(8,128)(2,1)S(1)}, bf16[256,768]{1,0:T(8,128)(2,1)S(1)}, u32[]{:S(2)}, u32[]{:S(2)}) collective-permute-start(bf16[256,768]{1,0:T(8,128)(2,1)S(1)} %expert_open.4.mine_ref), channel_id=1, source_target_pairs={{0,1},{1,0},{2,3},{3,2},{4,5},{5,4},{6,7},{7,6},{8,9},{9,8},{10,11... | collective-permute-start | bytes 1179656 | tf_op jit(solution)/shard_map/ppermute | solution.py:494
  203.3 13.6 %collective-permute-start.3 = (bf16[256,768]{1,0:T(8,128)(2,1)S(1)}, bf16[256,768]{1,0:T(8,128)(2,1)S(1)}, u32[]{:S(2)}, u32[]{:S(2)}) collective-permute-start(bf16[256,768]{1,0:T(8,128)(2,1)S(1)} %expert_open.5.mine_ref), channel_id=1, source_target_pairs={{0,1},{1,0},{2,3},{3,2},{4,5},{5,4},{6,7},{7,6},{8,9},{9,8},{10,11... | collective-permute-start | bytes 1179656 | tf_op jit(solution)/shard_map/ppermute | solution.py:494
  221.4 6.8 %collective-permute-start.5 = (bf16[256,768]{1,0:T(8,128)(2,1)S(1)}, bf16[256,768]{1,0:T(8,128)(2,1)S(1)}, u32[]{:S(2)}, u32[]{:S(2)}) collective-permute-start(bf16[256,768]{1,0:T(8,128)(2,1)S(1)} %expert_open.7.mine_ref), channel_id=1, source_target_pairs={{0,1},{1,0},{2,3},{3,2},{4,5},{5,4},{6,7},{7,6},{8,9},{9,8},{10,11... | collective-permute-start | bytes 1179656 | tf_op jit(solution)/shard_map/ppermute | solution.py:494
  227.1 11.3 %collective-permute-start.4 = (bf16[256,768]{1,0:T(8,128)(2,1)S(1)}, bf16[256,768]{1,0:T(8,128)(2,1)S(1)}, u32[]{:S(2)}, u32[]{:S(2)}) collective-permute-start(bf16[256,768]{1,0:T(8,128)(2,1)S(1)} %expert_open.6.mine_ref), channel_id=1, source_target_pairs={{0,1},{1,0},{2,3},{3,2},{4,5},{5,4},{6,7},{7,6},{8,9},{9,8},{10,11... | collective-permute-start | bytes 1179656 | tf_op jit(solution)/shard_map/ppermute | solution.py:494
  242.8 2.0 copy-start
  244.8 11.2 %copy-start.1 = (bf16[2,4,128,512]{3,2,1,0:T(8,128)(2,1)S(1)}, bf16[2,4,128,512]{3,2,1,0:T(8,128)(2,1)}, u32[]{:S(2)}) copy-start(bf16[2,4,128,512]{3,2,1,0:T(8,128)(2,1)} %get-tuple-element.52) | copy-start | bytes 3145732
  244.8 69.9 %all-to-all-start.2 = ((bf16[128,8,2048]{2,1,0:T(8,128)(2,1)}), bf16[128,8,2048]{2,1,0:T(8,128)(2,1)}, u32[]{:S(2)}, u32[]{:S(2)}) async-start(bf16[128,8,2048]{2,1,0:T(8,128)(2,1)} %bitcast.55), calls=%async_computation.2 | async-start | bytes 8388608 | tf_op jit(solution)/shard_map/all_to_all | solution.py:436
  256.1 2.8 collective-permute-start.6
  259.8 47.9 %collective-permute-start.9 = (bf16[2,128,512]{2,1,0:T(8,128)(2,1)S(1)}, bf16[2,128,512]{2,1,0:T(8,128)(2,1)S(1)}, u32[]{:S(2)}, u32[]{:S(2)}) collective-permute-start(bf16[2,128,512]{2,1,0:T(8,128)(2,1)S(1)} %get-tuple-element.55), channel_id=1, source_target_pairs={{0,96},{16,112},{32,0},{48,16},{64,32},{80,48},{96,64},{112,80},{1... | collective-permute-start | bytes 786440 | tf_op jit(solution)/shard_map/ppermute | solution.py:430
  261.9 47.1 %collective-permute-start.7 = (bf16[2,128,512]{2,1,0:T(8,128)(2,1)S(1)}, bf16[2,128,512]{2,1,0:T(8,128)(2,1)S(1)}, u32[]{:S(2)}, u32[]{:S(2)}) collective-permute-start(bf16[2,128,512]{2,1,0:T(8,128)(2,1)S(1)} %get-tuple-element.57), channel_id=1, source_target_pairs={{0,32},{16,48},{32,64},{48,80},{64,96},{80,112},{96,0},{112,16},{1... | collective-permute-start | bytes 786440 | tf_op jit(solution)/shard_map/ppermute | solution.py:430
  261.9 52.9 %collective-permute-start.8 = (bf16[2,128,512]{2,1,0:T(8,128)(2,1)S(1)}, bf16[2,128,512]{2,1,0:T(8,128)(2,1)S(1)}, u32[]{:S(2)}, u32[]{:S(2)}) collective-permute-start(bf16[2,128,512]{2,1,0:T(8,128)(2,1)S(1)} %get-tuple-element.58), channel_id=1, source_target_pairs={{0,64},{16,80},{32,96},{48,112},{64,0},{80,16},{96,32},{112,48},{1... | collective-permute-start | bytes 786440 | tf_op jit(solution)/shard_map/ppermute | solution.py:430
  307.7 7.0 %copy-start.2 = (bf16[2,128,512]{2,1,0:T(8,128)(2,1)}, bf16[2,128,512]{2,1,0:T(8,128)(2,1)S(1)}, u32[]{:S(2)}) copy-start(bf16[2,128,512]{2,1,0:T(8,128)(2,1)S(1)} %collective-permute-done.9.rest_3_) | copy-start | bytes 786436
  309.0 5.8 %copy-start.3 = (bf16[2,128,512]{2,1,0:T(8,128)(2,1)}, bf16[2,128,512]{2,1,0:T(8,128)(2,1)S(1)}, u32[]{:S(2)}) copy-start(bf16[2,128,512]{2,1,0:T(8,128)(2,1)S(1)} %collective-permute-done.7.rest_1_) | copy-start | bytes 786436
  314.7 0.7 copy-start.4

commit v5 on v4

v5 whole, which is shorter than its diff:
```python
import functools
import math

import jax
import jax.numpy as jnp
from jax import lax
from jax.experimental import pallas as pl
from jax.experimental.pallas import tpu as pltpu
from jax.sharding import PartitionSpec as P

HEAD_DIM = 128
TOP = 8
SLOTS = 8
bf16 = jnp.bfloat16
f32 = jnp.float32


def params(mib):
    return pltpu.CompilerParams(vmem_limit_bytes=mib * 1024 * 1024)


def iota(shape, dim):
    return lax.broadcasted_iota(jnp.int32, shape, dim)


def ones(where):
    return jnp.where(where, jnp.float32(1.0), jnp.float32(0.0)).astype(bf16)


def dot(a, b, dims=((1,), (0,))):
    return lax.dot_general(a, b, (dims, ((), ())), preferred_element_type=f32)


def half_kernel(half_ref, down_ref, out_ref):
    del half_ref
    out_ref[...] = down_ref[...]


def take_half(half, down):
    depth, width = down.shape
    steps = 4
    span = width // 2 // steps
    return pl.pallas_call(
        half_kernel,
        grid_spec=pltpu.PrefetchScalarGridSpec(
            num_scalar_prefetch=1,
            grid=(steps,),
            in_specs=[pl.BlockSpec((depth, span), lambda c, half: (0, half[0] * steps + c))],
            out_specs=pl.BlockSpec((depth, span), lambda c, half: (0, c)),
        ),
        out_shape=jax.ShapeDtypeStruct((depth, width // 2), bf16),
        compiler_params=params(60),
        name="take_half",
    )(half, down)


def prepare_kernel(
    q_ref,
    k_ref,
    v_ref,
    res_ref,
    flag_ref,
    ids_ref,
    gates_ref,
    out_ref,
    own_ref,
    pick_ref,
    table_ref,
):
    rows = q_ref.shape[0]
    merge, _, cols = out_ref.shape
    experts, most = table_ref.shape
    extra = 3 * rows + most

    @pl.when(pl.program_id(0) == 0)
    def _():
        upper = ones(iota((rows, rows), 0) < iota((rows, rows), 1))
        masked = flag_ref[...] == 1
        rank = dot(ones(jnp.broadcast_to(flag_ref[...], (16, rows)) == 1), upper)[:1]
        pick = ones((iota((most, rows), 0).astype(f32) == rank) & masked)
        pick_ref[...] = pick
        slow = iota((experts, rows), 0)
        order = slow % TOP * TOP + slow // TOP
        named = jnp.zeros((experts, rows), f32)
        gates = jnp.zeros((experts, rows), f32)
        for k in range(TOP):
            hit = (order == ids_ref[k : k + 1, :]) & masked
            named = jnp.where(hit, 1.0, named)
            gates = jnp.where(hit, gates_ref[k : k + 1, :], gates)
        place = (named * (dot(named.astype(bf16), upper) + 1.0)).astype(bf16)
        high = gates.astype(bf16)
        own_ref[0] = place
        own_ref[1] = high
        own_ref[2] = (gates - high.astype(f32)).astype(bf16)
        table_ref[...] = dot(place, pick, ((1,), (1,))).astype(bf16)

    numbers = iota((16, rows), 1).astype(f32).astype(bf16)
    spot = dot(numbers, pick_ref[...], ((1,), (1,)))
    count = dot(jnp.ones((16, rows), bf16), pick_ref[...], ((1,), (1,)))
    spot = jnp.where(count > 0.5, spot, -1.0).astype(bf16)
    for m in range(merge):
        here = slice(m * cols, (m + 1) * cols)
        out_ref[m, :rows] = q_ref[:, here]
        out_ref[m, rows : 2 * rows] = k_ref[:, here]
        out_ref[m, 2 * rows : 3 * rows] = v_ref[:, here]
        out_ref[m, 3 * rows : extra] = dot(pick_ref[...], res_ref[:, here]).astype(bf16)
        out_ref[m, extra:] = jnp.zeros((16, cols), bf16)
        for h in range(experts // 16):
            out_ref[m, extra:, h * 128 : h * 128 + most] = table_ref[h * 16 : (h + 1) * 16]
            out_ref[m, extra:, h * 128 + 64 : h * 128 + 64 + most] = spot


def prepare(q, k, v, res, flags, ids, gates, groups, experts, most):
    rows, width = q.shape
    cols = width // groups
    total = 3 * rows + most + 16
    merge = 2
    piece = pl.BlockSpec((rows, merge * cols), lambda j: (0, j))
    return pl.pallas_call(
        prepare_kernel,
        grid=(groups // merge,),
        in_specs=[
            piece,
            piece,
            piece,
            piece,
            pl.BlockSpec((1, rows), lambda j: (0, 0)),
            pl.BlockSpec((TOP, rows), lambda j: (0, 0)),
            pl.BlockSpec((TOP, rows), lambda j: (0, 0)),
        ],
        out_specs=[
            pl.BlockSpec((merge, total, cols), lambda j: (j, 0, 0)),
            pl.BlockSpec((3, experts, rows), lambda j: (0, 0, 0)),
        ],
        out_shape=[
            jax.ShapeDtypeStruct((groups, total, cols), bf16),
            jax.ShapeDtypeStruct((3, experts, rows), bf16),
        ],
        scratch_shapes=[pltpu.VMEM((most, rows), bf16), pltpu.VMEM((experts, most), bf16)],
        compiler_params=params(60),
        name="prepare",
    )(q, k, v, res, flags, ids, gates)


def attend_kernel(in_ref, attn_ref, v_ref):
    blocks, rows, cols = attn_ref.shape
    length = blocks * rows
    scale = math.log2(math.e) / math.sqrt(HEAD_DIM)
    step = 2
    v_ref[:, HEAD_DIM:] = jnp.ones((length, HEAD_DIM), bf16)
    for h in range(cols // HEAD_DIM):
        here = slice(h * HEAD_DIM, (h + 1) * HEAD_DIM)
        k_all = in_ref[:, rows : 2 * rows, here].reshape(length, HEAD_DIM)
        v_ref[:, :HEAD_DIM] = in_ref[:, 2 * rows : 3 * rows, here].reshape(length, HEAD_DIM)
        for first in range(0, blocks, step):
            q_part = in_ref[first : first + step, :rows, here].reshape(step * rows, HEAD_DIM)
            scores = dot(q_part, k_all, ((1,), (1,)))
            peak = jnp.max(scores, axis=-1, keepdims=True)
            expo = jnp.exp2((scores - peak) * scale).astype(bf16)
            mixed = dot(expo, v_ref[...])
            attn = (mixed[:, :HEAD_DIM] / mixed[:, HEAD_DIM:]).astype(bf16)
            attn_ref[first : first + step, :, here] = attn.reshape(step, rows, HEAD_DIM)


def attend(pieces, rows, heads=2):
    blocks, _, cols = pieces.shape
    span = heads * HEAD_DIM
    return pl.pallas_call(
        attend_kernel,
        grid=(cols // span,),
        in_specs=[pl.BlockSpec((blocks, 3 * rows, span), lambda h: (0, 0, h))],
        out_specs=pl.BlockSpec((blocks, rows, span), lambda h: (0, 0, h)),
        out_shape=jax.ShapeDtypeStruct((blocks, rows, cols), bf16),
        scratch_shapes=[pltpu.VMEM((blocks * rows, 2 * HEAD_DIM), bf16)],
        compiler_params=params(60),
        name="attend",
    )(pieces)


def pick_kernel(attn_ref, res_ref, table_ref, gain_ref, out_ref, place_ref, spot_ref):
    blocks, rows, cols = attn_ref.shape
    experts, most = place_ref.shape[1] // SLOTS, place_ref.shape[2]

    @pl.when(pl.program_id(0) == 0)
    def _():
        wanted = iota((16, SLOTS, most), 1).astype(f32) + 1.0
        for b in range(blocks):
            for h in range(experts // 16):
                table = table_ref[b, :, h * 128 : h * 128 + most].astype(f32)
                hit = jnp.where(table[:, None, :] == wanted, 1.0, 0.0)
                place_ref[b, h * 128 : (h + 1) * 128] = hit.reshape(128, most).astype(bf16)
            spot = table_ref[b, :, 64 : 64 + most].astype(f32)[:1]
            spot_ref[b] = ones(iota((rows, most), 0).astype(f32) == spot)

    gain = gain_ref[...].astype(f32)
    for b in range(blocks):
        hidden = dot(spot_ref[b], attn_ref[b], ((0,), (0,))) + res_ref[b].astype(f32)
        sent = dot(place_ref[b], (hidden * gain).astype(bf16))
        sent = sent.reshape(TOP, experts // TOP, SLOTS, cols).astype(bf16)
        out_ref[:, 0, :, b] = sent
        out_ref[:, 1, :, b] = sent


def pick(attn, pieces, gain, experts):
    blocks, rows, cols = attn.shape
    total = pieces.shape[1]
    most = total - 3 * rows - 16
    span = 256
    blocked = experts // TOP
    return pl.pallas_call(
        pick_kernel,
        grid=(cols // span,),
        in_specs=[
            pl.BlockSpec((blocks, rows, span), lambda h: (0, 0, h)),
            pl.BlockSpec((blocks, most, span), lambda h: (0, 3 * rows // most, h)),
            pl.BlockSpec((blocks, 16, cols), lambda h: (0, total // 16 - 1, 0)),
            pl.BlockSpec((1, span), lambda h: (0, h)),
        ],
        out_specs=pl.BlockSpec(
            (TOP, 2, blocked, blocks, SLOTS, span), lambda h: (0, 0, 0, 0, 0, h)
        ),
        out_shape=jax.ShapeDtypeStruct((TOP, 2, blocked, blocks, SLOTS, cols), bf16),
        scratch_shapes=[
            pltpu.VMEM((blocks, experts * SLOTS, most), bf16),
            pltpu.VMEM((blocks, rows, most), bf16),
        ],
        compiler_params=params(60),
        name="pick",
    )(attn, pieces, pieces, gain)


def open_kernel(
    rows_ref, weigh_ref, gate_ref, up_ref, out_ref, gates_ref, ups_ref, square_ref
):
    step = pl.program_id(0)
    last = pl.num_programs(0) - 1
    count, merge, per, cols = rows_ref.shape
    total = count * per

    @pl.when(step == 0)
    def _():
        gates_ref[...] = jnp.zeros_like(gates_ref)
        ups_ref[...] = jnp.zeros_like(ups_ref)
        square_ref[...] = jnp.zeros_like(square_ref)

    tiles = max(total // 256, 1)
    tile = total // tiles
    for t in range(tiles):
        inside = slice(t * count // tiles, (t + 1) * count // tiles)
        rows = slice(t * tile, (t + 1) * tile)
        gate_part = gates_ref[rows]
        up_part = ups_ref[rows]
        square = square_ref[rows]
        for m in range(merge):
            here = slice(m * cols, (m + 1) * cols)
            x = rows_ref[inside, m].reshape(tile, cols)
            gate_part += dot(x, gate_ref[here])
            up_part += dot(x, up_ref[here])
            square += dot(x * x, weigh_ref[here])
        gates_ref[rows] = gate_part
        ups_ref[rows] = up_part
        square_ref[rows] = square

    @pl.when(step == last)
    def _():
        mean = (square_ref[:, :1] + square_ref[:, 1:2]) / ((last + 1) * merge * cols)
        scale = lax.rsqrt(mean + 1e-06)
        gate_full = gates_ref[...] * scale
        act = gate_full / (1.0 + jnp.exp(-gate_full)) * (ups_ref[...] * scale)
        out_ref[...] = act.astype(bf16)


def expert_open(arrived, part, per, weigh, gate, up):
    count, groups, _, cols = arrived.shape
    width, half = gate.shape
    total = count * per
    merge = 2
    weight = pl.BlockSpec((merge * cols, half), lambda n: (n, 0))
    return pl.pallas_call(
        open_kernel,
        grid=(groups // merge,),
        in_specs=[
            pl.BlockSpec((count, merge, per, cols), lambda n: (0, n, part, 0)),
            pl.BlockSpec((merge * cols, 128), lambda n: (n, 0)),
            weight,
            weight,
        ],
        out_specs=pl.BlockSpec((total, half), lambda n: (0, 0)),
        out_shape=jax.ShapeDtypeStruct((total, half), bf16),
        scratch_shapes=[
            pltpu.VMEM((total, half), f32),
            pltpu.VMEM((total, half), f32),
            pltpu.VMEM((total, 128), f32),
        ],
        compiler_params=params(52),
        cost_estimate=pl.CostEstimate(
            flops=4 * total * width * half,
            bytes_accessed=4 * width * half + 2 * total * (width + half),
            transcendentals=total * half,
        ),
        name="expert_open",
    )(arrived, weigh, gate, up)


def close_kernel(
    role_ref, first_ref, mine_ref, second_ref, first_down, own_down, second_down, *rest
):
    out_ref = rest[-1]
    def emit(act_ref, down_ref):
        result = dot(first_ref[...], first_down[...]) + dot(act_ref[...], down_ref[...])
        out_ref[...] = result.reshape(out_ref.shape).astype(bf16)

    @pl.when(role_ref[0] == 1)
    def _():
        emit(mine_ref, own_down)

    @pl.when(role_ref[0] == 0)
    def _():
        emit(second_ref, second_down)


def expert_close(role, acts, downs, part, groups, count, done):
    total, half = acts[0].shape
    width = downs[0].shape[1]
    span = 512
    steps = width // span
    merge = total // (count * SLOTS)
    act = pl.BlockSpec((total, half), lambda c, role: (0, 0))
    held = [] if done is None else [done]

    def down(place):
        return pl.BlockSpec((half, span), lambda c, role: (0, place(c, role)))

    return pl.pallas_call(
        close_kernel,
        grid_spec=pltpu.PrefetchScalarGridSpec(
            num_scalar_prefetch=1,
            grid=(steps,),
            in_specs=[
                act,
                act,
                act,
                down(lambda c, role: c),
                down(lambda c, role: role[0] * (role[1] * steps + c)),
                down(lambda c, role: (1 - role[0]) * c),
            ]
            + [pl.BlockSpec(memory_space=pl.ANY)] * len(held),
            out_specs=pl.BlockSpec((count, merge, SLOTS, span), lambda c, role: (0, part, 0, c)),
        ),
        out_shape=jax.ShapeDtypeStruct((count, groups, SLOTS, width), bf16),
        input_output_aliases={7: 0} if held else {},
        compiler_params=params(44),
        cost_estimate=pl.CostEstimate(
            flops=4 * total * width * half,
            bytes_accessed=2 * (2 * width * half + total * (2 * half + width)),
            transcendentals=0,
        ),
        name="expert_close",
    )(role, *acts, *downs, *held)


def combine_kernel(back_ref, own_ref, attn_ref, res_ref, cached_ref, out_ref, mix_ref):
    _, experts, rows = own_ref.shape
    slots = experts * SLOTS
    cols = out_ref.shape[1]

    @pl.when(pl.program_id(0) == 0)
    def _():
        column = iota((experts, slots), 1) // SLOTS
        order = column // 8 * 8 + column % 4 * 2 + column // 4 % 2
        spread = ones(iota((experts, slots), 0) == order)
        slot = (iota((rows, slots), 1) % SLOTS + 1).astype(f32)
        hit = dot(own_ref[0], spread, ((0,), (0,))) == slot
        for i in range(2):
            gates = dot(own_ref[1 + i], spread, ((0,), (0,)))
            mix_ref[i * rows : (i + 1) * rows] = jnp.where(hit, gates, 0.0).astype(bf16)

    both = dot(mix_ref[...], back_ref[...].reshape(slots, cols))
    mixed = both[:rows] + both[rows:]
    named = dot(own_ref[0], jnp.ones((experts, 128), bf16), ((0,), (0,)))
    moe = jnp.where(named[:, :1] > 0.5, mixed, cached_ref[...].astype(f32))
    merge, _, piece = attn_ref.shape
    for m in range(merge):
        here = slice(m * piece, (m + 1) * piece)
        hid = res_ref[:, here].astype(f32) + attn_ref[m].astype(f32)
        out_ref[:, here] = (hid + moe[:, here]).astype(bf16)


def combine(back, own, attn, residual, cached, span=1024):
    count, chips, cores, _, half = back.shape
    groups, rows, piece = attn.shape
    width = groups * piece
    experts = own.shape[1]
    merge = span // piece
    steps = half // span
    flat = pl.BlockSpec((rows, span), lambda j: (0, j))
    return pl.pallas_call(
        combine_kernel,
        grid=(width // span,),
        in_specs=[
            pl.BlockSpec(
                (count, chips, 1, SLOTS, span), lambda j: (0, 0, j // steps, 0, j % steps)
            ),
            pl.BlockSpec(own.shape, lambda j: (0, 0, 0)),
            pl.BlockSpec((merge, rows, piece), lambda j: (j, 0, 0)),
            flat,
            flat,
        ],
        out_specs=flat,
        out_shape=jax.ShapeDtypeStruct((rows, width), bf16),
        scratch_shapes=[pltpu.VMEM((2 * rows, experts * SLOTS), bf16)],
        compiler_params=params(60),
        name="combine",
    )(back, own, attn, residual, cached)


def exchange(blocks, axes):
    return lax.all_to_all(blocks, axes, split_axis=0, concat_axis=0, tiled=True)


def per_device(
    queries,
    keys,
    values,
    residual_in,
    cached_moe,
    norm_gain,
    still_masked,
    expert_ids,
    gate_weights,
    w_gate,
    w_up,
    w_down,
):
    rows, width = queries.shape[1:]
    seq_count = lax.axis_size("seq")
    exp_count = lax.axis_size("exp")
    devices = seq_count * exp_count
    experts = devices // 2
    cols = width // seq_count
    most = rows * 3 // 8
    all_axes = ("seq", "exp")
    gain = norm_gain[None, :]
    own_gain = lax.dynamic_slice_in_dim(gain, lax.axis_index("seq") * cols, cols, 1)
    weigh = 1.0 / jnp.square(norm_gain.astype(f32))
    high = weigh.astype(bf16)
    low = (weigh - high.astype(f32)).astype(bf16)
    weigh = jnp.pad(jnp.stack([high, low], axis=1), ((0, 0), (0, 126)))

    ring, cross, beside = [], [], []
    for s in range(seq_count):
        for p in range(exp_count):
            here = s * exp_count + p
            other_core = (s ^ 1) * exp_count + p
            other_chip = s * exp_count + (p ^ 1)
            both = (s ^ 1) * exp_count + (p ^ 1)
            if p % 2 == s % 2:
                ring.append((here, other_core))
                beside.append((here, other_core))
            else:
                ring.append((here, other_chip))
                cross.append((here, both))
    core = lax.axis_index("seq") % 2
    odd = lax.axis_index("exp") % 2
    role = jnp.stack([(core == odd).astype(jnp.int32), core.astype(jnp.int32)])

    first_down = take_half((1 - odd)[None].astype(jnp.int32), w_down[0])
    first_down = lax.ppermute(first_down, all_axes, ring)
    second_down = take_half(odd[None].astype(jnp.int32), w_down[0])
    second_down = lax.ppermute(second_down, all_axes, cross)
    pieces, own = prepare(
        queries[0],
        keys[0],
        values[0],
        residual_in[0],
        still_masked,
        expert_ids[0].T,
        gate_weights[0].T,
        seq_count,
        experts,
        most,
    )
    pieces = exchange(pieces, "seq")
    tied = lax.optimization_barrier((pieces, weigh, own_gain, first_down))
    pieces, weigh, own_gain, first_down = tied

    attn = attend(pieces, rows)
    sent = pick(attn, pieces, own_gain, experts)
    attn = exchange(attn, "seq")
    sent, attn, second_down = lax.optimization_barrier((sent, attn, second_down))
    arrived = exchange(sent.reshape(devices, seq_count * SLOTS, cols), ("exp", "seq"))
    arrived = arrived.reshape(exp_count, seq_count, seq_count * SLOTS, cols)

    parts = 2
    per = seq_count * SLOTS // parts
    mine, first = [], []
    for part in range(parts):
        mine.append(expert_open(arrived, part, per, weigh, w_gate[0], w_up[0]))
        arrived, mine[part] = lax.optimization_barrier((arrived, mine[part]))
        first.append(lax.ppermute(mine[part], all_axes, ring))
    first[0], mine[1] = lax.optimization_barrier((first[0], mine[1]))
    downs = (first_down, w_down[0], second_down)
    done = None
    for part in range(parts):
        second = lax.ppermute(first[part], all_axes, beside)
        acts = (first[part], mine[part], second)
        done = expert_close(role, acts, downs, part, seq_count, exp_count, done)
        if part == 0:
            first[1], done = lax.optimization_barrier((first[1], done))
    back = exchange(done.reshape(devices, SLOTS, width // 2), ("exp", "seq"))
    back = back.reshape(exp_count, seq_count // 2, 2, SLOTS, width // 2)
    out = combine(back, own, attn, residual_in[0], cached_moe[0])
    return out[None]


def solution(mesh):
    return jax.shard_map(
        per_device,
        mesh=mesh,
        in_specs=(
            P("exp", "seq", None),
            P("exp", "seq", None),
            P("exp", "seq", None),
            P("exp", "seq", None),
            P("exp", "seq", None),
            P(),
            P("exp", "seq"),
            P("exp", "seq", None),
            P("exp", "seq", None),
            P(("seq", "exp"), None, None),
            P(("seq", "exp"), None, None),
            P(("seq", "exp"), None, None),
        ),
        out_specs=P("exp", "seq", None),
        check_vma=False,
    )
```

time: 323 us -> 310 us (0.960)
  waiting for transfers between devices: 117 us -> 42 us
  blocking collectives: 108 us -> 166 us
  Pallas kernels: 65.4 us -> 73.6 us
  starting transfers between devices: 26.9 us -> 21.5 us
    ppermute x10 -> x6, waiting for transfers between devices: 109 us -> 38.9 us  [the longest x1 23.4 us: per_device(): first_down = lax.ppermute(first_down, all_axes, ring)]
    all_to_all x1 -> x2, blocking collectives: 108 us -> 166 us  [exchange(): return lax.all_to_all(blocks, axes, split_axis=0, concat_axis=0, tiled=True)]
    pallas_call x2 -> x4, Pallas kernels: 10 us -> 20.9 us  [the longest x2 8.55 us: take_half(): pl.pallas_call(half_kernel, grid_spec=pltpu.PrefetchScalarGridSpec(num_sc...]
    all_to_all x2, starting transfers between devices: 17.2 us -> 10.8 us  [exchange(): return lax.all_to_all(blocks, axes, split_axis=0, concat_axis=0, tiled=True)]
    all_to_all x2, waiting for transfers between devices: 7.42 us -> 3.11 us  [exchange(): return lax.all_to_all(blocks, axes, split_axis=0, concat_axis=0, tiled=True)]
    pallas_call x1, Pallas kernels: 12.2 us -> 8.12 us  [attend(): pl.pallas_call(attend_kernel, grid=(cols // span,), in_specs=[pl.BlockSpe...]
    pallas_call x4 -> x2, Pallas kernels: 20.5 us -> 24 us  [expert_open(): pl.pallas_call(open_kernel, grid=(groups // merge,), in_specs=[pl.BlockSp...]
    pallas_call x4 -> x2, Pallas kernels: 17.6 us -> 15.5 us  [expert_close(): pl.pallas_call(close_kernel, grid_spec=pltpu.PrefetchScalarGridSpec(num_s...]
  transfers between devices with their start and end apart: 12 -> 8, of which waited for: 9 -> 5; matrix products, arithmetic and copies ran while one was open for 0% -> 1% of each run, Pallas kernels for 11% -> 14%
where the time goes in v5:
time: 310 us; the launch traced here: 309 us
  blocking collectives  166 us (54%)
  Pallas kernels  73.6 us (24%)
  waiting for transfers between devices  42 us (14%)
  starting transfers between devices  21.5 us (7%)
  local copies, waits for them, and re-layouts  5.63 us (2%)
    all_to_all x2, blocking collectives, exchange(): return lax.all_to_all(blocks, axes, split_axis=0, concat_axis=0, tiled=True)  166 us
    pallas_call x2, Pallas kernels, expert_open(): pl.pallas_call(open_kernel, grid=(groups // merge,), in_specs=[pl.BlockSp...  24 us
    ppermute x1, waiting for transfers between devices, per_device(): first_down = lax.ppermute(first_down, all_axes, ring)  23.4 us
    pallas_call x2, Pallas kernels, expert_close(): pl.pallas_call(close_kernel, grid_spec=pltpu.PrefetchScalarGridSpec(num_s...  15.5 us
    ppermute x1, waiting for transfers between devices, per_device(): second_down = lax.ppermute(second_down, all_axes, cross)  12.2 us
    all_to_all x2, starting transfers between devices, exchange(): return lax.all_to_all(blocks, axes, split_axis=0, concat_axis=0, tiled=True)  10.8 us
    pallas_call x2, Pallas kernels, take_half(): pl.pallas_call(half_kernel, grid_spec=pltpu.PrefetchScalarGridSpec(num_sc...  8.55 us
    pallas_call x1, Pallas kernels, attend(): pl.pallas_call(attend_kernel, grid=(cols // span,), in_specs=[pl.BlockSpe...  8.12 us
  transfers between devices with their start and end apart: 8, of which 5 were waited for; matrix products, arithmetic and copies ran while one was open for 1% of the time, Pallas kernels for 14%

profile of v5, /device:TPU:1, one launch (start us, length us, event | category | flops | bytes accessed | tf_op | source)
XLA Modules:
  0.0 309.3 jit_solution(5080846812309225034)
XLA Ops:
  0.0 5.1 %prepare.1 = (bf16[8,448,512]{2,1,0:T(8,128)(2,1)}, bf16[3,64,128]{2,1,0:T(8,128)(2,1)}) custom-call(bf16[128,4096]{1,0:T(8,128)(2,1)} %bitcast.34, bf16[128,4096]{1,0:T(8,128)(2,1)} %bitcast.35, bf16[128,4096]{1,0:T(8,128)(2,1)} %bitcast.36, bf16[128,4096]{1,0:T(8,128)(2,1)} %bitcast.32, s32[1,128]{1,0:T(1,128)} %flag_ref.1, s32[8,128]{1,0:T(8,128)} %bitcast.38, ...), custom_call_target="tpu_custom_call" | custom-call | tf_op jit(solution)/shard_map/prepare/pallas_call | solution.py:119
  5.1 5.8 %all-to-all-start = ((bf16[8,448,512]{2,1,0:T(8,128)(2,1)}), bf16[8,448,512]{2,1,0:T(8,128)(2,1)}, u32[]{:S(2)}, u32[]{:S(2)}) async-start(bf16[8,448,512]{2,1,0:T(8,128)(2,1)} %get-tuple-element.21), calls=%async_computation | async-start | bytes 7340032 | tf_op jit(solution)/shard_map/all_to_all | solution.py:418
  10.9 4.3 %take_half.2 = bf16[768,2048]{1,0:T(8,128)(2,1)} custom-call(s32[1]{0:T(128)} %bitcast.10.half_ref, bf16[768,4096]{1,0:T(8,128)(2,1)} %bitcast.23), custom_call_target="tpu_custom_call" | custom-call | tf_op jit(solution)/shard_map/take_half/pallas_call | solution.py:43
  15.2 1.4 collective-permute-start
  16.5 0.0 copy-start.3
  16.5 4.3 %take_half.3 = bf16[768,2048]{1,0:T(8,128)(2,1)} custom-call(s32[1]{0:T(128)} %bitcast.12.half_ref, bf16[768,4096]{1,0:T(8,128)(2,1)} %bitcast.24), custom_call_target="tpu_custom_call" | custom-call | tf_op jit(solution)/shard_map/take_half/pallas_call | solution.py:43
  20.8 2.3 collective-permute-start.1
  23.1 0.0 copy-done.3
  23.1 0.1 dynamic-slice.3
  23.2 0.6 dynamic_slice.3.gain_ref
  23.9 1.4 copy.16
  25.3 2.4 pad.4.weigh_ref
  27.7 23.4 %collective-permute-done.first_down = bf16[768,2048]{1,0:T(8,128)(2,1)S(1)} collective-permute-done((bf16[768,2048]{1,0:T(8,128)(2,1)}, bf16[768,2048]{1,0:T(8,128)(2,1)S(1)}, u32[]{:S(2)}, u32[]{:S(2)}) %collective-permute-start) | collective-permute-done | bytes 3145760 | tf_op jit(solution)/shard_map/ppermute | solution.py:468
  51.1 3.1 %all-to-all-done.in_ref.res_ref.table_ref = bf16[8,448,512]{2,1,0:T(8,128)(2,1)} async-done(((bf16[8,448,512]{2,1,0:T(8,128)(2,1)}), bf16[8,448,512]{2,1,0:T(8,128)(2,1)}, u32[]{:S(2)}, u32[]{:S(2)}) %all-to-all-start) | async-done | bytes 3670048 | tf_op jit(solution)/shard_map/all_to_all | solution.py:418
  54.2 8.1 %attend.1.attn_ref = bf16[8,128,512]{2,1,0:T(8,128)(2,1)} custom-call(bf16[8,448,512]{2,1,0:T(8,128)(2,1)} %all-to-all-done.in_ref.res_ref.table_ref), custom_call_target="tpu_custom_call" | custom-call | tf_op jit(solution)/shard_map/attend/pallas_call | solution.py:168
  62.3 5.0 %all-to-all-start.1 = ((bf16[8,128,512]{2,1,0:T(8,128)(2,1)}), bf16[8,128,512]{2,1,0:T(8,128)(2,1)}, u32[]{:S(2)}, u32[]{:S(2)}) async-start(bf16[8,128,512]{2,1,0:T(8,128)(2,1)} %attend.1.attn_ref), calls=%async_computation.1 | async-start | bytes 2097152 | tf_op jit(solution)/shard_map/all_to_all | solution.py:418
  67.3 6.4 %pick.1 = bf16[8,2,8,8,8,512]{5,4,3,2,1,0:T(8,128)(2,1)} custom-call(bf16[8,128,512]{2,1,0:T(8,128)(2,1)} %attend.1.attn_ref, bf16[8,448,512]{2,1,0:T(8,128)(2,1)} %all-to-all-done.in_ref.res_ref.table_ref, bf16[8,448,512]{2,1,0:T(8,128)(2,1)} %all-to-all-done.in_ref.res_ref.table_ref, bf16[1,512]{1,0:T(2,128)(2,1)} %dynamic_slice.3.gain_ref), custom_call_target="tpu_custom_call" | custom-call | tf_op jit(solution)/shard_map/pick/pallas_call | solution.py:210
  73.7 12.2 %collective-permute-done.1.second_down = bf16[768,2048]{1,0:T(8,128)(2,1)} collective-permute-done((bf16[768,2048]{1,0:T(8,128)(2,1)}, bf16[768,2048]{1,0:T(8,128)(2,1)}, u32[]{:S(2)}, u32[]{:S(2)}) %collective-permute-start.1) | collective-permute-done | bytes 3145760 | tf_op jit(solution)/shard_map/ppermute | solution.py:470
  85.9 0.0 all-to-all-done.1.attn_ref
  85.9 0.0 copy-start
  85.9 108.6 %all_to_all.20 = bf16[128,64,512]{2,1,0:T(8,128)(2,1)} all-to-all(bf16[128,64,512]{2,1,0:T(8,128)(2,1)} %bitcast.28), channel_id=1, replica_groups=mesh['seq'=8,'exp'=16] {'exp','seq'}, dimensions={0} | all-to-all | bytes 16777216 | tf_op jit(solution)/shard_map/all_to_all | solution.py:418
  194.5 0.0 copy-done
  194.5 11.6 %expert_open.2.mine_ref = bf16[512,768]{1,0:T(8,128)(2,1)S(1)} custom-call(bf16[16,8,64,512]{3,2,1,0:T(8,128)(2,1)} %bitcast.30, bf16[4096,128]{1,0:T(8,128)(2,1)S(1)} %copy-done, bf16[4096,768]{1,0:T(8,128)(2,1)} %bitcast.40, bf16[4096,768]{1,0:T(8,128)(2,1)} %bitcast.42), custom_call_target="tpu_custom_call" | custom-call | flops 6442450944 | bytes 17563648 | tf_op jit(solution)/shard_map/expert_open/pallas_call | solution.py:279
  206.1 0.0 copy-start.1
  206.1 0.3 collective-permute-start.3
  206.4 12.4 %expert_open.3.mine_ref = bf16[512,768]{1,0:T(8,128)(2,1)} custom-call(bf16[16,8,64,512]{3,2,1,0:T(8,128)(2,1)} %bitcast.31, bf16[4096,128]{1,0:T(8,128)(2,1)S(1)} %copy-done, bf16[4096,768]{1,0:T(8,128)(2,1)} %bitcast.41, bf16[4096,768]{1,0:T(8,128)(2,1)} %bitcast.43), custom_call_target="tpu_custom_call" | custom-call | flops 6442450944 | bytes 17563648 | tf_op jit(solution)/shard_map/expert_open/pallas_call | solution.py:279
  218.8 0.0 copy-done.1
  218.8 0.0 collective-permute-done.3.first_ref
  218.8 1.3 collective-permute-start.4
  220.1 4.2 %collective-permute-start.2 = (bf16[512,768]{1,0:T(8,128)(2,1)}, bf16[512,768]{1,0:T(8,128)(2,1)}, u32[]{:S(2)}, u32[]{:S(2)}) collective-permute-start(bf16[512,768]{1,0:T(8,128)(2,1)} %expert_open.3.mine_ref), channel_id=1, source_target_pairs={{0,16},{1,0},{2,18},{3,2},{4,20},{5,4},{6,22},{7,6},{8,24},{9,8},{... | collective-permute-start | bytes 2359304 | tf_op jit(solution)/shard_map/ppermute | solution.py:500
  224.3 0.1 pad_add_fusion.role_ref
  224.4 0.0 collective-permute-done.4.second_ref
  224.4 0.0 copy-start.2
  224.4 1.1 copy-done.2
  225.5 7.7 %expert_close.2.rest_0_ = bf16[16,8,8,2048]{3,2,1,0:T(8,128)(2,1)} custom-call(s32[2]{0:T(128)S(1)} %pad_add_fusion.role_ref, bf16[512,768]{1,0:T(8,128)(2,1)} %collective-permute-done.3.first_ref, bf16[512,768]{1,0:T(8,128)(2,1)S(1)} %copy-done.2, bf16[512,768]{1,0:T(8,128)(2,1)} %collective-permute-done.4.second_ref, ...), custom_call_target="tpu_custom_call" | custom-call | flops 3221225472 | bytes 9961472 | tf_op jit(solution)/shard_map/expert_close/pallas_call | solution.py:334
  233.3 0.3 collective-permute-done.2.first_ref
  233.6 1.3 collective-permute-start.5
  234.8 3.1 collective-permute-done.5.second_ref
  237.9 7.8 %expert_close.3 = bf16[16,8,8,2048]{3,2,1,0:T(8,128)(2,1)} custom-call(s32[2]{0:T(128)S(1)} %pad_add_fusion.role_ref, bf16[512,768]{1,0:T(8,128)(2,1)} %collective-permute-done.2.first_ref, bf16[512,768]{1,0:T(8,128)(2,1)} %expert_open.3.mine_ref, bf16[512,768]{1,0:T(8,128)(2,1)S(1)} %collective-permute-done.5.second_ref, ...), custom_call_target="tpu_custom_call", output_to_operand_aliasing={{}: (7, {})} | custom-call | flops 3221225472 | bytes 9961472 | tf_op jit(solution)/shard_map/expert_close/pallas_call | solution.py:334
  245.7 57.7 %all_to_all.21 = bf16[128,8,2048]{2,1,0:T(8,128)(2,1)} all-to-all(bf16[128,8,2048]{2,1,0:T(8,128)(2,1)} %bitcast.27), channel_id=1, replica_groups=mesh['seq'=8,'exp'=16] {'exp','seq'}, dimensions={0} | all-to-all | bytes 8388608 | tf_op jit(solution)/shard_map/all_to_all | solution.py:418
  303.4 5.9 %combine.1 = bf16[128,4096]{1,0:T(8,128)(2,1)} custom-call(bf16[16,4,2,8,2048]{4,3,2,1,0:T(8,128)(2,1)} %bitcast.29, bf16[3,64,128]{2,1,0:T(8,128)(2,1)} %get-tuple-element.35.own_ref, bf16[8,128,512]{2,1,0:T(8,128)(2,1)} %all-to-all-done.1.attn_ref, bf16[128,4096]{1,0:T(8,128)(2,1)} %bitcast.33, bf16[128,4096]{1,0:T(8,128)(2,1)} %bitcast.37), custom_call_target="tpu_custom_call" | custom-call | tf_op jit(solution)/shard_map/combine/pallas_call | solution.py:397
  (4 shorter events, 0.1 us)
Async XLA Ops:
  5.1 49.1 %all-to-all-start = ((bf16[8,448,512]{2,1,0:T(8,128)(2,1)}), bf16[8,448,512]{2,1,0:T(8,128)(2,1)}, u32[]{:S(2)}, u32[]{:S(2)}) async-start(bf16[8,448,512]{2,1,0:T(8,128)(2,1)} %get-tuple-element.21), calls=%async_computation | async-start | bytes 7340032 | tf_op jit(solution)/shard_map/all_to_all | solution.py:418
  15.2 35.9 %collective-permute-start = (bf16[768,2048]{1,0:T(8,128)(2,1)}, bf16[768,2048]{1,0:T(8,128)(2,1)S(1)}, u32[]{:S(2)}, u32[]{:S(2)}) collective-permute-start(bf16[768,2048]{1,0:T(8,128)(2,1)} %take_half.2), channel_id=1, source_target_pairs={{0,16},{1,0},{2,18},{3,2},{4,20},{5,4},{6,22},{7,6},{8,24},{9,8},{... | collective-permute-start | bytes 9437192 | tf_op jit(solution)/shard_map/ppermute | solution.py:468
  16.5 6.6 %copy-start.3 = (bf16[4096]{0:T(1024)(128)(2,1)S(1)}, bf16[4096]{0:T(1024)(128)(2,1)}, u32[]{:S(2)}) copy-start(bf16[4096]{0:T(1024)(128)(2,1)} %param.17) | copy-start | bytes 24580
  20.8 65.1 %collective-permute-start.1 = (bf16[768,2048]{1,0:T(8,128)(2,1)}, bf16[768,2048]{1,0:T(8,128)(2,1)}, u32[]{:S(2)}, u32[]{:S(2)}) collective-permute-start(bf16[768,2048]{1,0:T(8,128)(2,1)} %take_half.3), channel_id=1, source_target_pairs={{1,16},{3,18},{5,20},{7,22},{9,24},{11,26},{13,28},{15,30},{16,1},... | collective-permute-start | bytes 9437192 | tf_op jit(solution)/shard_map/ppermute | solution.py:470
  62.3 23.6 %all-to-all-start.1 = ((bf16[8,128,512]{2,1,0:T(8,128)(2,1)}), bf16[8,128,512]{2,1,0:T(8,128)(2,1)}, u32[]{:S(2)}, u32[]{:S(2)}) async-start(bf16[8,128,512]{2,1,0:T(8,128)(2,1)} %attend.1.attn_ref), calls=%async_computation.1 | async-start | bytes 2097152 | tf_op jit(solution)/shard_map/all_to_all | solution.py:418
  85.9 108.6 %copy-start = (bf16[4096,128]{1,0:T(8,128)(2,1)S(1)}, bf16[4096,128]{1,0:T(8,128)(2,1)}, u32[]{:S(2)}) copy-start(bf16[4096,128]{1,0:T(8,128)(2,1)} %pad.4.weigh_ref) | copy-start | bytes 3145732
  206.1 12.7 %copy-start.1 = (bf16[512,768]{1,0:T(8,128)(2,1)}, bf16[512,768]{1,0:T(8,128)(2,1)S(1)}, u32[]{:S(2)}) copy-start(bf16[512,768]{1,0:T(8,128)(2,1)S(1)} %expert_open.2.mine_ref) | copy-start | bytes 2359300
  206.1 12.7 %collective-permute-start.3 = (bf16[512,768]{1,0:T(8,128)(2,1)S(1)}, bf16[512,768]{1,0:T(8,128)(2,1)}, u32[]{:S(2)}, u32[]{:S(2)}) collective-permute-start(bf16[512,768]{1,0:T(8,128)(2,1)S(1)} %expert_open.2.mine_ref), channel_id=1, source_target_pairs={{0,16},{1,0},{2,18},{3,2},{4,20},{5,4},{6,22},{7,6},{8,24},{9,8},{... | collective-permute-start | bytes 2359304 | tf_op jit(solution)/shard_map/ppermute | solution.py:500
  218.8 5.5 %collective-permute-start.4 = (bf16[512,768]{1,0:T(8,128)(2,1)}, bf16[512,768]{1,0:T(8,128)(2,1)}, u32[]{:S(2)}, u32[]{:S(2)}) collective-permute-start(bf16[512,768]{1,0:T(8,128)(2,1)} %collective-permute-done.3.first_ref), channel_id=1, source_target_pairs={{0,16},{2,18},{4,20},{6,22},{8,24},{10,26},{12,28},{14,30},{17,1},... | collective-permute-start | bytes 2359304 | tf_op jit(solution)/shard_map/ppermute | solution.py:505
  220.1 13.4 %collective-permute-start.2 = (bf16[512,768]{1,0:T(8,128)(2,1)}, bf16[512,768]{1,0:T(8,128)(2,1)}, u32[]{:S(2)}, u32[]{:S(2)}) collective-permute-start(bf16[512,768]{1,0:T(8,128)(2,1)} %expert_open.3.mine_ref), channel_id=1, source_target_pairs={{0,16},{1,0},{2,18},{3,2},{4,20},{5,4},{6,22},{7,6},{8,24},{9,8},{... | collective-permute-start | bytes 2359304 | tf_op jit(solution)/shard_map/ppermute | solution.py:500
  224.4 1.1 copy-start.2
  233.6 4.4 %collective-permute-start.5 = (bf16[512,768]{1,0:T(8,128)(2,1)}, bf16[512,768]{1,0:T(8,128)(2,1)S(1)}, u32[]{:S(2)}, u32[]{:S(2)}) collective-permute-start(bf16[512,768]{1,0:T(8,128)(2,1)} %collective-permute-done.2.first_ref), channel_id=1, source_target_pairs={{0,16},{2,18},{4,20},{6,22},{8,24},{10,26},{12,28},{14,30},{17,1},... | collective-permute-start | bytes 2359304 | tf_op jit(solution)/shard_map/ppermute | solution.py:505

commit v6 on v5

--- a/solution.py
+++ b/solution.py
@@ -52,6 +52,29 @@
         compiler_params=params(60),
         name="take_half",
     )(half, down)
+
+
+def stage_kernel(gate_ref, up_ref, gate_out, up_out):
+    gate_out[...] = gate_ref[...]
+    up_out[...] = up_ref[...]
+
+
+def stage(gate, up):
+    width, depth = gate.shape
+    steps = 8
+    spec = pl.BlockSpec((width // steps, depth), lambda r: (r, 0))
+    return pl.pallas_call(
+        stage_kernel,
+        grid=(steps,),
+        in_specs=[spec, spec],
+        out_specs=[spec, spec],
+        out_shape=[
+            jax.ShapeDtypeStruct(gate.shape, bf16),
+            jax.ShapeDtypeStruct(up.shape, bf16),
+        ],
+        compiler_params=params(16),
+        name="stage",
+    )(gate, up)
 
 
 def prepare_kernel(
@@ -292,7 +315,7 @@
             pltpu.VMEM((total, half), f32),
             pltpu.VMEM((total, 128), f32),
         ],
-        compiler_params=params(52),
+        compiler_params=params(26),
         cost_estimate=pl.CostEstimate(
             flops=4 * total * width * half,
             bytes_accessed=4 * width * half + 2 * total * (width + half),
@@ -409,7 +432,7 @@
         out_specs=flat,
         out_shape=jax.ShapeDtypeStruct((rows, width), bf16),
         scratch_shapes=[pltpu.VMEM((2 * rows, experts * SLOTS), bf16)],
-        compiler_params=params(60),
+        compiler_params=params(30),
         name="combine",
     )(back, own, attn, residual, cached)
 
@@ -487,7 +510,10 @@
     attn = attend(pieces, rows)
     sent = pick(attn, pieces, own_gain, experts)
     attn = exchange(attn, "seq")
-    sent, attn, second_down = lax.optimization_barrier((sent, attn, second_down))
+    gate, sent = lax.optimization_barrier((w_gate[0], sent))
+    gate, up = stage(gate, w_up[0])
+    tied = lax.optimization_barrier((sent, attn, second_down, gate, up))
+    sent, attn, second_down, gate, up = tied
     arrived = exchange(sent.reshape(devices, seq_count * SLOTS, cols), ("exp", "seq"))
     arrived = arrived.reshape(exp_count, seq_count, seq_count * SLOTS, cols)
 
@@ -495,7 +521,7 @@
     per = seq_count * SLOTS // parts
     mine, first = [], []
     for part in range(parts):
-        mine.append(expert_open(arrived, part, per, weigh, w_gate[0], w_up[0]))
+        mine.append(expert_open(arrived, part, per, weigh, gate, up))
         arrived, mine[part] = lax.optimization_barrier((arrived, mine[part]))
         first.append(lax.ppermute(mine[part], all_axes, ring))
     first[0], mine[1] = lax.optimization_barrier((first[0], mine[1]))

time: 310 us -> 306 us (0.987)
  local copies, waits for them, and re-layouts: 5.63 us -> 16.5 us
  waiting for transfers between devices: 42 us -> 31.5 us
  Pallas kernels: 73.6 us -> 69.6 us
    ppermute x1, waiting for transfers between devices: 12.2 us -> 0.41 us  [per_device(): second_down = lax.ppermute(second_down, all_axes, cross)]
    unnamed x8 -> x26, local copies, waits for them, and re-layouts: 1.15 us -> 12 us
    pallas_call x2, Pallas kernels: 24 us -> 19.9 us  [expert_open(): pl.pallas_call(open_kernel, grid=(groups // merge,), in_specs=[pl.BlockSp...]
  transfers between devices with their start and end apart: 8 -> 8, of which waited for: 5 -> 5; matrix products, arithmetic and copies ran while one was open for 1% -> 2% of each run, Pallas kernels for 14% -> 14%
where the time goes in v6:
time: 306 us; the launch traced here: 305 us
  blocking collectives  166 us (54%)
  Pallas kernels  69.6 us (23%)
  waiting for transfers between devices  31.5 us (10%)
  starting transfers between devices  21.5 us (7%)
  local copies, waits for them, and re-layouts  16.5 us (5%)
    all_to_all x2, blocking collectives, exchange(): return lax.all_to_all(blocks, axes, split_axis=0, concat_axis=0, tiled=True)  166 us
    ppermute x1, waiting for transfers between devices, per_device(): first_down = lax.ppermute(first_down, all_axes, ring)  23.4 us
    pallas_call x2, Pallas kernels, expert_open(): pl.pallas_call(open_kernel, grid=(groups // merge,), in_specs=[pl.BlockSp...  19.9 us
    pallas_call x2, Pallas kernels, expert_close(): pl.pallas_call(close_kernel, grid_spec=pltpu.PrefetchScalarGridSpec(num_s...  15.5 us
    unnamed x26, local copies, waits for them, and re-layouts  12 us
    all_to_all x2, starting transfers between devices, exchange(): return lax.all_to_all(blocks, axes, split_axis=0, concat_axis=0, tiled=True)  10.8 us
    pallas_call x2, Pallas kernels, take_half(): pl.pallas_call(half_kernel, grid_spec=pltpu.PrefetchScalarGridSpec(num_sc...  8.63 us
    pallas_call x1, Pallas kernels, attend(): pl.pallas_call(attend_kernel, grid=(cols // span,), in_specs=[pl.BlockSpe...  8.12 us
  transfers between devices with their start and end apart: 8, of which 5 were waited for; matrix products, arithmetic and copies ran while one was open for 2% of the time, Pallas kernels for 14%

profile of v6, /device:TPU:1, one launch (start us, length us, event | category | flops | bytes accessed | tf_op | source)
XLA Modules:
  0.0 305.0 jit_solution(11549113011549958295)
XLA Ops:
  0.0 5.1 %prepare.1 = (bf16[8,448,512]{2,1,0:T(8,128)(2,1)}, bf16[3,64,128]{2,1,0:T(8,128)(2,1)}) custom-call(bf16[128,4096]{1,0:T(8,128)(2,1)} %bitcast.37, bf16[128,4096]{1,0:T(8,128)(2,1)} %bitcast.38, bf16[128,4096]{1,0:T(8,128)(2,1)} %bitcast.39, bf16[128,4096]{1,0:T(8,128)(2,1)} %bitcast.28, s32[1,128]{1,0:T(1,128)} %flag_ref.1, s32[8,128]{1,0:T(8,128)} %bitcast.40, ...), custom_call_target="tpu_custom_call" | custom-call | tf_op jit(solution)/shard_map/prepare/pallas_call | solution.py:142
  5.1 5.8 %all-to-all-start = ((bf16[8,448,512]{2,1,0:T(8,128)(2,1)}), bf16[8,448,512]{2,1,0:T(8,128)(2,1)}, u32[]{:S(2)}, u32[]{:S(2)}) async-start(bf16[8,448,512]{2,1,0:T(8,128)(2,1)} %get-tuple-element.27), calls=%async_computation | async-start | bytes 7340032 | tf_op jit(solution)/shard_map/all_to_all | solution.py:441
  10.9 4.3 %take_half.2 = bf16[768,2048]{1,0:T(8,128)(2,1)} custom-call(s32[1]{0:T(128)} %bitcast.11.half_ref, bf16[768,4096]{1,0:T(8,128)(2,1)} %bitcast.31), custom_call_target="tpu_custom_call" | custom-call | tf_op jit(solution)/shard_map/take_half/pallas_call | solution.py:43
  15.2 1.4 collective-permute-start
  16.6 4.3 %take_half.3 = bf16[768,2048]{1,0:T(8,128)(2,1)} custom-call(s32[1]{0:T(128)} %bitcast.13.half_ref, bf16[768,4096]{1,0:T(8,128)(2,1)} %bitcast.32), custom_call_target="tpu_custom_call" | custom-call | tf_op jit(solution)/shard_map/take_half/pallas_call | solution.py:43
  20.9 2.3 collective-permute-start.1
  23.2 0.0 copy-done.12
  23.2 0.1 dynamic-slice.3
  23.3 0.5 dynamic_slice.3.gain_ref
  24.0 1.4 copy.16
  25.3 2.4 pad.4.weigh_ref
  27.8 23.4 %collective-permute-done.first_down = bf16[768,2048]{1,0:T(8,128)(2,1)S(1)} collective-permute-done((bf16[768,2048]{1,0:T(8,128)(2,1)}, bf16[768,2048]{1,0:T(8,128)(2,1)S(1)}, u32[]{:S(2)}, u32[]{:S(2)}) %collective-permute-start) | collective-permute-done | bytes 3145760 | tf_op jit(solution)/shard_map/ppermute | solution.py:491
  51.1 3.1 %all-to-all-done.in_ref.res_ref.table_ref = bf16[8,448,512]{2,1,0:T(8,128)(2,1)} async-done(((bf16[8,448,512]{2,1,0:T(8,128)(2,1)}), bf16[8,448,512]{2,1,0:T(8,128)(2,1)}, u32[]{:S(2)}, u32[]{:S(2)}) %all-to-all-start) | async-done | bytes 3670048 | tf_op jit(solution)/shard_map/all_to_all | solution.py:441
  54.2 8.1 %attend.1.attn_ref = bf16[8,128,512]{2,1,0:T(8,128)(2,1)} custom-call(bf16[8,448,512]{2,1,0:T(8,128)(2,1)} %all-to-all-done.in_ref.res_ref.table_ref), custom_call_target="tpu_custom_call" | custom-call | tf_op jit(solution)/shard_map/attend/pallas_call | solution.py:191
  62.3 5.0 %all-to-all-start.1 = ((bf16[8,128,512]{2,1,0:T(8,128)(2,1)}), bf16[8,128,512]{2,1,0:T(8,128)(2,1)}, u32[]{:S(2)}, u32[]{:S(2)}) async-start(bf16[8,128,512]{2,1,0:T(8,128)(2,1)} %attend.1.attn_ref), calls=%async_computation.1 | async-start | bytes 2097152 | tf_op jit(solution)/shard_map/all_to_all | solution.py:441
  67.3 6.5 %pick.1 = bf16[8,2,8,8,8,512]{5,4,3,2,1,0:T(8,128)(2,1)} custom-call(bf16[8,128,512]{2,1,0:T(8,128)(2,1)} %attend.1.attn_ref, bf16[8,448,512]{2,1,0:T(8,128)(2,1)} %all-to-all-done.in_ref.res_ref.table_ref, bf16[8,448,512]{2,1,0:T(8,128)(2,1)} %all-to-all-done.in_ref.res_ref.table_ref, bf16[1,512]{1,0:T(2,128)(2,1)} %dynamic_slice.3.gain_ref), custom_call_target="tpu_custom_call" | custom-call | tf_op jit(solution)/shard_map/pick/pallas_call | solution.py:233
  73.8 2.8 copy-done
  76.6 2.8 copy-done.1
  79.4 0.9 stage.1
  80.3 0.0 copy-start.8
  80.3 2.7 copy-done.8
  83.0 2.6 copy-done.10
  85.5 0.4 collective-permute-done.1.second_down
  86.0 0.0 all-to-all-done.1.attn_ref
  86.0 108.5 %all_to_all.20 = bf16[128,64,512]{2,1,0:T(8,128)(2,1)S(1)} all-to-all(bf16[128,64,512]{2,1,0:T(8,128)(2,1)} %bitcast.36), channel_id=1, replica_groups=mesh['seq'=8,'exp'=16] {'exp','seq'}, dimensions={0} | all-to-all | bytes 16777216 | tf_op jit(solution)/shard_map/all_to_all | solution.py:441
  194.5 0.0 copy-done.3
  194.5 0.0 copy-done.9
  194.5 0.0 copy-done.11
  194.5 9.5 %expert_open.2.mine_ref = bf16[512,768]{1,0:T(8,128)(2,1)S(1)} custom-call(bf16[16,8,64,512]{3,2,1,0:T(8,128)(2,1)S(1)} %bitcast.24, bf16[4096,128]{1,0:T(8,128)(2,1)S(1)} %copy-done.3, bf16[4096,768]{1,0:T(8,128)(2,1)S(1)} %copy-done.9, bf16[4096,768]{1,0:T(8,128)(2,1)S(1)} %copy-done.11), custom_call_target="tpu_custom_call" | custom-call | flops 6442450944 | bytes 17563648 | tf_op jit(solution)/shard_map/expert_open/pallas_call | solution.py:302
  204.0 0.0 copy-start.5
  204.0 0.3 collective-permute-start.3
  204.3 10.4 %expert_open.3.mine_ref = bf16[512,768]{1,0:T(8,128)(2,1)} custom-call(bf16[16,8,64,512]{3,2,1,0:T(8,128)(2,1)S(1)} %bitcast.25, bf16[4096,128]{1,0:T(8,128)(2,1)S(1)} %copy-done.3, bf16[4096,768]{1,0:T(8,128)(2,1)S(1)} %copy-done.9, bf16[4096,768]{1,0:T(8,128)(2,1)S(1)} %copy-done.11), custom_call_target="tpu_custom_call" | custom-call | flops 6442450944 | bytes 17563648 | tf_op jit(solution)/shard_map/expert_open/pallas_call | solution.py:302
  214.7 0.0 copy-done.5
  214.7 0.0 collective-permute-done.3.first_ref
  214.7 1.3 collective-permute-start.4
  216.0 4.1 %collective-permute-start.2 = (bf16[512,768]{1,0:T(8,128)(2,1)}, bf16[512,768]{1,0:T(8,128)(2,1)}, u32[]{:S(2)}, u32[]{:S(2)}) collective-permute-start(bf16[512,768]{1,0:T(8,128)(2,1)} %expert_open.3.mine_ref), channel_id=1, source_target_pairs={{0,16},{1,0},{2,18},{3,2},{4,20},{5,4},{6,22},{7,6},{8,24},{9,8},{... | collective-permute-start | bytes 2359304 | tf_op jit(solution)/shard_map/ppermute | solution.py:526
  220.1 0.1 pad_add_fusion.role_ref
  220.2 0.5 collective-permute-done.4.second_ref
  220.7 1.1 copy-done.6
  221.8 7.8 %expert_close.2.rest_0_ = bf16[16,8,8,2048]{3,2,1,0:T(8,128)(2,1)} custom-call(s32[2]{0:T(128)S(1)} %pad_add_fusion.role_ref, bf16[512,768]{1,0:T(8,128)(2,1)} %collective-permute-done.3.first_ref, bf16[512,768]{1,0:T(8,128)(2,1)S(1)} %copy-done.6, bf16[512,768]{1,0:T(8,128)(2,1)} %collective-permute-done.4.second_ref, ...), custom_call_target="tpu_custom_call" | custom-call | flops 3221225472 | bytes 9961472 | tf_op jit(solution)/shard_map/expert_close/pallas_call | solution.py:357
  229.6 0.0 collective-permute-done.2.first_ref
  229.6 1.3 collective-permute-start.5
  230.9 4.2 %collective-permute-done.5.second_ref = bf16[512,768]{1,0:T(8,128)(2,1)S(1)} collective-permute-done((bf16[512,768]{1,0:T(8,128)(2,1)}, bf16[512,768]{1,0:T(8,128)(2,1)S(1)}, u32[]{:S(2)}, u32[]{:S(2)}) %collective-permute-start.5) | collective-permute-done | bytes 786464 | tf_op jit(solution)/shard_map/ppermute | solution.py:531
  235.0 7.8 %expert_close.3 = bf16[16,8,8,2048]{3,2,1,0:T(8,128)(2,1)} custom-call(s32[2]{0:T(128)S(1)} %pad_add_fusion.role_ref, bf16[512,768]{1,0:T(8,128)(2,1)} %collective-permute-done.2.first_ref, bf16[512,768]{1,0:T(8,128)(2,1)} %expert_open.3.mine_ref, bf16[512,768]{1,0:T(8,128)(2,1)S(1)} %collective-permute-done.5.second_ref, ...), custom_call_target="tpu_custom_call", output_to_operand_aliasing={{}: (7, {})} | custom-call | flops 3221225472 | bytes 9961472 | tf_op jit(solution)/shard_map/expert_close/pallas_call | solution.py:357
  242.8 57.1 %all_to_all.21 = bf16[128,8,2048]{2,1,0:T(8,128)(2,1)S(1)} all-to-all(bf16[128,8,2048]{2,1,0:T(8,128)(2,1)} %bitcast.35), channel_id=1, replica_groups=mesh['seq'=8,'exp'=16] {'exp','seq'}, dimensions={0} | all-to-all | bytes 8388608 | tf_op jit(solution)/shard_map/all_to_all | solution.py:441
  300.0 0.0 copy-done.2
  300.0 0.0 copy-done.4
  300.0 5.0 %combine.1 = bf16[128,4096]{1,0:T(8,128)(2,1)} custom-call(bf16[16,4,2,8,2048]{4,3,2,1,0:T(8,128)(2,1)S(1)} %bitcast.23, bf16[3,64,128]{2,1,0:T(8,128)(2,1)S(1)} %copy-done.7, bf16[8,128,512]{2,1,0:T(8,128)(2,1)} %all-to-all-done.1.attn_ref, bf16[128,4096]{1,0:T(8,128)(2,1)S(1)} %bitcast.29, bf16[128,4096]{1,0:T(8,128)(2,1)S(1)} %bitcast.30), custom_call_target="tpu_custom_call" | custom-call | tf_op jit(solution)/shard_map/combine/pallas_call | solution.py:420
  (16 shorter events, 0.1 us)
Async XLA Ops:
  5.1 49.1 %all-to-all-start = ((bf16[8,448,512]{2,1,0:T(8,128)(2,1)}), bf16[8,448,512]{2,1,0:T(8,128)(2,1)}, u32[]{:S(2)}, u32[]{:S(2)}) async-start(bf16[8,448,512]{2,1,0:T(8,128)(2,1)} %get-tuple-element.27), calls=%async_computation | async-start | bytes 7340032 | tf_op jit(solution)/shard_map/all_to_all | solution.py:441
  15.2 35.9 %collective-permute-start = (bf16[768,2048]{1,0:T(8,128)(2,1)}, bf16[768,2048]{1,0:T(8,128)(2,1)S(1)}, u32[]{:S(2)}, u32[]{:S(2)}) collective-permute-start(bf16[768,2048]{1,0:T(8,128)(2,1)} %take_half.2), channel_id=1, source_target_pairs={{0,16},{1,0},{2,18},{3,2},{4,20},{5,4},{6,22},{7,6},{8,24},{9,8},{... | collective-permute-start | bytes 9437192 | tf_op jit(solution)/shard_map/ppermute | solution.py:491
  16.6 6.6 %copy-start.12 = (bf16[4096]{0:T(1024)(128)(2,1)S(1)}, bf16[4096]{0:T(1024)(128)(2,1)}, u32[]{:S(2)}) copy-start(bf16[4096]{0:T(1024)(128)(2,1)} %param.17) | copy-start | bytes 24580
  20.9 65.0 %collective-permute-start.1 = (bf16[768,2048]{1,0:T(8,128)(2,1)}, bf16[768,2048]{1,0:T(8,128)(2,1)}, u32[]{:S(2)}, u32[]{:S(2)}) collective-permute-start(bf16[768,2048]{1,0:T(8,128)(2,1)} %take_half.3), channel_id=1, source_target_pairs={{1,16},{3,18},{5,20},{7,22},{9,24},{11,26},{13,28},{15,30},{16,1},... | collective-permute-start | bytes 9437192 | tf_op jit(solution)/shard_map/ppermute | solution.py:493
  62.3 23.6 %all-to-all-start.1 = ((bf16[8,128,512]{2,1,0:T(8,128)(2,1)}), bf16[8,128,512]{2,1,0:T(8,128)(2,1)}, u32[]{:S(2)}, u32[]{:S(2)}) async-start(bf16[8,128,512]{2,1,0:T(8,128)(2,1)} %attend.1.attn_ref), calls=%async_computation.1 | async-start | bytes 2097152 | tf_op jit(solution)/shard_map/all_to_all | solution.py:441
  73.8 2.8 copy-start
  76.6 2.8 copy-start.1
  80.3 2.7 copy-start.8
  83.0 2.6 copy-start.10
  86.0 108.5 %copy-start.3 = (bf16[4096,128]{1,0:T(8,128)(2,1)S(1)}, bf16[4096,128]{1,0:T(8,128)(2,1)}, u32[]{:S(2)}) copy-start(bf16[4096,128]{1,0:T(8,128)(2,1)} %pad.4.weigh_ref) | copy-start | bytes 3145732
  86.0 108.5 %copy-start.9 = (bf16[4096,768]{1,0:T(8,128)(2,1)S(1)}, bf16[4096,768]{1,0:T(8,128)(2,1)}, u32[]{:S(2)}) copy-start(bf16[4096,768]{1,0:T(8,128)(2,1)} %copy-done.8) | copy-start | bytes 18874372
  86.0 108.5 %copy-start.11 = (bf16[4096,768]{1,0:T(8,128)(2,1)S(1)}, bf16[4096,768]{1,0:T(8,128)(2,1)}, u32[]{:S(2)}) copy-start(bf16[4096,768]{1,0:T(8,128)(2,1)} %copy-done.10) | copy-start | bytes 18874372
  204.0 10.7 %copy-start.5 = (bf16[512,768]{1,0:T(8,128)(2,1)}, bf16[512,768]{1,0:T(8,128)(2,1)S(1)}, u32[]{:S(2)}) copy-start(bf16[512,768]{1,0:T(8,128)(2,1)S(1)} %expert_open.2.mine_ref) | copy-start | bytes 2359300
  204.0 10.7 %collective-permute-start.3 = (bf16[512,768]{1,0:T(8,128)(2,1)S(1)}, bf16[512,768]{1,0:T(8,128)(2,1)}, u32[]{:S(2)}, u32[]{:S(2)}) collective-permute-start(bf16[512,768]{1,0:T(8,128)(2,1)S(1)} %expert_open.2.mine_ref), channel_id=1, source_target_pairs={{0,16},{1,0},{2,18},{3,2},{4,20},{5,4},{6,22},{7,6},{8,24},{9,8},{... | collective-permute-start | bytes 2359304 | tf_op jit(solution)/shard_map/ppermute | solution.py:526
  214.7 6.0 %collective-permute-start.4 = (bf16[512,768]{1,0:T(8,128)(2,1)}, bf16[512,768]{1,0:T(8,128)(2,1)}, u32[]{:S(2)}, u32[]{:S(2)}) collective-permute-start(bf16[512,768]{1,0:T(8,128)(2,1)} %collective-permute-done.3.first_ref), channel_id=1, source_target_pairs={{0,16},{2,18},{4,20},{6,22},{8,24},{10,26},{12,28},{14,30},{17,1},... | collective-permute-start | bytes 2359304 | tf_op jit(solution)/shard_map/ppermute | solution.py:531
  216.0 13.6 %collective-permute-start.2 = (bf16[512,768]{1,0:T(8,128)(2,1)}, bf16[512,768]{1,0:T(8,128)(2,1)}, u32[]{:S(2)}, u32[]{:S(2)}) collective-permute-start(bf16[512,768]{1,0:T(8,128)(2,1)} %expert_open.3.mine_ref), channel_id=1, source_target_pairs={{0,16},{1,0},{2,18},{3,2},{4,20},{5,4},{6,22},{7,6},{8,24},{9,8},{... | collective-permute-start | bytes 2359304 | tf_op jit(solution)/shard_map/ppermute | solution.py:526
  220.7 1.1 copy-start.6
  229.6 5.4 %collective-permute-start.5 = (bf16[512,768]{1,0:T(8,128)(2,1)}, bf16[512,768]{1,0:T(8,128)(2,1)S(1)}, u32[]{:S(2)}, u32[]{:S(2)}) collective-permute-start(bf16[512,768]{1,0:T(8,128)(2,1)} %collective-permute-done.2.first_ref), channel_id=1, source_target_pairs={{0,16},{2,18},{4,20},{6,22},{8,24},{10,26},{12,28},{14,30},{17,1},... | collective-permute-start | bytes 2359304 | tf_op jit(solution)/shard_map/ppermute | solution.py:531
  242.8 57.1 %copy-start.2 = (bf16[1,128,4096]{2,1,0:T(8,128)(2,1)S(1)}, bf16[1,128,4096]{2,1,0:T(8,128)(2,1)}, u32[]{:S(2)}) copy-start(bf16[1,128,4096]{2,1,0:T(8,128)(2,1)} %param.15) | copy-start | bytes 3145732
  242.8 57.1 %copy-start.4 = (bf16[1,128,4096]{2,1,0:T(8,128)(2,1)S(1)}, bf16[1,128,4096]{2,1,0:T(8,128)(2,1)}, u32[]{:S(2)}) copy-start(bf16[1,128,4096]{2,1,0:T(8,128)(2,1)} %param.16) | copy-start | bytes 3145732
  242.8 57.1 %copy-start.7 = (bf16[3,64,128]{2,1,0:T(8,128)(2,1)S(1)}, bf16[3,64,128]{2,1,0:T(8,128)(2,1)}, u32[]{:S(2)}) copy-start(bf16[3,64,128]{2,1,0:T(8,128)(2,1)} %get-tuple-element.47.own_ref) | copy-start | bytes 147460

commit v7 on v6

--- a/solution.py
+++ b/solution.py
@@ -345,7 +345,7 @@
 def expert_close(role, acts, downs, part, groups, count, done):
     total, half = acts[0].shape
     width = downs[0].shape[1]
-    span = 512
+    span = 1024
     steps = width // span
     merge = total // (count * SLOTS)
     act = pl.BlockSpec((total, half), lambda c, role: (0, 0))
@@ -409,7 +409,7 @@
         out_ref[:, here] = (hid + moe[:, here]).astype(bf16)
 
 
-def combine(back, own, attn, residual, cached, span=1024):
+def combine(back, own, attn, residual, cached, span=2048):
     count, chips, cores, _, half = back.shape
     groups, rows, piece = attn.shape
     width = groups * piece

time: 306 us -> 305 us (level)
  no operation moved by 1% of the time
where the time goes in v7:
time: 305 us; the launch traced here: 304 us
  blocking collectives  166 us (54%)
  Pallas kernels  68.6 us (22%)
  waiting for transfers between devices  31.6 us (10%)
  starting transfers between devices  21.5 us (7%)
  local copies, waits for them, and re-layouts  16.5 us (5%)
    all_to_all x2, blocking collectives, exchange(): return lax.all_to_all(blocks, axes, split_axis=0, concat_axis=0, tiled=True)  166 us
    ppermute x1, waiting for transfers between devices, per_device(): first_down = lax.ppermute(first_down, all_axes, ring)  23.4 us
    pallas_call x2, Pallas kernels, expert_open(): pl.pallas_call(open_kernel, grid=(groups // merge,), in_specs=[pl.BlockSp...  19.9 us
    pallas_call x2, Pallas kernels, expert_close(): pl.pallas_call(close_kernel, grid_spec=pltpu.PrefetchScalarGridSpec(num_s...  15.4 us
    unnamed x26, local copies, waits for them, and re-layouts  12 us
    all_to_all x2, starting transfers between devices, exchange(): return lax.all_to_all(blocks, axes, split_axis=0, concat_axis=0, tiled=True)  10.8 us
    pallas_call x2, Pallas kernels, take_half(): pl.pallas_call(half_kernel, grid_spec=pltpu.PrefetchScalarGridSpec(num_sc...  8.63 us
    pallas_call x1, Pallas kernels, attend(): pl.pallas_call(attend_kernel, grid=(cols // span,), in_specs=[pl.BlockSpe...  8.12 us
  transfers between devices with their start and end apart: 8, of which 5 were waited for; matrix products, arithmetic and copies ran while one was open for 2% of the time, Pallas kernels for 14%

profile of v7, /device:TPU:1, one launch (start us, length us, event | category | flops | bytes accessed | tf_op | source)
XLA Modules:
  0.0 304.1 jit_solution(4964985239627263022)
XLA Ops:
  0.0 5.1 %prepare.1 = (bf16[8,448,512]{2,1,0:T(8,128)(2,1)}, bf16[3,64,128]{2,1,0:T(8,128)(2,1)}) custom-call(bf16[128,4096]{1,0:T(8,128)(2,1)} %bitcast.37, bf16[128,4096]{1,0:T(8,128)(2,1)} %bitcast.38, bf16[128,4096]{1,0:T(8,128)(2,1)} %bitcast.39, bf16[128,4096]{1,0:T(8,128)(2,1)} %bitcast.28, s32[1,128]{1,0:T(1,128)} %flag_ref.1, s32[8,128]{1,0:T(8,128)} %bitcast.40, ...), custom_call_target="tpu_custom_call" | custom-call | tf_op jit(solution)/shard_map/prepare/pallas_call | solution.py:142
  5.1 5.8 %all-to-all-start = ((bf16[8,448,512]{2,1,0:T(8,128)(2,1)}), bf16[8,448,512]{2,1,0:T(8,128)(2,1)}, u32[]{:S(2)}, u32[]{:S(2)}) async-start(bf16[8,448,512]{2,1,0:T(8,128)(2,1)} %get-tuple-element.27), calls=%async_computation | async-start | bytes 7340032 | tf_op jit(solution)/shard_map/all_to_all | solution.py:441
  10.9 4.3 %take_half.2 = bf16[768,2048]{1,0:T(8,128)(2,1)} custom-call(s32[1]{0:T(128)} %bitcast.11.half_ref, bf16[768,4096]{1,0:T(8,128)(2,1)} %bitcast.31), custom_call_target="tpu_custom_call" | custom-call | tf_op jit(solution)/shard_map/take_half/pallas_call | solution.py:43
  15.2 1.4 collective-permute-start
  16.6 4.3 %take_half.3 = bf16[768,2048]{1,0:T(8,128)(2,1)} custom-call(s32[1]{0:T(128)} %bitcast.13.half_ref, bf16[768,4096]{1,0:T(8,128)(2,1)} %bitcast.32), custom_call_target="tpu_custom_call" | custom-call | tf_op jit(solution)/shard_map/take_half/pallas_call | solution.py:43
  20.9 2.3 collective-permute-start.1
  23.2 0.0 copy-done.12
  23.2 0.1 dynamic-slice.3
  23.3 0.5 dynamic_slice.3.gain_ref
  24.0 1.4 copy.16
  25.3 2.4 pad.4.weigh_ref
  27.8 23.4 %collective-permute-done.first_down = bf16[768,2048]{1,0:T(8,128)(2,1)S(1)} collective-permute-done((bf16[768,2048]{1,0:T(8,128)(2,1)}, bf16[768,2048]{1,0:T(8,128)(2,1)S(1)}, u32[]{:S(2)}, u32[]{:S(2)}) %collective-permute-start) | collective-permute-done | bytes 3145760 | tf_op jit(solution)/shard_map/ppermute | solution.py:491
  51.1 3.1 %all-to-all-done.in_ref.res_ref.table_ref = bf16[8,448,512]{2,1,0:T(8,128)(2,1)} async-done(((bf16[8,448,512]{2,1,0:T(8,128)(2,1)}), bf16[8,448,512]{2,1,0:T(8,128)(2,1)}, u32[]{:S(2)}, u32[]{:S(2)}) %all-to-all-start) | async-done | bytes 3670048 | tf_op jit(solution)/shard_map/all_to_all | solution.py:441
  54.2 8.1 %attend.1.attn_ref = bf16[8,128,512]{2,1,0:T(8,128)(2,1)} custom-call(bf16[8,448,512]{2,1,0:T(8,128)(2,1)} %all-to-all-done.in_ref.res_ref.table_ref), custom_call_target="tpu_custom_call" | custom-call | tf_op jit(solution)/shard_map/attend/pallas_call | solution.py:191
  62.3 5.0 %all-to-all-start.1 = ((bf16[8,128,512]{2,1,0:T(8,128)(2,1)}), bf16[8,128,512]{2,1,0:T(8,128)(2,1)}, u32[]{:S(2)}, u32[]{:S(2)}) async-start(bf16[8,128,512]{2,1,0:T(8,128)(2,1)} %attend.1.attn_ref), calls=%async_computation.1 | async-start | bytes 2097152 | tf_op jit(solution)/shard_map/all_to_all | solution.py:441
  67.3 6.5 %pick.1 = bf16[8,2,8,8,8,512]{5,4,3,2,1,0:T(8,128)(2,1)} custom-call(bf16[8,128,512]{2,1,0:T(8,128)(2,1)} %attend.1.attn_ref, bf16[8,448,512]{2,1,0:T(8,128)(2,1)} %all-to-all-done.in_ref.res_ref.table_ref, bf16[8,448,512]{2,1,0:T(8,128)(2,1)} %all-to-all-done.in_ref.res_ref.table_ref, bf16[1,512]{1,0:T(2,128)(2,1)} %dynamic_slice.3.gain_ref), custom_call_target="tpu_custom_call" | custom-call | tf_op jit(solution)/shard_map/pick/pallas_call | solution.py:233
  73.8 2.8 copy-done
  76.6 2.8 copy-done.1
  79.4 0.9 stage.1
  80.3 0.0 copy-start.8
  80.3 2.7 copy-done.8
  83.0 2.6 copy-done.10
  85.5 0.4 collective-permute-done.1.second_down
  86.0 0.0 all-to-all-done.1.attn_ref
  86.0 108.5 %all_to_all.20 = bf16[128,64,512]{2,1,0:T(8,128)(2,1)S(1)} all-to-all(bf16[128,64,512]{2,1,0:T(8,128)(2,1)} %bitcast.36), channel_id=1, replica_groups=mesh['seq'=8,'exp'=16] {'exp','seq'}, dimensions={0} | all-to-all | bytes 16777216 | tf_op jit(solution)/shard_map/all_to_all | solution.py:441
  194.5 0.0 copy-done.3
  194.5 0.0 copy-done.9
  194.5 0.0 copy-done.11
  194.5 9.5 %expert_open.2.mine_ref = bf16[512,768]{1,0:T(8,128)(2,1)S(1)} custom-call(bf16[16,8,64,512]{3,2,1,0:T(8,128)(2,1)S(1)} %bitcast.24, bf16[4096,128]{1,0:T(8,128)(2,1)S(1)} %copy-done.3, bf16[4096,768]{1,0:T(8,128)(2,1)S(1)} %copy-done.9, bf16[4096,768]{1,0:T(8,128)(2,1)S(1)} %copy-done.11), custom_call_target="tpu_custom_call" | custom-call | flops 6442450944 | bytes 17563648 | tf_op jit(solution)/shard_map/expert_open/pallas_call | solution.py:302
  204.0 0.0 copy-start.5
  204.0 0.3 collective-permute-start.3
  204.3 10.4 %expert_open.3.mine_ref = bf16[512,768]{1,0:T(8,128)(2,1)} custom-call(bf16[16,8,64,512]{3,2,1,0:T(8,128)(2,1)S(1)} %bitcast.25, bf16[4096,128]{1,0:T(8,128)(2,1)S(1)} %copy-done.3, bf16[4096,768]{1,0:T(8,128)(2,1)S(1)} %copy-done.9, bf16[4096,768]{1,0:T(8,128)(2,1)S(1)} %copy-done.11), custom_call_target="tpu_custom_call" | custom-call | flops 6442450944 | bytes 17563648 | tf_op jit(solution)/shard_map/expert_open/pallas_call | solution.py:302
  214.7 0.0 copy-done.5
  214.7 0.0 collective-permute-done.3.first_ref
  214.7 1.3 collective-permute-start.4
  216.0 4.1 %collective-permute-start.2 = (bf16[512,768]{1,0:T(8,128)(2,1)}, bf16[512,768]{1,0:T(8,128)(2,1)}, u32[]{:S(2)}, u32[]{:S(2)}) collective-permute-start(bf16[512,768]{1,0:T(8,128)(2,1)} %expert_open.3.mine_ref), channel_id=1, source_target_pairs={{0,16},{1,0},{2,18},{3,2},{4,20},{5,4},{6,22},{7,6},{8,24},{9,8},{... | collective-permute-start | bytes 2359304 | tf_op jit(solution)/shard_map/ppermute | solution.py:526
  220.1 0.1 pad_add_fusion.role_ref
  220.2 0.5 collective-permute-done.4.second_ref
  220.7 1.1 copy-done.6
  221.8 7.6 %expert_close.2.rest_0_ = bf16[16,8,8,2048]{3,2,1,0:T(8,128)(2,1)} custom-call(s32[2]{0:T(128)S(1)} %pad_add_fusion.role_ref, bf16[512,768]{1,0:T(8,128)(2,1)} %collective-permute-done.3.first_ref, bf16[512,768]{1,0:T(8,128)(2,1)S(1)} %copy-done.6, bf16[512,768]{1,0:T(8,128)(2,1)} %collective-permute-done.4.second_ref, ...), custom_call_target="tpu_custom_call" | custom-call | flops 3221225472 | bytes 9961472 | tf_op jit(solution)/shard_map/expert_close/pallas_call | solution.py:357
  229.5 0.0 collective-permute-done.2.first_ref
  229.5 1.3 collective-permute-start.5
  230.8 4.3 %collective-permute-done.5.second_ref = bf16[512,768]{1,0:T(8,128)(2,1)S(1)} collective-permute-done((bf16[512,768]{1,0:T(8,128)(2,1)}, bf16[512,768]{1,0:T(8,128)(2,1)S(1)}, u32[]{:S(2)}, u32[]{:S(2)}) %collective-permute-start.5) | collective-permute-done | bytes 786464 | tf_op jit(solution)/shard_map/ppermute | solution.py:531
  235.0 7.7 %expert_close.3 = bf16[16,8,8,2048]{3,2,1,0:T(8,128)(2,1)} custom-call(s32[2]{0:T(128)S(1)} %pad_add_fusion.role_ref, bf16[512,768]{1,0:T(8,128)(2,1)} %collective-permute-done.2.first_ref, bf16[512,768]{1,0:T(8,128)(2,1)} %expert_open.3.mine_ref, bf16[512,768]{1,0:T(8,128)(2,1)S(1)} %collective-permute-done.5.second_ref, ...), custom_call_target="tpu_custom_call", output_to_operand_aliasing={{}: (7, {})} | custom-call | flops 3221225472 | bytes 9961472 | tf_op jit(solution)/shard_map/expert_close/pallas_call | solution.py:357
  242.8 57.1 %all_to_all.21 = bf16[128,8,2048]{2,1,0:T(8,128)(2,1)S(1)} all-to-all(bf16[128,8,2048]{2,1,0:T(8,128)(2,1)} %bitcast.35), channel_id=1, replica_groups=mesh['seq'=8,'exp'=16] {'exp','seq'}, dimensions={0} | all-to-all | bytes 8388608 | tf_op jit(solution)/shard_map/all_to_all | solution.py:441
  299.9 0.0 copy-done.2
  299.9 0.0 copy-done.4
  299.9 4.2 %combine.1 = bf16[128,4096]{1,0:T(8,128)(2,1)} custom-call(bf16[16,4,2,8,2048]{4,3,2,1,0:T(8,128)(2,1)S(1)} %bitcast.23, bf16[3,64,128]{2,1,0:T(8,128)(2,1)S(1)} %copy-done.7, bf16[8,128,512]{2,1,0:T(8,128)(2,1)} %all-to-all-done.1.attn_ref, bf16[128,4096]{1,0:T(8,128)(2,1)S(1)} %bitcast.29, bf16[128,4096]{1,0:T(8,128)(2,1)S(1)} %bitcast.30), custom_call_target="tpu_custom_call" | custom-call | tf_op jit(solution)/shard_map/combine/pallas_call | solution.py:420
  (16 shorter events, 0.1 us)
Async XLA Ops:
  5.1 49.1 %all-to-all-start = ((bf16[8,448,512]{2,1,0:T(8,128)(2,1)}), bf16[8,448,512]{2,1,0:T(8,128)(2,1)}, u32[]{:S(2)}, u32[]{:S(2)}) async-start(bf16[8,448,512]{2,1,0:T(8,128)(2,1)} %get-tuple-element.27), calls=%async_computation | async-start | bytes 7340032 | tf_op jit(solution)/shard_map/all_to_all | solution.py:441
  15.2 35.9 %collective-permute-start = (bf16[768,2048]{1,0:T(8,128)(2,1)}, bf16[768,2048]{1,0:T(8,128)(2,1)S(1)}, u32[]{:S(2)}, u32[]{:S(2)}) collective-permute-start(bf16[768,2048]{1,0:T(8,128)(2,1)} %take_half.2), channel_id=1, source_target_pairs={{0,16},{1,0},{2,18},{3,2},{4,20},{5,4},{6,22},{7,6},{8,24},{9,8},{... | collective-permute-start | bytes 9437192 | tf_op jit(solution)/shard_map/ppermute | solution.py:491
  16.6 6.6 %copy-start.12 = (bf16[4096]{0:T(1024)(128)(2,1)S(1)}, bf16[4096]{0:T(1024)(128)(2,1)}, u32[]{:S(2)}) copy-start(bf16[4096]{0:T(1024)(128)(2,1)} %param.17) | copy-start | bytes 24580
  20.9 65.0 %collective-permute-start.1 = (bf16[768,2048]{1,0:T(8,128)(2,1)}, bf16[768,2048]{1,0:T(8,128)(2,1)}, u32[]{:S(2)}, u32[]{:S(2)}) collective-permute-start(bf16[768,2048]{1,0:T(8,128)(2,1)} %take_half.3), channel_id=1, source_target_pairs={{1,16},{3,18},{5,20},{7,22},{9,24},{11,26},{13,28},{15,30},{16,1},... | collective-permute-start | bytes 9437192 | tf_op jit(solution)/shard_map/ppermute | solution.py:493
  62.3 23.6 %all-to-all-start.1 = ((bf16[8,128,512]{2,1,0:T(8,128)(2,1)}), bf16[8,128,512]{2,1,0:T(8,128)(2,1)}, u32[]{:S(2)}, u32[]{:S(2)}) async-start(bf16[8,128,512]{2,1,0:T(8,128)(2,1)} %attend.1.attn_ref), calls=%async_computation.1 | async-start | bytes 2097152 | tf_op jit(solution)/shard_map/all_to_all | solution.py:441
  73.8 2.8 copy-start
  76.6 2.8 copy-start.1
  80.3 2.7 copy-start.8
  83.0 2.6 copy-start.10
  86.0 108.5 %copy-start.3 = (bf16[4096,128]{1,0:T(8,128)(2,1)S(1)}, bf16[4096,128]{1,0:T(8,128)(2,1)}, u32[]{:S(2)}) copy-start(bf16[4096,128]{1,0:T(8,128)(2,1)} %pad.4.weigh_ref) | copy-start | bytes 3145732
  86.0 108.5 %copy-start.9 = (bf16[4096,768]{1,0:T(8,128)(2,1)S(1)}, bf16[4096,768]{1,0:T(8,128)(2,1)}, u32[]{:S(2)}) copy-start(bf16[4096,768]{1,0:T(8,128)(2,1)} %copy-done.8) | copy-start | bytes 18874372
  86.0 108.5 %copy-start.11 = (bf16[4096,768]{1,0:T(8,128)(2,1)S(1)}, bf16[4096,768]{1,0:T(8,128)(2,1)}, u32[]{:S(2)}) copy-start(bf16[4096,768]{1,0:T(8,128)(2,1)} %copy-done.10) | copy-start | bytes 18874372
  204.0 10.7 %copy-start.5 = (bf16[512,768]{1,0:T(8,128)(2,1)}, bf16[512,768]{1,0:T(8,128)(2,1)S(1)}, u32[]{:S(2)}) copy-start(bf16[512,768]{1,0:T(8,128)(2,1)S(1)} %expert_open.2.mine_ref) | copy-start | bytes 2359300
  204.0 10.7 %collective-permute-start.3 = (bf16[512,768]{1,0:T(8,128)(2,1)S(1)}, bf16[512,768]{1,0:T(8,128)(2,1)}, u32[]{:S(2)}, u32[]{:S(2)}) collective-permute-start(bf16[512,768]{1,0:T(8,128)(2,1)S(1)} %expert_open.2.mine_ref), channel_id=1, source_target_pairs={{0,16},{1,0},{2,18},{3,2},{4,20},{5,4},{6,22},{7,6},{8,24},{9,8},{... | collective-permute-start | bytes 2359304 | tf_op jit(solution)/shard_map/ppermute | solution.py:526
  214.7 6.0 %collective-permute-start.4 = (bf16[512,768]{1,0:T(8,128)(2,1)}, bf16[512,768]{1,0:T(8,128)(2,1)}, u32[]{:S(2)}, u32[]{:S(2)}) collective-permute-start(bf16[512,768]{1,0:T(8,128)(2,1)} %collective-permute-done.3.first_ref), channel_id=1, source_target_pairs={{0,16},{2,18},{4,20},{6,22},{8,24},{10,26},{12,28},{14,30},{17,1},... | collective-permute-start | bytes 2359304 | tf_op jit(solution)/shard_map/ppermute | solution.py:531
  216.0 13.5 %collective-permute-start.2 = (bf16[512,768]{1,0:T(8,128)(2,1)}, bf16[512,768]{1,0:T(8,128)(2,1)}, u32[]{:S(2)}, u32[]{:S(2)}) collective-permute-start(bf16[512,768]{1,0:T(8,128)(2,1)} %expert_open.3.mine_ref), channel_id=1, source_target_pairs={{0,16},{1,0},{2,18},{3,2},{4,20},{5,4},{6,22},{7,6},{8,24},{9,8},{... | collective-permute-start | bytes 2359304 | tf_op jit(solution)/shard_map/ppermute | solution.py:526
  220.7 1.1 copy-start.6
  229.5 5.6 %collective-permute-start.5 = (bf16[512,768]{1,0:T(8,128)(2,1)}, bf16[512,768]{1,0:T(8,128)(2,1)S(1)}, u32[]{:S(2)}, u32[]{:S(2)}) collective-permute-start(bf16[512,768]{1,0:T(8,128)(2,1)} %collective-permute-done.2.first_ref), channel_id=1, source_target_pairs={{0,16},{2,18},{4,20},{6,22},{8,24},{10,26},{12,28},{14,30},{17,1},... | collective-permute-start | bytes 2359304 | tf_op jit(solution)/shard_map/ppermute | solution.py:531
  242.8 57.1 %copy-start.2 = (bf16[1,128,4096]{2,1,0:T(8,128)(2,1)S(1)}, bf16[1,128,4096]{2,1,0:T(8,128)(2,1)}, u32[]{:S(2)}) copy-start(bf16[1,128,4096]{2,1,0:T(8,128)(2,1)} %param.15) | copy-start | bytes 3145732
  242.8 57.1 %copy-start.4 = (bf16[1,128,4096]{2,1,0:T(8,128)(2,1)S(1)}, bf16[1,128,4096]{2,1,0:T(8,128)(2,1)}, u32[]{:S(2)}) copy-start(bf16[1,128,4096]{2,1,0:T(8,128)(2,1)} %param.16) | copy-start | bytes 3145732
  242.8 57.1 %copy-start.7 = (bf16[3,64,128]{2,1,0:T(8,128)(2,1)S(1)}, bf16[3,64,128]{2,1,0:T(8,128)(2,1)}, u32[]{:S(2)}) copy-start(bf16[3,64,128]{2,1,0:T(8,128)(2,1)} %get-tuple-element.47.own_ref) | copy-start | bytes 147460

commit v8 on v7

--- a/solution.py
+++ b/solution.py
@@ -38,7 +38,7 @@
 
 def take_half(half, down):
     depth, width = down.shape
-    steps = 4
+    steps = 2
     span = width // 2 // steps
     return pl.pallas_call(
         half_kernel,
@@ -137,7 +137,7 @@
     rows, width = q.shape
     cols = width // groups
     total = 3 * rows + most + 16
-    merge = 2
+    merge = 4
     piece = pl.BlockSpec((rows, merge * cols), lambda j: (0, j))
     return pl.pallas_call(
         prepare_kernel,

time: 305 us -> 303 us (level)
  Pallas kernels: 68.6 us -> 65.3 us
  transfers between devices with their start and end apart: 8 -> 8, of which waited for: 5 -> 4; matrix products, arithmetic and copies ran while one was open for 2% -> 2% of each run, Pallas kernels for 14% -> 13%
where the time goes in v8:
time: 303 us
  blocking collectives  166 us (55%)
  Pallas kernels  65.3 us (22%)
  waiting for transfers between devices  33.3 us (11%)
  starting transfers between devices  21.5 us (7%)
  local copies, waits for them, and re-layouts  16.5 us (5%)
    all_to_all x2, blocking collectives, exchange(): return lax.all_to_all(blocks, axes, split_axis=0, concat_axis=0, tiled=True)  166 us
    ppermute x1, waiting for transfers between devices, per_device(): first_down = lax.ppermute(first_down, all_axes, ring)  24.4 us
    pallas_call x2, Pallas kernels, expert_open(): pl.pallas_call(open_kernel, grid=(groups // merge,), in_specs=[pl.BlockSp...  19.9 us
    pallas_call x2, Pallas kernels, expert_close(): pl.pallas_call(close_kernel, grid_spec=pltpu.PrefetchScalarGridSpec(num_s...  15.4 us
    unnamed x26, local copies, waits for them, and re-layouts  12 us
    all_to_all x2, starting transfers between devices, exchange(): return lax.all_to_all(blocks, axes, split_axis=0, concat_axis=0, tiled=True)  10.8 us
    pallas_call x1, Pallas kernels, attend(): pl.pallas_call(attend_kernel, grid=(cols // span,), in_specs=[pl.BlockSpe...  8.12 us
    pallas_call x2, Pallas kernels, take_half(): pl.pallas_call(half_kernel, grid_spec=pltpu.PrefetchScalarGridSpec(num_sc...  6.5 us
  transfers between devices with their start and end apart: 8, of which 4 were waited for; matrix products, arithmetic and copies ran while one was open for 2% of the time, Pallas kernels for 13%

profile of v8, /device:TPU:1, one launch (start us, length us, event | category | flops | bytes accessed | tf_op | source)
XLA Modules:
  0.0 302.5 jit_solution(3737331382879860912)
XLA Ops:
  0.0 3.9 %prepare.1 = (bf16[8,448,512]{2,1,0:T(8,128)(2,1)}, bf16[3,64,128]{2,1,0:T(8,128)(2,1)}) custom-call(bf16[128,4096]{1,0:T(8,128)(2,1)} %bitcast.37, bf16[128,4096]{1,0:T(8,128)(2,1)} %bitcast.38, bf16[128,4096]{1,0:T(8,128)(2,1)} %bitcast.39, bf16[128,4096]{1,0:T(8,128)(2,1)} %bitcast.28, s32[1,128]{1,0:T(1,128)} %flag_ref.1, s32[8,128]{1,0:T(8,128)} %bitcast.40, ...), custom_call_target="tpu_custom_call" | custom-call | tf_op jit(solution)/shard_map/prepare/pallas_call | solution.py:142
  3.9 5.8 %all-to-all-start = ((bf16[8,448,512]{2,1,0:T(8,128)(2,1)}), bf16[8,448,512]{2,1,0:T(8,128)(2,1)}, u32[]{:S(2)}, u32[]{:S(2)}) async-start(bf16[8,448,512]{2,1,0:T(8,128)(2,1)} %get-tuple-element.27), calls=%async_computation | async-start | bytes 7340032 | tf_op jit(solution)/shard_map/all_to_all | solution.py:441
  9.7 3.2 %take_half.2 = bf16[768,2048]{1,0:T(8,128)(2,1)} custom-call(s32[1]{0:T(128)} %bitcast.11.half_ref, bf16[768,4096]{1,0:T(8,128)(2,1)} %bitcast.31), custom_call_target="tpu_custom_call" | custom-call | tf_op jit(solution)/shard_map/take_half/pallas_call | solution.py:43
  12.9 1.4 collective-permute-start
  14.3 3.3 %take_half.3 = bf16[768,2048]{1,0:T(8,128)(2,1)} custom-call(s32[1]{0:T(128)} %bitcast.13.half_ref, bf16[768,4096]{1,0:T(8,128)(2,1)} %bitcast.32), custom_call_target="tpu_custom_call" | custom-call | tf_op jit(solution)/shard_map/take_half/pallas_call | solution.py:43
  17.6 2.3 collective-permute-start.1
  19.9 0.0 copy-done.12
  19.9 0.1 dynamic-slice.3
  20.0 0.5 dynamic_slice.3.gain_ref
  20.6 1.4 copy.16
  22.0 2.4 pad.4.weigh_ref
  24.4 24.4 %collective-permute-done.first_down = bf16[768,2048]{1,0:T(8,128)(2,1)S(1)} collective-permute-done((bf16[768,2048]{1,0:T(8,128)(2,1)}, bf16[768,2048]{1,0:T(8,128)(2,1)S(1)}, u32[]{:S(2)}, u32[]{:S(2)}) %collective-permute-start) | collective-permute-done | bytes 3145760 | tf_op jit(solution)/shard_map/ppermute | solution.py:491
  48.8 4.2 %all-to-all-done.in_ref.res_ref.table_ref = bf16[8,448,512]{2,1,0:T(8,128)(2,1)} async-done(((bf16[8,448,512]{2,1,0:T(8,128)(2,1)}), bf16[8,448,512]{2,1,0:T(8,128)(2,1)}, u32[]{:S(2)}, u32[]{:S(2)}) %all-to-all-start) | async-done | bytes 3670048 | tf_op jit(solution)/shard_map/all_to_all | solution.py:441
  53.0 8.1 %attend.1.attn_ref = bf16[8,128,512]{2,1,0:T(8,128)(2,1)} custom-call(bf16[8,448,512]{2,1,0:T(8,128)(2,1)} %all-to-all-done.in_ref.res_ref.table_ref), custom_call_target="tpu_custom_call" | custom-call | tf_op jit(solution)/shard_map/attend/pallas_call | solution.py:191
  61.1 5.0 %all-to-all-start.1 = ((bf16[8,128,512]{2,1,0:T(8,128)(2,1)}), bf16[8,128,512]{2,1,0:T(8,128)(2,1)}, u32[]{:S(2)}, u32[]{:S(2)}) async-start(bf16[8,128,512]{2,1,0:T(8,128)(2,1)} %attend.1.attn_ref), calls=%async_computation.1 | async-start | bytes 2097152 | tf_op jit(solution)/shard_map/all_to_all | solution.py:441
  66.1 6.5 %pick.1 = bf16[8,2,8,8,8,512]{5,4,3,2,1,0:T(8,128)(2,1)} custom-call(bf16[8,128,512]{2,1,0:T(8,128)(2,1)} %attend.1.attn_ref, bf16[8,448,512]{2,1,0:T(8,128)(2,1)} %all-to-all-done.in_ref.res_ref.table_ref, bf16[8,448,512]{2,1,0:T(8,128)(2,1)} %all-to-all-done.in_ref.res_ref.table_ref, bf16[1,512]{1,0:T(2,128)(2,1)} %dynamic_slice.3.gain_ref), custom_call_target="tpu_custom_call" | custom-call | tf_op jit(solution)/shard_map/pick/pallas_call | solution.py:233
  72.6 2.8 copy-done
  75.4 2.8 copy-done.1
  78.2 0.9 stage.1
  79.1 0.0 copy-start.8
  79.1 2.7 copy-done.8
  81.8 2.6 copy-done.10
  84.3 0.0 collective-permute-done.1.second_down
  84.3 0.0 all-to-all-done.1.attn_ref
  84.4 0.0 copy-start.9
  84.4 0.0 copy-start.11
  84.4 108.6 %all_to_all.20 = bf16[128,64,512]{2,1,0:T(8,128)(2,1)S(1)} all-to-all(bf16[128,64,512]{2,1,0:T(8,128)(2,1)} %bitcast.36), channel_id=1, replica_groups=mesh['seq'=8,'exp'=16] {'exp','seq'}, dimensions={0} | all-to-all | bytes 16777216 | tf_op jit(solution)/shard_map/all_to_all | solution.py:441
  192.9 0.0 copy-done.3
  192.9 0.0 copy-done.9
  193.0 0.0 copy-done.11
  193.0 9.5 %expert_open.2.mine_ref = bf16[512,768]{1,0:T(8,128)(2,1)S(1)} custom-call(bf16[16,8,64,512]{3,2,1,0:T(8,128)(2,1)S(1)} %bitcast.24, bf16[4096,128]{1,0:T(8,128)(2,1)S(1)} %copy-done.3, bf16[4096,768]{1,0:T(8,128)(2,1)S(1)} %copy-done.9, bf16[4096,768]{1,0:T(8,128)(2,1)S(1)} %copy-done.11), custom_call_target="tpu_custom_call" | custom-call | flops 6442450944 | bytes 17563648 | tf_op jit(solution)/shard_map/expert_open/pallas_call | solution.py:302
  202.5 0.0 copy-start.5
  202.5 0.3 collective-permute-start.3
  202.8 10.4 %expert_open.3.mine_ref = bf16[512,768]{1,0:T(8,128)(2,1)} custom-call(bf16[16,8,64,512]{3,2,1,0:T(8,128)(2,1)S(1)} %bitcast.25, bf16[4096,128]{1,0:T(8,128)(2,1)S(1)} %copy-done.3, bf16[4096,768]{1,0:T(8,128)(2,1)S(1)} %copy-done.9, bf16[4096,768]{1,0:T(8,128)(2,1)S(1)} %copy-done.11), custom_call_target="tpu_custom_call" | custom-call | flops 6442450944 | bytes 17563648 | tf_op jit(solution)/shard_map/expert_open/pallas_call | solution.py:302
  213.1 0.0 copy-done.5
  213.1 0.0 collective-permute-done.3.first_ref
  213.1 1.3 collective-permute-start.4
  214.4 4.1 %collective-permute-start.2 = (bf16[512,768]{1,0:T(8,128)(2,1)}, bf16[512,768]{1,0:T(8,128)(2,1)}, u32[]{:S(2)}, u32[]{:S(2)}) collective-permute-start(bf16[512,768]{1,0:T(8,128)(2,1)} %expert_open.3.mine_ref), channel_id=1, source_target_pairs={{0,16},{1,0},{2,18},{3,2},{4,20},{5,4},{6,22},{7,6},{8,24},{9,8},{... | collective-permute-start | bytes 2359304 | tf_op jit(solution)/shard_map/ppermute | solution.py:526
  218.6 0.1 pad_add_fusion.role_ref
  218.6 0.5 collective-permute-done.4.second_ref
  219.2 1.1 copy-done.6
  220.3 7.6 %expert_close.2.rest_0_ = bf16[16,8,8,2048]{3,2,1,0:T(8,128)(2,1)} custom-call(s32[2]{0:T(128)S(1)} %pad_add_fusion.role_ref, bf16[512,768]{1,0:T(8,128)(2,1)} %collective-permute-done.3.first_ref, bf16[512,768]{1,0:T(8,128)(2,1)S(1)} %copy-done.6, bf16[512,768]{1,0:T(8,128)(2,1)} %collective-permute-done.4.second_ref, ...), custom_call_target="tpu_custom_call" | custom-call | flops 3221225472 | bytes 9961472 | tf_op jit(solution)/shard_map/expert_close/pallas_call | solution.py:357
  227.9 0.0 collective-permute-done.2.first_ref
  227.9 1.3 collective-permute-start.5
  229.2 4.3 %collective-permute-done.5.second_ref = bf16[512,768]{1,0:T(8,128)(2,1)S(1)} collective-permute-done((bf16[512,768]{1,0:T(8,128)(2,1)}, bf16[512,768]{1,0:T(8,128)(2,1)S(1)}, u32[]{:S(2)}, u32[]{:S(2)}) %collective-permute-start.5) | collective-permute-done | bytes 786464 | tf_op jit(solution)/shard_map/ppermute | solution.py:531
  233.5 7.7 %expert_close.3 = bf16[16,8,8,2048]{3,2,1,0:T(8,128)(2,1)} custom-call(s32[2]{0:T(128)S(1)} %pad_add_fusion.role_ref, bf16[512,768]{1,0:T(8,128)(2,1)} %collective-permute-done.2.first_ref, bf16[512,768]{1,0:T(8,128)(2,1)} %expert_open.3.mine_ref, bf16[512,768]{1,0:T(8,128)(2,1)S(1)} %collective-permute-done.5.second_ref, ...), custom_call_target="tpu_custom_call", output_to_operand_aliasing={{}: (7, {})} | custom-call | flops 3221225472 | bytes 9961472 | tf_op jit(solution)/shard_map/expert_close/pallas_call | solution.py:357
  241.2 57.1 %all_to_all.21 = bf16[128,8,2048]{2,1,0:T(8,128)(2,1)S(1)} all-to-all(bf16[128,8,2048]{2,1,0:T(8,128)(2,1)} %bitcast.35), channel_id=1, replica_groups=mesh['seq'=8,'exp'=16] {'exp','seq'}, dimensions={0} | all-to-all | bytes 8388608 | tf_op jit(solution)/shard_map/all_to_all | solution.py:441
  298.3 4.2 %combine.1 = bf16[128,4096]{1,0:T(8,128)(2,1)} custom-call(bf16[16,4,2,8,2048]{4,3,2,1,0:T(8,128)(2,1)S(1)} %bitcast.23, bf16[3,64,128]{2,1,0:T(8,128)(2,1)S(1)} %copy-done.7, bf16[8,128,512]{2,1,0:T(8,128)(2,1)} %all-to-all-done.1.attn_ref, bf16[128,4096]{1,0:T(8,128)(2,1)S(1)} %bitcast.29, bf16[128,4096]{1,0:T(8,128)(2,1)S(1)} %bitcast.30), custom_call_target="tpu_custom_call" | custom-call | tf_op jit(solution)/shard_map/combine/pallas_call | solution.py:420
  (16 shorter events, 0.1 us)
Async XLA Ops:
  3.9 49.1 %all-to-all-start = ((bf16[8,448,512]{2,1,0:T(8,128)(2,1)}), bf16[8,448,512]{2,1,0:T(8,128)(2,1)}, u32[]{:S(2)}, u32[]{:S(2)}) async-start(bf16[8,448,512]{2,1,0:T(8,128)(2,1)} %get-tuple-element.27), calls=%async_computation | async-start | bytes 7340032 | tf_op jit(solution)/shard_map/all_to_all | solution.py:441
  12.9 35.9 %collective-permute-start = (bf16[768,2048]{1,0:T(8,128)(2,1)}, bf16[768,2048]{1,0:T(8,128)(2,1)S(1)}, u32[]{:S(2)}, u32[]{:S(2)}) collective-permute-start(bf16[768,2048]{1,0:T(8,128)(2,1)} %take_half.2), channel_id=1, source_target_pairs={{0,16},{1,0},{2,18},{3,2},{4,20},{5,4},{6,22},{7,6},{8,24},{9,8},{... | collective-permute-start | bytes 9437192 | tf_op jit(solution)/shard_map/ppermute | solution.py:491
  14.3 5.6 %copy-start.12 = (bf16[4096]{0:T(1024)(128)(2,1)S(1)}, bf16[4096]{0:T(1024)(128)(2,1)}, u32[]{:S(2)}) copy-start(bf16[4096]{0:T(1024)(128)(2,1)} %param.17) | copy-start | bytes 24580
  17.6 66.8 %collective-permute-start.1 = (bf16[768,2048]{1,0:T(8,128)(2,1)}, bf16[768,2048]{1,0:T(8,128)(2,1)}, u32[]{:S(2)}, u32[]{:S(2)}) collective-permute-start(bf16[768,2048]{1,0:T(8,128)(2,1)} %take_half.3), channel_id=1, source_target_pairs={{1,16},{3,18},{5,20},{7,22},{9,24},{11,26},{13,28},{15,30},{16,1},... | collective-permute-start | bytes 9437192 | tf_op jit(solution)/shard_map/ppermute | solution.py:493
  61.1 23.2 %all-to-all-start.1 = ((bf16[8,128,512]{2,1,0:T(8,128)(2,1)}), bf16[8,128,512]{2,1,0:T(8,128)(2,1)}, u32[]{:S(2)}, u32[]{:S(2)}) async-start(bf16[8,128,512]{2,1,0:T(8,128)(2,1)} %attend.1.attn_ref), calls=%async_computation.1 | async-start | bytes 2097152 | tf_op jit(solution)/shard_map/all_to_all | solution.py:441
  72.6 2.8 copy-start
  75.4 2.8 copy-start.1
  79.1 2.7 copy-start.8
  81.8 2.6 copy-start.10
  84.4 108.6 %copy-start.3 = (bf16[4096,128]{1,0:T(8,128)(2,1)S(1)}, bf16[4096,128]{1,0:T(8,128)(2,1)}, u32[]{:S(2)}) copy-start(bf16[4096,128]{1,0:T(8,128)(2,1)} %pad.4.weigh_ref) | copy-start | bytes 3145732
  84.4 108.6 %copy-start.9 = (bf16[4096,768]{1,0:T(8,128)(2,1)S(1)}, bf16[4096,768]{1,0:T(8,128)(2,1)}, u32[]{:S(2)}) copy-start(bf16[4096,768]{1,0:T(8,128)(2,1)} %copy-done.8) | copy-start | bytes 18874372
  84.4 108.6 %copy-start.11 = (bf16[4096,768]{1,0:T(8,128)(2,1)S(1)}, bf16[4096,768]{1,0:T(8,128)(2,1)}, u32[]{:S(2)}) copy-start(bf16[4096,768]{1,0:T(8,128)(2,1)} %copy-done.10) | copy-start | bytes 18874372
  202.5 10.7 %copy-start.5 = (bf16[512,768]{1,0:T(8,128)(2,1)}, bf16[512,768]{1,0:T(8,128)(2,1)S(1)}, u32[]{:S(2)}) copy-start(bf16[512,768]{1,0:T(8,128)(2,1)S(1)} %expert_open.2.mine_ref) | copy-start | bytes 2359300
  202.5 10.7 %collective-permute-start.3 = (bf16[512,768]{1,0:T(8,128)(2,1)S(1)}, bf16[512,768]{1,0:T(8,128)(2,1)}, u32[]{:S(2)}, u32[]{:S(2)}) collective-permute-start(bf16[512,768]{1,0:T(8,128)(2,1)S(1)} %expert_open.2.mine_ref), channel_id=1, source_target_pairs={{0,16},{1,0},{2,18},{3,2},{4,20},{5,4},{6,22},{7,6},{8,24},{9,8},{... | collective-permute-start | bytes 2359304 | tf_op jit(solution)/shard_map/ppermute | solution.py:526
  213.1 6.0 %collective-permute-start.4 = (bf16[512,768]{1,0:T(8,128)(2,1)}, bf16[512,768]{1,0:T(8,128)(2,1)}, u32[]{:S(2)}, u32[]{:S(2)}) collective-permute-start(bf16[512,768]{1,0:T(8,128)(2,1)} %collective-permute-done.3.first_ref), channel_id=1, source_target_pairs={{0,16},{2,18},{4,20},{6,22},{8,24},{10,26},{12,28},{14,30},{17,1},... | collective-permute-start | bytes 2359304 | tf_op jit(solution)/shard_map/ppermute | solution.py:531
  214.4 13.5 %collective-permute-start.2 = (bf16[512,768]{1,0:T(8,128)(2,1)}, bf16[512,768]{1,0:T(8,128)(2,1)}, u32[]{:S(2)}, u32[]{:S(2)}) collective-permute-start(bf16[512,768]{1,0:T(8,128)(2,1)} %expert_open.3.mine_ref), channel_id=1, source_target_pairs={{0,16},{1,0},{2,18},{3,2},{4,20},{5,4},{6,22},{7,6},{8,24},{9,8},{... | collective-permute-start | bytes 2359304 | tf_op jit(solution)/shard_map/ppermute | solution.py:526
  219.2 1.1 copy-start.6
  227.9 5.6 %collective-permute-start.5 = (bf16[512,768]{1,0:T(8,128)(2,1)}, bf16[512,768]{1,0:T(8,128)(2,1)S(1)}, u32[]{:S(2)}, u32[]{:S(2)}) collective-permute-start(bf16[512,768]{1,0:T(8,128)(2,1)} %collective-permute-done.2.first_ref), channel_id=1, source_target_pairs={{0,16},{2,18},{4,20},{6,22},{8,24},{10,26},{12,28},{14,30},{17,1},... | collective-permute-start | bytes 2359304 | tf_op jit(solution)/shard_map/ppermute | solution.py:531
  241.2 57.1 %copy-start.2 = (bf16[1,128,4096]{2,1,0:T(8,128)(2,1)S(1)}, bf16[1,128,4096]{2,1,0:T(8,128)(2,1)}, u32[]{:S(2)}) copy-start(bf16[1,128,4096]{2,1,0:T(8,128)(2,1)} %param.15) | copy-start | bytes 3145732
  241.2 57.1 %copy-start.4 = (bf16[1,128,4096]{2,1,0:T(8,128)(2,1)S(1)}, bf16[1,128,4096]{2,1,0:T(8,128)(2,1)}, u32[]{:S(2)}) copy-start(bf16[1,128,4096]{2,1,0:T(8,128)(2,1)} %param.16) | copy-start | bytes 3145732
  241.2 57.1 %copy-start.7 = (bf16[3,64,128]{2,1,0:T(8,128)(2,1)S(1)}, bf16[3,64,128]{2,1,0:T(8,128)(2,1)}, u32[]{:S(2)}) copy-start(bf16[3,64,128]{2,1,0:T(8,128)(2,1)} %get-tuple-element.47.own_ref) | copy-start | bytes 147460
